TPU v7x, 32 devices: a whole 2x2x4 slice. The times are simulated.
32 devices in a mesh: grp: 8 (over y, x, core), tile: 4 (over z).
Axes of the slice: x: 2, y: 2, z: 4, core: 2. Of those that a mesh axis runs over, the one named last changes fastest.
Arguments:
- log_cond: float32 [8, 32, 32, 128], P('grp', 'tile'), may hold values from -3 to 3
- potential: float32 [8, 32, 32, 128], P('grp', 'tile'), may hold values from -6 to 6
- noise: float32 [2, 8, 32, 32, 128], P(None, 'grp', 'tile'), may hold values from -3 to 3
- source: float32 [32, 32, 128], P('tile'), may hold values from -6 to 6
- parents: int32 [8], replicated, may hold values from 0 to 7
- accept: int32 [2, 8], P(None, 'grp'), may hold values 0 or 1
- weights: float32 [8], P('grp'), may hold values from 0.1 to 10
Outputs:
- conduct_out: float32 [8, 32, 32, 128], P('grp', 'tile')
- potential_out: float32 [8, 32, 32, 128], P('grp', 'tile')
- moments: float32 [1024, 1024], P('tile')
Inputs may be any that keep to these rules, and one draw needn't show every extreme that they name: `parents`: parent indices of offspring.
All inputs are finite; a program needn't handle non-finite values. No bound on the sum of `accept` on one device may be relied on, other than what follows from the above.
Results may differ from a plain program's by a relative error of at most 0.0001.
Values sent between devices are 32-bit elements; how exact they have to be, the bound alone decides.
No kernel may reach another device: no remote copies, remote signals or barrier semaphores. Data moves between devices by JAX's collectives and lax.ppermute only.
A program may use at most 64 MiB of HBM per device.

v0:
```python
import functools

import jax
import jax.numpy as jnp
from jax import lax
from jax.experimental import pallas as pl
from jax.experimental.pallas import tpu as pltpu
from jax.sharding import PartitionSpec as P

prior_keep = 0.8
prior_fresh = 0.6
relax_weight = 0.8
pair = 2
group = ("pairs", "member")

SMEM = pl.BlockSpec(memory_space=pltpu.SMEM)
VMEM = pl.BlockSpec(memory_space=pltpu.VMEM)
ANY = pl.BlockSpec(memory_space=pl.ANY)


def in_vmem(array):
    return pltpu.with_memory_space_constraint(array, pltpu.VMEM)


def pack_kernel(
    rows, depth, weight_ref, cond_ref, pot_ref, noise_ref, source_ref,
    pieces_ref, noise_out, source_out, low_ref, high_ref, sems,
):
    moves = noise_ref.shape[0]
    pairs = []
    for piece in range(pieces_ref.shape[0]):
        row = piece * rows
        field = cond_ref if row < cond_ref.shape[0] else pot_ref
        row %= cond_ref.shape[0]
        pairs.append((field.at[pl.ds(row, rows)], pieces_ref.at[piece, pl.ds(0, rows)]))
    pairs += [(noise_ref, noise_out), (source_ref, source_out)]
    at = 0
    for field, h in zip([noise_ref.at[m] for m in range(moves)] + [source_ref], depth):
        pairs.append((field.at[pl.ds(0, h)], low_ref.at[pl.ds(at, h)]))
        pairs.append((field.at[pl.ds(field.shape[0] - h, h)], high_ref.at[pl.ds(at, h)]))
        at += h
    copies = [
        pltpu.make_async_copy(here, there, sems.at[i]) for i, (here, there) in enumerate(pairs)
    ]
    for copy in copies:
        copy.start()
    weight = jnp.full((8, pieces_ref.shape[2]), weight_ref[0], jnp.float32)
    for piece in range(pieces_ref.shape[0]):
        pieces_ref[piece, rows:rows + 8] = weight
    for copy in copies:
        copy.wait()


def pack(weights, log_cond, potential, noise, source, particles, depth):
    _, ny, nz = source.shape
    rows = 2 * log_cond.size // (particles * nz)
    edge = pltpu.VMEM((sum(depth), ny, nz), jnp.float32)
    return pl.pallas_call(
        functools.partial(pack_kernel, rows, depth),
        out_shape=(
            pltpu.VMEM((particles, rows + 8, nz), jnp.float32),
            pltpu.VMEM(noise.shape, jnp.float32),
            pltpu.VMEM(source.shape, jnp.float32),
            edge,
            edge,
        ),
        in_specs=[SMEM, ANY, ANY, ANY, ANY],
        out_specs=(VMEM,) * 5,
        scratch_shapes=[pltpu.SemaphoreType.DMA((particles + 2 + 2 * len(depth),))],
        name="pack",
    )(weights, log_cond.reshape(-1, nz), potential.reshape(-1, nz), noise, source)


def choose_kernel(parents_ref, weight_ref, pieces_ref, chosen_ref, root_ref):
    rows = chosen_ref.shape[1]
    for place in range(chosen_ref.shape[0]):
        chosen_ref[place] = pieces_ref[parents_ref[place], pl.ds(0, rows)]
    total = pieces_ref[0, rows:rows + 8]
    for place in range(1, pieces_ref.shape[0]):
        total += pieces_ref[place, rows:rows + 8]
    root_ref[...] = jnp.sqrt(weight_ref[0] / total)


def choose(parents, weights, pieces):
    particles, rows, nz = pieces.shape
    return pl.pallas_call(
        choose_kernel,
        out_shape=(
            pltpu.VMEM((particles, rows - 8, nz), jnp.float32),
            pltpu.VMEM((8, nz), jnp.float32),
        ),
        in_specs=[SMEM, SMEM, VMEM],
        out_specs=(VMEM, VMEM),
        name="choose",
    )(parents, weights, in_vmem(pieces))


def six_sum(before, here, after, edge):
    row = lax.broadcasted_iota(jnp.int32, here.shape, 0)
    lane = lax.broadcasted_iota(jnp.int32, here.shape, 1)
    ny, nz = here.shape
    down = jnp.where(row == 0, edge, pltpu.roll(here, 1, 0))
    up = jnp.where(row == ny - 1, edge, pltpu.roll(here, ny - 1, 0))
    left = jnp.where(lane == 0, edge, pltpu.roll(here, 1, 1))
    right = jnp.where(lane == nz - 1, edge, pltpu.roll(here, nz - 1, 1))
    return ((before + after) + (down + up)) + (left + right)


def moves_kernel(
    depth, accept_ref, root_ref, moved_ref, noise_ref, source_ref,
    moved_low, moved_high, fixed_low, fixed_high,
    cond_out, pot_out, traces_out, cond, pot, once, conductivity, gain,
):
    moves, width, _, nz = noise_ref.shape
    reach = 2 * moves
    span = width + 2 * reach
    tile = lax.axis_index("tile")
    first = tile == 0
    last = tile == lax.axis_size("tile") - 1

    def fetch(field, low, high, at, h, i):
        if i < 0:
            return low[at + h + i]
        if i >= width:
            return high[at + i - width]
        return field[i]

    def keep_inside(value, i):
        outside = (first & (i < reach)) | (last & (i >= reach + width))
        return jnp.where(outside, 0.0, value)

    for i in range(span):
        cond[i] = fetch(moved_ref.at[0], moved_low, moved_high, 0, reach, i - reach)
        pot[i] = fetch(moved_ref.at[1], moved_low, moved_high, reach, reach, i - reach)

    source_at = sum(depth[:moves])
    for m in range(moves):
        start = 2 * m
        noise_at = sum(depth[:m])
        accepted = accept_ref[m] > 0

        def sweep(old, lo, hi):
            for i in range(lo, hi):
                here, here_k = old[i], conductivity[i]
                before, after = old[i - 1], old[i + 1]
                plain = six_sum(before, here, after, 0.0)
                scaled = six_sum(
                    before * conductivity[i - 1], here * here_k, after * conductivity[i + 1], 0.0
                )
                source = fetch(
                    source_ref, fixed_low, fixed_high, source_at, depth[moves], i - reach
                )
                value = (1.0 - relax_weight) * here + (
                    2.0 * source + (here_k * plain + scaled)
                ) * gain[i]
                yield i, keep_inside(value, i)

        for i in range(start, span - start):
            proposal = prior_keep * cond[i] + prior_fresh * fetch(
                noise_ref.at[m], fixed_low, fixed_high, noise_at, depth[m], i - reach
            )
            conductivity[i] = jnp.exp(proposal)
            cond[i] = jnp.where(accepted, proposal, cond[i])
        for i in range(start + 1, span - start - 1):
            here_k = conductivity[i]
            gain[i] = relax_weight / (
                6.0 * here_k + six_sum(conductivity[i - 1], here_k, conductivity[i + 1], 1.0)
            )
        for i, value in sweep(pot, start + 1, span - start - 1):
            once[i] = value
        for i, value in sweep(once, start + 2, span - start - 2):
            pot[i] = jnp.where(accepted, value, pot[i])

    root = root_ref[0:1]
    for i in range(width):
        cond_out[i] = cond[i + reach]
        value = pot[i + reach]
        pot_out[i] = value
        traces_out[:, i * nz:(i + 1) * nz] = value * root


def run_moves(depth, accept, root, *fields):
    moves, width, ny, nz = fields[1].shape
    span = width + 4 * moves
    return pl.pallas_call(
        functools.partial(moves_kernel, depth),
        out_shape=(
            pltpu.VMEM((width, ny, nz), jnp.float32),
            pltpu.VMEM((width, ny, nz), jnp.float32),
            pltpu.VMEM((ny, width * nz), jnp.float32),
        ),
        in_specs=[SMEM] + [VMEM] * (1 + len(fields)),
        out_specs=(VMEM, VMEM, VMEM),
        scratch_shapes=[pltpu.VMEM((span, ny, nz), jnp.float32)] * 5,
        name="moves",
    )(accept, in_vmem(root), *[in_vmem(field) for field in fields])


def sum_copies_kernel(parts_ref, copies_ref):
    total = parts_ref[0]
    for place in range(1, parts_ref.shape[0]):
        total += parts_ref[place]
    for place in range(copies_ref.shape[0]):
        copies_ref[place] = total


def sum_copies(parts):
    return pl.pallas_call(
        sum_copies_kernel,
        out_shape=pltpu.VMEM(parts.shape, jnp.float32),
        in_specs=[VMEM],
        out_specs=VMEM,
        name="sum_copies",
    )(in_vmem(parts))


def interleave_kernel(mine_ref, other_ref, out_ref, sems):
    member = lax.axis_index("member")
    copies = [
        pltpu.make_async_copy(mine_ref, out_ref.at[:, member], sems.at[0]),
        pltpu.make_async_copy(other_ref, out_ref.at[:, 1 - member], sems.at[1]),
    ]
    for copy in copies:
        copy.start()
    for copy in copies:
        copy.wait()


def interleave(mine, other):
    return pl.pallas_call(
        interleave_kernel,
        out_shape=jax.ShapeDtypeStruct(
            (mine.shape[0], pair) + mine.shape[1:], jnp.float32
        ),
        in_specs=[VMEM, VMEM],
        out_specs=ANY,
        scratch_shapes=[pltpu.SemaphoreType.DMA((2,))],
        name="interleave",
    )(in_vmem(mine), in_vmem(other))


def exchange_halo(low_edge, high_edge):
    count = lax.axis_size("tile")
    forward = [(i, i + 1) for i in range(count - 1)]
    backward = [(target, source) for source, target in forward]
    low = lax.ppermute(high_edge, "tile", forward)
    high = lax.ppermute(low_edge, "tile", backward)
    return low, high


def swap(block):
    return lax.ppermute(block, "member", [(0, 1), (1, 0)])


def local(log_cond, potential, noise, source, parents, accept, weights):
    moves = noise.shape[0]
    width, ny, nz = source.shape
    reach = 2 * moves
    particles = lax.axis_size(group)

    depth = tuple(reach - 2 * m for m in range(moves)) + (reach - 1,)
    pieces, noise, source, low_edge, high_edge = pack(
        weights, log_cond, potential, noise[:, 0], source, particles, depth
    )
    pieces = lax.all_to_all(pieces, group, 0, 0, tiled=True)
    fixed_low, fixed_high = exchange_halo(low_edge, high_edge)
    chosen, root = choose(parents, weights, pieces)
    moved = lax.all_to_all(chosen, group, 0, 0, tiled=True).reshape(2, width, ny, nz)
    moved_low, moved_high = exchange_halo(
        moved[:, :reach].reshape(-1, ny, nz), moved[:, width - reach:].reshape(-1, ny, nz)
    )
    conduct, pot, traces = run_moves(
        depth, accept[:, 0], root, moved, noise, source, moved_low, moved_high, fixed_low, fixed_high
    )

    rows_here = traces.shape[1] // lax.axis_size("tile")
    own_start = lax.axis_index("tile") * rows_here
    piece = lax.all_gather(traces, "tile", axis=0, tiled=True)
    columns = lax.dynamic_slice_in_dim(piece, own_start, rows_here, 1)
    product = lax.dot_general(
        columns,
        piece,
        (((0,), (0,)), ((), ())),
        precision=lax.Precision.HIGHEST,
        preferred_element_type=jnp.float32,
    )
    member = lax.axis_index("member")
    blocks = product.reshape(particles // pair, pair, rows_here // particles, -1)
    keep = lax.dynamic_index_in_dim(blocks, member, 1, keepdims=False)
    give = lax.dynamic_index_in_dim(blocks, 1 - member, 1, keepdims=False)
    parts = lax.all_to_all(keep + swap(give), "pairs", 0, 0, tiled=True)
    mine = lax.all_to_all(sum_copies(parts), "pairs", 0, 0, tiled=True)
    other = swap(mine)
    moments = interleave(mine, other).reshape(rows_here, -1)
    return (conduct[None], pot[None], moments)


def solution(mesh):
    tiles = mesh.shape["tile"]
    split = jax.sharding.Mesh(
        mesh.devices.reshape(-1, pair, tiles), ("pairs", "member", "tile")
    )
    placed = (
        P(group, "tile", None, None),
        P(group, "tile", None, None),
        P(None, group, "tile", None, None),
        P("tile", None, None),
        P(),
        P(None, group),
        P(group),
    )
    return jax.shard_map(
        local,
        mesh=split,
        in_specs=placed,
        out_specs=(P(group, "tile", None, None), P(group, "tile", None, None), P("tile", None)),
        check_vma=False,
    )
```

profile of v0, /device:TPU:0, one launch (start us, length us, event | category | flops | bytes accessed | tf_op | source)
XLA Modules:
  0.0 82.6 jit_solution(7346797795324048871)
XLA Ops:
  1.3 1.3 %pack.1 = (f32[8,72,128]{2,1,0:T(8,128)S(1)}, f32[2,8,32,128]{3,2,1,0:T(8,128)S(1)}, f32[8,32,128]{2,1,0:T(8,128)S(1)}, f32[9,32,128]{2,1,0:T(8,128)S(1)}, f32[9,32,128]{2,1,0:T(8,128)S(1)}) custom-call(f32[1]{0:T(128)S(6)} %copy.16.weight_ref, f32[256,128]{1,0:T(8,128)} %bitcast.28, f32[256,128]{1,0:T(8,128)} %bitcast.29, f32[2,8,32,128]{3,2,1,0:T(8,128)} %bitcast.27, ...), custom_call_target="tpu_custom_call" | custom-call | tf_op jit(solution)/shard_map/pack/pallas_call | solution.py:58
  2.6 12.3 %all_to_all.20.pieces_ref = f32[8,72,128]{2,1,0:T(8,128)S(1)} all-to-all(f32[8,72,128]{2,1,0:T(8,128)S(1)} %get-tuple-element.13), channel_id=1, replica_groups=mesh['pairs'=4,'member'=2,'tile'=4] {'pairs','member'}, dimensions={0} | all-to-all | bytes 589824 | tf_op jit(solution)/shard_map/all_to_all | solution.py:265
  14.8 1.4 %choose.1 = (f32[8,64,128]{2,1,0:T(8,128)}, f32[8,128]{1,0:T(8,128)S(1)}) custom-call(s32[8]{0:T(128)} %parents_ref.1, f32[1]{0:T(128)S(6)} %copy.16.weight_ref, f32[8,72,128]{2,1,0:T(8,128)S(1)} %all_to_all.20.pieces_ref), custom_call_target="tpu_custom_call" | custom-call | tf_op jit(solution)/shard_map/choose/pallas_call | solution.py:86
  16.2 3.4 %all-to-all-start.1 = ((f32[8,64,128]{2,1,0:T(8,128)}), f32[8,64,128]{2,1,0:T(8,128)S(1)}, u32[]{:S(2)}, u32[]{:S(2)}) async-start(f32[8,64,128]{2,1,0:T(8,128)} %get-tuple-element.15), calls=%async_computation.1 | async-start | bytes 524288 | tf_op jit(solution)/shard_map/all_to_all | solution.py:268
  19.6 3.5 %collective-permute-start.2 = (f32[9,32,128]{2,1,0:T(8,128)S(1)}, f32[9,32,128]{2,1,0:T(8,128)S(1)}, u32[]{:S(2)}, u32[]{:S(2)}) collective-permute-start(f32[9,32,128]{2,1,0:T(8,128)S(1)} %get-tuple-element.18), channel_id=1, source_target_pairs={{0,1},{1,2},{2,3},{4,5},{5,6},{6,7},{8,9},{9,10},{10,11},{12,13},{... | collective-permute-start | bytes 442376 | tf_op jit(solution)/shard_map/ppermute | solution.py:246
  23.2 1.3 %collective-permute-start.3 = (f32[9,32,128]{2,1,0:T(8,128)S(1)}, f32[9,32,128]{2,1,0:T(8,128)S(1)}, u32[]{:S(2)}, u32[]{:S(2)}) collective-permute-start(f32[9,32,128]{2,1,0:T(8,128)S(1)} %get-tuple-element.19), channel_id=1, source_target_pairs={{1,0},{2,1},{3,2},{5,4},{6,5},{7,6},{9,8},{10,9},{11,10},{13,12},{... | collective-permute-start | bytes 442376 | tf_op jit(solution)/shard_map/ppermute | solution.py:247
  24.5 2.0 %all-to-all-done.1 = f32[8,64,128]{2,1,0:T(8,128)S(1)} async-done(((f32[8,64,128]{2,1,0:T(8,128)}), f32[8,64,128]{2,1,0:T(8,128)S(1)}, u32[]{:S(2)}, u32[]{:S(2)}) %all-to-all-start.1) | async-done | bytes 262176 | tf_op jit(solution)/shard_map/all_to_all | solution.py:268
  26.5 3.5 %collective-permute-start = (f32[8,32,128]{2,1,0:T(8,128)S(1)}, f32[8,32,128]{2,1,0:T(8,128)S(1)}, u32[]{:S(2)}, u32[]{:S(2)}) collective-permute-start(f32[8,32,128]{2,1,0:T(8,128)S(1)} %bitcast.31), channel_id=1, source_target_pairs={{0,1},{1,2},{2,3},{4,5},{5,6},{6,7},{8,9},{9,10},{10,11},{12,13},{... | collective-permute-start | bytes 393224 | tf_op jit(solution)/shard_map/ppermute | solution.py:246
  30.0 1.3 %collective-permute-start.1 = (f32[8,32,128]{2,1,0:T(8,128)S(1)}, f32[8,32,128]{2,1,0:T(8,128)S(1)}, u32[]{:S(2)}, u32[]{:S(2)}) collective-permute-start(f32[8,32,128]{2,1,0:T(8,128)S(1)} %bitcast.30), channel_id=1, source_target_pairs={{1,0},{2,1},{3,2},{5,4},{6,5},{7,6},{9,8},{10,9},{11,10},{13,12},{... | collective-permute-start | bytes 393224 | tf_op jit(solution)/shard_map/ppermute | solution.py:247
  31.3 0.0 collective-permute-done.2.fixed_low
  31.4 1.2 %collective-permute-done.moved_low = f32[8,32,128]{2,1,0:T(8,128)S(1)} collective-permute-done((f32[8,32,128]{2,1,0:T(8,128)S(1)}, f32[8,32,128]{2,1,0:T(8,128)S(1)}, u32[]{:S(2)}, u32[]{:S(2)}) %collective-permute-start) | collective-permute-done | bytes 131104 | tf_op jit(solution)/shard_map/ppermute | solution.py:246
  32.5 4.4 %collective-permute-done.1.moved_high = f32[8,32,128]{2,1,0:T(8,128)S(1)} collective-permute-done((f32[8,32,128]{2,1,0:T(8,128)S(1)}, f32[8,32,128]{2,1,0:T(8,128)S(1)}, u32[]{:S(2)}, u32[]{:S(2)}) %collective-permute-start.1) | collective-permute-done | bytes 131104 | tf_op jit(solution)/shard_map/ppermute | solution.py:247
  36.9 1.8 %moves.1 = (f32[8,32,128]{2,1,0:T(8,128)S(1)}, f32[8,32,128]{2,1,0:T(8,128)S(1)}, f32[32,1024]{1,0:T(8,128)S(1)}) custom-call(s32[2]{0:T(128)} %bitcast.32, f32[8,128]{1,0:T(8,128)S(1)} %get-tuple-element.14.root_ref, f32[2,8,32,128]{3,2,1,0:T(8,128)S(1)} %bitcast.23, f32[2,8,32,128]{3,2,1,0:T(8,128)S(1)} %get-tuple-element.16.noise_ref, ...), custom_call_target="tpu_custom_call" | custom-call | tf_op jit(solution)/shard_map/moves/pallas_call | solution.py:185
  38.7 15.9 %all_gather.3 = f32[128,1024]{1,0:T(8,128)S(1)} all-gather(f32[32,1024]{1,0:T(8,128)S(1)} %get-tuple-element.22), channel_id=1, replica_groups=mesh['pairs'=4,'member'=2,'tile'=4] {'tile'}, dimensions={0}, use_global_device_ids=true | all-gather | bytes 655360 | tf_op jit(solution)/shard_map/all_gather | solution.py:278
  54.6 1.0 %fusion = f32[256,1024]{1,0:T(8,128)S(1)} fusion(f32[128,1024]{1,0:T(8,128)S(1)} %all_gather.3, s32[]{:T(128)S(6)} %select_n.10), kind=kOutput, calls=%fused_computation.2 | convolution fusion | flops 402653184 | bytes 1703940 | tf_op jit(solution)/shard_map/dot_general | solution.py:280
  55.7 0.1 collective-permute-start.4
  55.7 1.9 %collective-permute-done.4 = f32[4,32,1024]{2,1,0:T(8,128)S(1)} collective-permute-done((f32[4,32,1024]{2,1,0:T(8,128)S(1)}, f32[4,32,1024]{2,1,0:T(8,128)S(1)}, u32[]{:S(2)}, u32[]{:S(2)}) %collective-permute-start.4) | collective-permute-done | bytes 524320 | tf_op jit(solution)/shard_map/ppermute | solution.py:252
  57.6 0.1 bitcast_add_fusion
  57.7 12.1 %all_to_all.21.parts_ref = f32[4,32,1024]{2,1,0:T(8,128)S(1)} all-to-all(f32[4,32,1024]{2,1,0:T(8,128)S(1)} %bitcast_add_fusion), channel_id=1, replica_groups=mesh['pairs'=4,'member'=2,'tile'=4] {'pairs'}, dimensions={0} | all-to-all | bytes 1048576 | tf_op jit(solution)/shard_map/all_to_all | solution.py:291
  69.9 9.8 %all_to_all.22.mine_ref = f32[4,32,1024]{2,1,0:T(8,128)S(1)} all-to-all(f32[4,32,1024]{2,1,0:T(8,128)S(1)} %sum_copies.1), channel_id=1, replica_groups=mesh['pairs'=4,'member'=2,'tile'=4] {'pairs'}, dimensions={0} | all-to-all | bytes 1048576 | tf_op jit(solution)/shard_map/all_to_all | solution.py:292
  79.7 0.7 copy.14
  80.3 0.7 copy.15
  81.0 0.6 collective-permute-done.5.other_ref
  81.6 1.0 %interleave.1 = f32[4,2,32,1024]{3,2,1,0:T(8,128)} custom-call(f32[4,32,1024]{2,1,0:T(8,128)S(1)} %all_to_all.22.mine_ref, f32[4,32,1024]{2,1,0:T(8,128)S(1)} %collective-permute-done.5.other_ref), custom_call_target="tpu_custom_call" | custom-call | tf_op jit(solution)/shard_map/interleave/pallas_call | solution.py:230
  (5 shorter events, 0.1 us)
Async XLA Ops:
  16.2 10.3 %all-to-all-start.1 = ((f32[8,64,128]{2,1,0:T(8,128)}), f32[8,64,128]{2,1,0:T(8,128)S(1)}, u32[]{:S(2)}, u32[]{:S(2)}) async-start(f32[8,64,128]{2,1,0:T(8,128)} %get-tuple-element.15), calls=%async_computation.1 | async-start | bytes 524288 | tf_op jit(solution)/shard_map/all_to_all | solution.py:268
  19.6 11.7 %collective-permute-start.2 = (f32[9,32,128]{2,1,0:T(8,128)S(1)}, f32[9,32,128]{2,1,0:T(8,128)S(1)}, u32[]{:S(2)}, u32[]{:S(2)}) collective-permute-start(f32[9,32,128]{2,1,0:T(8,128)S(1)} %get-tuple-element.18), channel_id=1, source_target_pairs={{0,1},{1,2},{2,3},{4,5},{5,6},{6,7},{8,9},{9,10},{10,11},{12,13},{... | collective-permute-start | bytes 442376 | tf_op jit(solution)/shard_map/ppermute | solution.py:246
  23.2 8.2 %collective-permute-start.3 = (f32[9,32,128]{2,1,0:T(8,128)S(1)}, f32[9,32,128]{2,1,0:T(8,128)S(1)}, u32[]{:S(2)}, u32[]{:S(2)}) collective-permute-start(f32[9,32,128]{2,1,0:T(8,128)S(1)} %get-tuple-element.19), channel_id=1, source_target_pairs={{1,0},{2,1},{3,2},{5,4},{6,5},{7,6},{9,8},{10,9},{11,10},{13,12},{... | collective-permute-start | bytes 442376 | tf_op jit(solution)/shard_map/ppermute | solution.py:247
  26.5 6.0 %collective-permute-start = (f32[8,32,128]{2,1,0:T(8,128)S(1)}, f32[8,32,128]{2,1,0:T(8,128)S(1)}, u32[]{:S(2)}, u32[]{:S(2)}) collective-permute-start(f32[8,32,128]{2,1,0:T(8,128)S(1)} %bitcast.31), channel_id=1, source_target_pairs={{0,1},{1,2},{2,3},{4,5},{5,6},{6,7},{8,9},{9,10},{10,11},{12,13},{... | collective-permute-start | bytes 393224 | tf_op jit(solution)/shard_map/ppermute | solution.py:246
  30.0 6.9 %collective-permute-start.1 = (f32[8,32,128]{2,1,0:T(8,128)S(1)}, f32[8,32,128]{2,1,0:T(8,128)S(1)}, u32[]{:S(2)}, u32[]{:S(2)}) collective-permute-start(f32[8,32,128]{2,1,0:T(8,128)S(1)} %bitcast.30), channel_id=1, source_target_pairs={{1,0},{2,1},{3,2},{5,4},{6,5},{7,6},{9,8},{10,9},{11,10},{13,12},{... | collective-permute-start | bytes 393224 | tf_op jit(solution)/shard_map/ppermute | solution.py:247
  55.7 2.0 %collective-permute-start.4 = (f32[4,32,1024]{2,1,0:T(8,128)S(1)}, f32[4,32,1024]{2,1,0:T(8,128)S(1)}, u32[]{:S(2)}, u32[]{:S(2)}) collective-permute-start(f32[4,32,1024]{2,1,0:T(8,128)S(1)} %dynamic-slice_bitcast_fusion), channel_id=1, source_target_pairs={{0,4},{4,0},{1,5},{5,1},{2,6},{6,2},{3,7},{7,3},{8,12},{12,8},{9,1... | collective-permute-start | bytes 1572872 | tf_op jit(solution)/shard_map/ppermute | solution.py:252
  79.7 1.9 %collective-permute-start.5 = (f32[4,32,1024]{2,1,0:T(8,128)S(1)}, f32[4,32,1024]{2,1,0:T(8,128)S(1)}, u32[]{:S(2)}, u32[]{:S(2)}) collective-permute-start(f32[4,32,1024]{2,1,0:T(8,128)S(1)} %all_to_all.22.mine_ref), channel_id=1, source_target_pairs={{0,4},{4,0},{1,5},{5,1},{2,6},{6,2},{3,7},{7,3},{8,12},{12,8},{9,1... | collective-permute-start | bytes 1572872 | tf_op jit(solution)/shard_map/ppermute | solution.py:252
where the time goes:
time: 83 us; the launch traced here: 82.6 us
  blocking collectives  50 us (60%)
  starting transfers between devices  13.1 us (16%)
  waiting for transfers between devices  10.1 us (12%)
  Pallas kernels  5.48 us (7%)
  between operations  1.39 us (2%)
  local copies, waits for them, and re-layouts  1.38 us (2%)
  matrix products  1.04 us (1%)
    all_gather x1, blocking collectives, local(): piece = lax.all_gather(traces, 'tile', axis=0, tiled=True)  15.9 us
    all_to_all x1, blocking collectives, local(): pieces = lax.all_to_all(pieces, group, 0, 0, tiled=True)  12.3 us
    all_to_all x1, blocking collectives, local(): parts = lax.all_to_all(keep + swap(give), 'pairs', 0, 0, tiled=True)  12.1 us
    all_to_all x1, blocking collectives, local(): mine = lax.all_to_all(sum_copies(parts), 'pairs', 0, 0, tiled=True)  9.8 us
    ppermute x2, starting transfers between devices, exchange_halo(): low = lax.ppermute(high_edge, 'tile', forward)  7.01 us
    ppermute x2, waiting for transfers between devices, exchange_halo(): high = lax.ppermute(low_edge, 'tile', backward)  4.37 us
    all_to_all x1, starting transfers between devices, local(): lax.all_to_all(chosen, group, 0, 0, tiled=True).reshape(2, width, ny, nz)  3.41 us
    ppermute x2, starting transfers between devices, exchange_halo(): high = lax.ppermute(low_edge, 'tile', backward)  2.58 us
  transfers between devices with their start and end apart: 7, of which 5 were waited for; matrix products, arithmetic and copies ran while one was open for 2% of the time, Pallas kernels for 0%

commit v1 on v0

--- a/solution.py
+++ b/solution.py
@@ -51,14 +51,14 @@
         copy.wait()
 
 
-def pack(weights, log_cond, potential, noise, source, particles, depth):
+def pack(weights, log_cond, potential, noise, source, pairs, depth):
     _, ny, nz = source.shape
-    rows = 2 * log_cond.size // (particles * nz)
+    rows = 2 * log_cond.size // (pairs * nz)
     edge = pltpu.VMEM((sum(depth), ny, nz), jnp.float32)
     return pl.pallas_call(
         functools.partial(pack_kernel, rows, depth),
         out_shape=(
-            pltpu.VMEM((particles, rows + 8, nz), jnp.float32),
+            pltpu.VMEM((pairs, rows + 8, nz), jnp.float32),
             pltpu.VMEM(noise.shape, jnp.float32),
             pltpu.VMEM(source.shape, jnp.float32),
             edge,
@@ -66,33 +66,39 @@
         ),
         in_specs=[SMEM, ANY, ANY, ANY, ANY],
         out_specs=(VMEM,) * 5,
-        scratch_shapes=[pltpu.SemaphoreType.DMA((particles + 2 + 2 * len(depth),))],
+        scratch_shapes=[pltpu.SemaphoreType.DMA((pairs + 2 + 2 * len(depth),))],
         name="pack",
     )(weights, log_cond.reshape(-1, nz), potential.reshape(-1, nz), noise, source)
 
 
-def choose_kernel(parents_ref, weight_ref, pieces_ref, chosen_ref, root_ref):
+def choose_kernel(parents_ref, weight_ref, mine_ref, other_ref, chosen_ref, root_ref):
+    member = lax.axis_index("member")
     rows = chosen_ref.shape[1]
     for place in range(chosen_ref.shape[0]):
-        chosen_ref[place] = pieces_ref[parents_ref[place], pl.ds(0, rows)]
-    total = pieces_ref[0, rows:rows + 8]
-    for place in range(1, pieces_ref.shape[0]):
-        total += pieces_ref[place, rows:rows + 8]
+        parent = parents_ref[place * pair + member]
+        here = lax.rem(parent, pair) == member
+        at = lax.div(parent, pair)
+        chosen_ref[place] = jnp.where(
+            here, mine_ref[at, pl.ds(0, rows)], other_ref[at, pl.ds(0, rows)]
+        )
+    total = jnp.zeros_like(root_ref)
+    for place in range(chosen_ref.shape[0]):
+        total += mine_ref[place, rows:rows + 8] + other_ref[place, rows:rows + 8]
     root_ref[...] = jnp.sqrt(weight_ref[0] / total)
 
 
-def choose(parents, weights, pieces):
-    particles, rows, nz = pieces.shape
+def choose(parents, weights, mine, other):
+    pairs, rows, nz = mine.shape
     return pl.pallas_call(
         choose_kernel,
         out_shape=(
-            pltpu.VMEM((particles, rows - 8, nz), jnp.float32),
+            pltpu.VMEM((pairs, rows - 8, nz), jnp.float32),
             pltpu.VMEM((8, nz), jnp.float32),
         ),
-        in_specs=[SMEM, SMEM, VMEM],
+        in_specs=[SMEM, SMEM, VMEM, VMEM],
         out_specs=(VMEM, VMEM),
         name="choose",
-    )(parents, weights, in_vmem(pieces))
+    )(parents, weights, in_vmem(mine), in_vmem(other))
 
 
 def six_sum(before, here, after, edge):
@@ -214,11 +220,14 @@
     )(in_vmem(parts))
 
 
-def interleave_kernel(mine_ref, other_ref, out_ref, sems):
+def join_kernel(mine_ref, other_ref, out_ref, sems):
     member = lax.axis_index("member")
+    rows = mine_ref.shape[0]
     copies = [
-        pltpu.make_async_copy(mine_ref, out_ref.at[:, member], sems.at[0]),
-        pltpu.make_async_copy(other_ref, out_ref.at[:, 1 - member], sems.at[1]),
+        pltpu.make_async_copy(
+            ref, out_ref.at[pl.ds(pl.multiple_of(owner * rows, rows), rows)], sems.at[i]
+        )
+        for i, (ref, owner) in enumerate([(mine_ref, member), (other_ref, 1 - member)])
     ]
     for copy in copies:
         copy.start()
@@ -226,16 +235,14 @@
         copy.wait()
 
 
-def interleave(mine, other):
-    return pl.pallas_call(
-        interleave_kernel,
-        out_shape=jax.ShapeDtypeStruct(
-            (mine.shape[0], pair) + mine.shape[1:], jnp.float32
-        ),
+def join(mine, other):
+    return pl.pallas_call(
+        join_kernel,
+        out_shape=jax.ShapeDtypeStruct((pair * mine.shape[0], mine.shape[1]), jnp.float32),
         in_specs=[VMEM, VMEM],
         out_specs=ANY,
         scratch_shapes=[pltpu.SemaphoreType.DMA((2,))],
-        name="interleave",
+        name="join",
     )(in_vmem(mine), in_vmem(other))
 
 
@@ -256,16 +263,15 @@
     moves = noise.shape[0]
     width, ny, nz = source.shape
     reach = 2 * moves
-    particles = lax.axis_size(group)
 
     depth = tuple(reach - 2 * m for m in range(moves)) + (reach - 1,)
     pieces, noise, source, low_edge, high_edge = pack(
-        weights, log_cond, potential, noise[:, 0], source, particles, depth
-    )
-    pieces = lax.all_to_all(pieces, group, 0, 0, tiled=True)
+        weights, log_cond, potential, noise[:, 0], source, lax.axis_size("pairs"), depth
+    )
+    pieces = lax.all_to_all(pieces, "pairs", 0, 0, tiled=True)
     fixed_low, fixed_high = exchange_halo(low_edge, high_edge)
-    chosen, root = choose(parents, weights, pieces)
-    moved = lax.all_to_all(chosen, group, 0, 0, tiled=True).reshape(2, width, ny, nz)
+    chosen, root = choose(parents, weights, pieces, swap(pieces))
+    moved = lax.all_to_all(chosen, "pairs", 0, 0, tiled=True).reshape(2, width, ny, nz)
     moved_low, moved_high = exchange_halo(
         moved[:, :reach].reshape(-1, ny, nz), moved[:, width - reach:].reshape(-1, ny, nz)
     )
@@ -273,25 +279,26 @@
         depth, accept[:, 0], root, moved, noise, source, moved_low, moved_high, fixed_low, fixed_high
     )
 
-    rows_here = traces.shape[1] // lax.axis_size("tile")
-    own_start = lax.axis_index("tile") * rows_here
+    rows = traces.shape[1] // (lax.axis_size("tile") * pair)
+    member = lax.axis_index("member")
     piece = lax.all_gather(traces, "tile", axis=0, tiled=True)
-    columns = lax.dynamic_slice_in_dim(piece, own_start, rows_here, 1)
-    product = lax.dot_general(
-        columns,
-        piece,
-        (((0,), (0,)), ((), ())),
-        precision=lax.Precision.HIGHEST,
-        preferred_element_type=jnp.float32,
-    )
-    member = lax.axis_index("member")
-    blocks = product.reshape(particles // pair, pair, rows_here // particles, -1)
-    keep = lax.dynamic_index_in_dim(blocks, member, 1, keepdims=False)
-    give = lax.dynamic_index_in_dim(blocks, 1 - member, 1, keepdims=False)
-    parts = lax.all_to_all(keep + swap(give), "pairs", 0, 0, tiled=True)
+
+    def product(owner):
+        columns = lax.dynamic_slice_in_dim(
+            piece, (lax.axis_index("tile") * pair + owner) * rows, rows, 1
+        )
+        return lax.dot_general(
+            columns,
+            piece,
+            (((0,), (0,)), ((), ())),
+            precision=lax.Precision.HIGHEST,
+            preferred_element_type=jnp.float32,
+        ).reshape(lax.axis_size("pairs"), -1, piece.shape[1])
+
+    got = swap(product(1 - member))
+    parts = lax.all_to_all(product(member) + got, "pairs", 0, 0, tiled=True)
     mine = lax.all_to_all(sum_copies(parts), "pairs", 0, 0, tiled=True)
-    other = swap(mine)
-    moments = interleave(mine, other).reshape(rows_here, -1)
+    moments = join(mine.reshape(rows, -1), swap(mine).reshape(rows, -1))
     return (conduct[None], pot[None], moments)
 
 

time: 83 us -> 82.7 us (level)
    all_to_all x1, waiting for transfers between devices: 2.04 us -> 1.11 us  [local(): lax.all_to_all(chosen, 'pairs', 0, 0, tiled=True).reshape(2, width, ny, nz)]
    ppermute x2 -> x3, waiting for transfers between devices: 2.49 us -> 3.4 us  [swap(): return lax.ppermute(block, 'member', [(0, 1), (1, 0)])]
  transfers between devices with their start and end apart: 7 -> 8, of which waited for: 5 -> 7; matrix products, arithmetic and copies ran while one was open for 2% -> 2% of each run, Pallas kernels for 0% -> 0%
where the time goes in v1:
time: 82.7 us; the launch traced here: 82.3 us
  blocking collectives  49.7 us (60%)
  starting transfers between devices  13 us (16%)
  waiting for transfers between devices  10.1 us (12%)
  Pallas kernels  5.46 us (7%)
  between operations  1.4 us (2%)
  local copies, waits for them, and re-layouts  1.33 us (2%)
  matrix products  1.27 us (2%)
    all_gather x1, blocking collectives, local(): piece = lax.all_gather(traces, 'tile', axis=0, tiled=True)  16.1 us
    all_to_all x1, blocking collectives, local(): parts = lax.all_to_all(product(member) + got, 'pairs', 0, 0, tiled=True)  12.6 us
    all_to_all x1, blocking collectives, local(): pieces = lax.all_to_all(pieces, 'pairs', 0, 0, tiled=True)  11.2 us
    all_to_all x1, blocking collectives, local(): mine = lax.all_to_all(sum_copies(parts), 'pairs', 0, 0, tiled=True)  9.8 us
    ppermute x2, starting transfers between devices, exchange_halo(): low = lax.ppermute(high_edge, 'tile', forward)  6.98 us
    ppermute x2, waiting for transfers between devices, exchange_halo(): high = lax.ppermute(low_edge, 'tile', backward)  4.62 us
    all_to_all x1, starting transfers between devices, local(): lax.all_to_all(chosen, 'pairs', 0, 0, tiled=True).reshape(2, width, ny, nz)  3.41 us
    ppermute x3, waiting for transfers between devices, swap(): return lax.ppermute(block, 'member', [(0, 1), (1, 0)])  3.4 us
  transfers between devices with their start and end apart: 8, of which 7 were waited for; matrix products, arithmetic and copies ran while one was open for 2% of the time, Pallas kernels for 0%

profile of v1, /device:TPU:0, one launch (start us, length us, event | category | flops | bytes accessed | tf_op | source)
XLA Modules:
  0.0 82.3 jit_solution(8934681826339782865)
XLA Ops:
  1.3 1.2 %pack.1 = (f32[4,136,128]{2,1,0:T(8,128)S(1)}, f32[2,8,32,128]{3,2,1,0:T(8,128)S(1)}, f32[8,32,128]{2,1,0:T(8,128)S(1)}, f32[9,32,128]{2,1,0:T(8,128)S(1)}, f32[9,32,128]{2,1,0:T(8,128)S(1)}) custom-call(f32[1]{0:T(128)S(6)} %copy.12.weight_ref, f32[256,128]{1,0:T(8,128)} %bitcast.24, f32[256,128]{1,0:T(8,128)} %bitcast.25, f32[2,8,32,128]{3,2,1,0:T(8,128)} %bitcast.23, ...), custom_call_target="tpu_custom_call" | custom-call | tf_op jit(solution)/shard_map/pack/pallas_call | solution.py:58
  2.5 11.2 %all_to_all.20.mine_ref = f32[4,136,128]{2,1,0:T(8,128)S(1)} all-to-all(f32[4,136,128]{2,1,0:T(8,128)S(1)} %get-tuple-element.13), channel_id=1, replica_groups=mesh['pairs'=4,'member'=2,'tile'=4] {'pairs'}, dimensions={0} | all-to-all | bytes 557056 | tf_op jit(solution)/shard_map/all_to_all | solution.py:271
  13.7 1.6 %collective-permute-done.other_ref = f32[4,136,128]{2,1,0:T(8,128)S(1)} collective-permute-done((f32[4,136,128]{2,1,0:T(8,128)S(1)}, f32[4,136,128]{2,1,0:T(8,128)S(1)}, u32[]{:S(2)}, u32[]{:S(2)}) %collective-permute-start) | collective-permute-done | bytes 278560 | tf_op jit(solution)/shard_map/ppermute | solution.py:259
  15.2 1.4 %choose.1 = (f32[4,128,128]{2,1,0:T(8,128)}, f32[8,128]{1,0:T(8,128)S(1)}) custom-call(s32[8]{0:T(128)} %parents_ref.1, f32[1]{0:T(128)S(6)} %copy.12.weight_ref, f32[4,136,128]{2,1,0:T(8,128)S(1)} %all_to_all.20.mine_ref, f32[4,136,128]{2,1,0:T(8,128)S(1)} %collective-permute-done.other_ref), custom_call_target="tpu_custom_call" | custom-call | tf_op jit(solution)/shard_map/choose/pallas_call | solution.py:92
  16.7 3.4 %all-to-all-start.1 = ((f32[4,128,128]{2,1,0:T(8,128)}), f32[4,128,128]{2,1,0:T(8,128)S(1)}, u32[]{:S(2)}, u32[]{:S(2)}) async-start(f32[4,128,128]{2,1,0:T(8,128)} %get-tuple-element.15), calls=%async_computation.1 | async-start | bytes 524288 | tf_op jit(solution)/shard_map/all_to_all | solution.py:274
  20.1 3.5 %collective-permute-start.3 = (f32[9,32,128]{2,1,0:T(8,128)S(1)}, f32[9,32,128]{2,1,0:T(8,128)S(1)}, u32[]{:S(2)}, u32[]{:S(2)}) collective-permute-start(f32[9,32,128]{2,1,0:T(8,128)S(1)} %get-tuple-element.18), channel_id=1, source_target_pairs={{0,1},{1,2},{2,3},{4,5},{5,6},{6,7},{8,9},{9,10},{10,11},{12,13},{... | collective-permute-start | bytes 442376 | tf_op jit(solution)/shard_map/ppermute | solution.py:253
  23.6 1.3 %collective-permute-start.4 = (f32[9,32,128]{2,1,0:T(8,128)S(1)}, f32[9,32,128]{2,1,0:T(8,128)S(1)}, u32[]{:S(2)}, u32[]{:S(2)}) collective-permute-start(f32[9,32,128]{2,1,0:T(8,128)S(1)} %get-tuple-element.19), channel_id=1, source_target_pairs={{1,0},{2,1},{3,2},{5,4},{6,5},{7,6},{9,8},{10,9},{11,10},{13,12},{... | collective-permute-start | bytes 442376 | tf_op jit(solution)/shard_map/ppermute | solution.py:254
  24.9 1.1 %all-to-all-done.1 = f32[4,128,128]{2,1,0:T(8,128)S(1)} async-done(((f32[4,128,128]{2,1,0:T(8,128)}), f32[4,128,128]{2,1,0:T(8,128)S(1)}, u32[]{:S(2)}, u32[]{:S(2)}) %all-to-all-start.1) | async-done | bytes 262176 | tf_op jit(solution)/shard_map/all_to_all | solution.py:274
  26.0 3.5 %collective-permute-start.1 = (f32[8,32,128]{2,1,0:T(8,128)S(1)}, f32[8,32,128]{2,1,0:T(8,128)S(1)}, u32[]{:S(2)}, u32[]{:S(2)}) collective-permute-start(f32[8,32,128]{2,1,0:T(8,128)S(1)} %bitcast.27), channel_id=1, source_target_pairs={{0,1},{1,2},{2,3},{4,5},{5,6},{6,7},{8,9},{9,10},{10,11},{12,13},{... | collective-permute-start | bytes 393224 | tf_op jit(solution)/shard_map/ppermute | solution.py:253
  29.5 1.3 %collective-permute-start.2 = (f32[8,32,128]{2,1,0:T(8,128)S(1)}, f32[8,32,128]{2,1,0:T(8,128)S(1)}, u32[]{:S(2)}, u32[]{:S(2)}) collective-permute-start(f32[8,32,128]{2,1,0:T(8,128)S(1)} %bitcast.26), channel_id=1, source_target_pairs={{1,0},{2,1},{3,2},{5,4},{6,5},{7,6},{9,8},{10,9},{11,10},{13,12},{... | collective-permute-start | bytes 393224 | tf_op jit(solution)/shard_map/ppermute | solution.py:254
  30.8 0.3 collective-permute-done.4.fixed_high
  31.1 0.9 %collective-permute-done.1.moved_low = f32[8,32,128]{2,1,0:T(8,128)S(1)} collective-permute-done((f32[8,32,128]{2,1,0:T(8,128)S(1)}, f32[8,32,128]{2,1,0:T(8,128)S(1)}, u32[]{:S(2)}, u32[]{:S(2)}) %collective-permute-start.1) | collective-permute-done | bytes 131104 | tf_op jit(solution)/shard_map/ppermute | solution.py:253
  32.0 4.4 %collective-permute-done.2.moved_high = f32[8,32,128]{2,1,0:T(8,128)S(1)} collective-permute-done((f32[8,32,128]{2,1,0:T(8,128)S(1)}, f32[8,32,128]{2,1,0:T(8,128)S(1)}, u32[]{:S(2)}, u32[]{:S(2)}) %collective-permute-start.2) | collective-permute-done | bytes 131104 | tf_op jit(solution)/shard_map/ppermute | solution.py:254
  36.4 1.8 %moves.1 = (f32[8,32,128]{2,1,0:T(8,128)S(1)}, f32[8,32,128]{2,1,0:T(8,128)S(1)}, f32[32,1024]{1,0:T(8,128)S(1)}) custom-call(s32[2]{0:T(128)} %bitcast.28, f32[8,128]{1,0:T(8,128)S(1)} %get-tuple-element.14.root_ref, f32[2,8,32,128]{3,2,1,0:T(8,128)S(1)} %bitcast.18, f32[2,8,32,128]{3,2,1,0:T(8,128)S(1)} %get-tuple-element.16.noise_ref, ...), custom_call_target="tpu_custom_call" | custom-call | tf_op jit(solution)/shard_map/moves/pallas_call | solution.py:191
  38.2 16.1 %all_gather.3 = f32[128,1024]{1,0:T(8,128)S(1)} all-gather(f32[32,1024]{1,0:T(8,128)S(1)} %get-tuple-element.22), channel_id=1, replica_groups=mesh['pairs'=4,'member'=2,'tile'=4] {'tile'}, dimensions={0}, use_global_device_ids=true | all-gather | bytes 655360 | tf_op jit(solution)/shard_map/all_gather | solution.py:284
  54.3 0.6 fusion
  55.0 0.6 fusion.2
  55.7 1.2 %collective-permute-done.5 = f32[4,32,1024]{2,1,0:T(8,128)S(1)} collective-permute-done((f32[4,32,1024]{2,1,0:T(8,128)S(1)}, f32[4,32,1024]{2,1,0:T(8,128)S(1)}, u32[]{:S(2)}, u32[]{:S(2)}) %collective-permute-start.5) | collective-permute-done | bytes 524320 | tf_op jit(solution)/shard_map/ppermute | solution.py:259
  57.0 12.6 %all_to_all.21.parts_ref = f32[4,32,1024]{2,1,0:T(8,128)S(1)} all-to-all(f32[4,32,1024]{2,1,0:T(8,128)S(1)} %add.19), channel_id=1, replica_groups=mesh['pairs'=4,'member'=2,'tile'=4] {'pairs'}, dimensions={0} | all-to-all | bytes 1048576 | tf_op jit(solution)/shard_map/all_to_all | solution.py:299
  69.6 9.8 %all_to_all.22 = f32[4,32,1024]{2,1,0:T(8,128)S(1)} all-to-all(f32[4,32,1024]{2,1,0:T(8,128)S(1)} %sum_copies.1), channel_id=1, replica_groups=mesh['pairs'=4,'member'=2,'tile'=4] {'pairs'}, dimensions={0} | all-to-all | bytes 1048576 | tf_op jit(solution)/shard_map/all_to_all | solution.py:300
  79.4 0.7 copy.10
  80.1 0.7 copy.11
  80.7 0.6 collective-permute-done.6
  81.3 1.0 %join.1 = f32[256,1024]{1,0:T(8,128)} custom-call(f32[128,1024]{1,0:T(8,128)S(1)} %bitcast.19, f32[128,1024]{1,0:T(8,128)S(1)} %bitcast.20), custom_call_target="tpu_custom_call" | custom-call | tf_op jit(solution)/shard_map/join/pallas_call | solution.py:239
  (7 shorter events, 0.2 us)
Async XLA Ops:
  13.7 1.6 %collective-permute-start = (f32[4,136,128]{2,1,0:T(8,128)S(1)}, f32[4,136,128]{2,1,0:T(8,128)S(1)}, u32[]{:S(2)}, u32[]{:S(2)}) collective-permute-start(f32[4,136,128]{2,1,0:T(8,128)S(1)} %all_to_all.20.mine_ref), channel_id=1, source_target_pairs={{0,4},{4,0},{1,5},{5,1},{2,6},{6,2},{3,7},{7,3},{8,12},{12,8},{9,1... | collective-permute-start | bytes 835592 | tf_op jit(solution)/shard_map/ppermute | solution.py:259
  16.7 9.3 %all-to-all-start.1 = ((f32[4,128,128]{2,1,0:T(8,128)}), f32[4,128,128]{2,1,0:T(8,128)S(1)}, u32[]{:S(2)}, u32[]{:S(2)}) async-start(f32[4,128,128]{2,1,0:T(8,128)} %get-tuple-element.15), calls=%async_computation.1 | async-start | bytes 524288 | tf_op jit(solution)/shard_map/all_to_all | solution.py:274
  20.1 10.7 %collective-permute-start.3 = (f32[9,32,128]{2,1,0:T(8,128)S(1)}, f32[9,32,128]{2,1,0:T(8,128)S(1)}, u32[]{:S(2)}, u32[]{:S(2)}) collective-permute-start(f32[9,32,128]{2,1,0:T(8,128)S(1)} %get-tuple-element.18), channel_id=1, source_target_pairs={{0,1},{1,2},{2,3},{4,5},{5,6},{6,7},{8,9},{9,10},{10,11},{12,13},{... | collective-permute-start | bytes 442376 | tf_op jit(solution)/shard_map/ppermute | solution.py:253
  23.6 7.5 %collective-permute-start.4 = (f32[9,32,128]{2,1,0:T(8,128)S(1)}, f32[9,32,128]{2,1,0:T(8,128)S(1)}, u32[]{:S(2)}, u32[]{:S(2)}) collective-permute-start(f32[9,32,128]{2,1,0:T(8,128)S(1)} %get-tuple-element.19), channel_id=1, source_target_pairs={{1,0},{2,1},{3,2},{5,4},{6,5},{7,6},{9,8},{10,9},{11,10},{13,12},{... | collective-permute-start | bytes 442376 | tf_op jit(solution)/shard_map/ppermute | solution.py:254
  26.0 6.0 %collective-permute-start.1 = (f32[8,32,128]{2,1,0:T(8,128)S(1)}, f32[8,32,128]{2,1,0:T(8,128)S(1)}, u32[]{:S(2)}, u32[]{:S(2)}) collective-permute-start(f32[8,32,128]{2,1,0:T(8,128)S(1)} %bitcast.27), channel_id=1, source_target_pairs={{0,1},{1,2},{2,3},{4,5},{5,6},{6,7},{8,9},{9,10},{10,11},{12,13},{... | collective-permute-start | bytes 393224 | tf_op jit(solution)/shard_map/ppermute | solution.py:253
  29.5 6.9 %collective-permute-start.2 = (f32[8,32,128]{2,1,0:T(8,128)S(1)}, f32[8,32,128]{2,1,0:T(8,128)S(1)}, u32[]{:S(2)}, u32[]{:S(2)}) collective-permute-start(f32[8,32,128]{2,1,0:T(8,128)S(1)} %bitcast.26), channel_id=1, source_target_pairs={{1,0},{2,1},{3,2},{5,4},{6,5},{7,6},{9,8},{10,9},{11,10},{13,12},{... | collective-permute-start | bytes 393224 | tf_op jit(solution)/shard_map/ppermute | solution.py:254
  54.9 2.0 %collective-permute-start.5 = (f32[4,32,1024]{2,1,0:T(8,128)S(1)}, f32[4,32,1024]{2,1,0:T(8,128)S(1)}, u32[]{:S(2)}, u32[]{:S(2)}) collective-permute-start(f32[4,32,1024]{2,1,0:T(8,128)S(1)} %bitcast.22), channel_id=1, source_target_pairs={{0,4},{4,0},{1,5},{5,1},{2,6},{6,2},{3,7},{7,3},{8,12},{12,8},{9,1... | collective-permute-start | bytes 1572872 | tf_op jit(solution)/shard_map/ppermute | solution.py:259
  79.4 1.9 %collective-permute-start.6 = (f32[4,32,1024]{2,1,0:T(8,128)S(1)}, f32[4,32,1024]{2,1,0:T(8,128)S(1)}, u32[]{:S(2)}, u32[]{:S(2)}) collective-permute-start(f32[4,32,1024]{2,1,0:T(8,128)S(1)} %all_to_all.22), channel_id=1, source_target_pairs={{0,4},{4,0},{1,5},{5,1},{2,6},{6,2},{3,7},{7,3},{8,12},{12,8},{9,1... | collective-permute-start | bytes 1572872 | tf_op jit(solution)/shard_map/ppermute | solution.py:259

commit v2 on v1

--- a/solution.py
+++ b/solution.py
@@ -114,7 +114,7 @@
 
 def moves_kernel(
     depth, accept_ref, root_ref, moved_ref, noise_ref, source_ref,
-    moved_low, moved_high, fixed_low, fixed_high,
+    low_ref, high_ref,
     cond_out, pot_out, traces_out, cond, pot, once, conductivity, gain,
 ):
     moves, width, _, nz = noise_ref.shape
@@ -124,11 +124,11 @@
     first = tile == 0
     last = tile == lax.axis_size("tile") - 1
 
-    def fetch(field, low, high, at, h, i):
+    def fetch(field, at, h, i):
         if i < 0:
-            return low[at + h + i]
+            return low_ref[at + h + i]
         if i >= width:
-            return high[at + i - width]
+            return high_ref[at + i - width]
         return field[i]
 
     def keep_inside(value, i):
@@ -136,13 +136,13 @@
         return jnp.where(outside, 0.0, value)
 
     for i in range(span):
-        cond[i] = fetch(moved_ref.at[0], moved_low, moved_high, 0, reach, i - reach)
-        pot[i] = fetch(moved_ref.at[1], moved_low, moved_high, reach, reach, i - reach)
-
-    source_at = sum(depth[:moves])
+        cond[i] = fetch(moved_ref.at[0], 0, reach, i - reach)
+        pot[i] = fetch(moved_ref.at[1], reach, reach, i - reach)
+
+    source_at = 2 * reach + sum(depth[:moves])
     for m in range(moves):
         start = 2 * m
-        noise_at = sum(depth[:m])
+        noise_at = 2 * reach + sum(depth[:m])
         accepted = accept_ref[m] > 0
 
         def sweep(old, lo, hi):
@@ -154,7 +154,7 @@
                     before * conductivity[i - 1], here * here_k, after * conductivity[i + 1], 0.0
                 )
                 source = fetch(
-                    source_ref, fixed_low, fixed_high, source_at, depth[moves], i - reach
+                    source_ref, source_at, depth[moves], i - reach
                 )
                 value = (1.0 - relax_weight) * here + (
                     2.0 * source + (here_k * plain + scaled)
@@ -163,7 +163,7 @@
 
         for i in range(start, span - start):
             proposal = prior_keep * cond[i] + prior_fresh * fetch(
-                noise_ref.at[m], fixed_low, fixed_high, noise_at, depth[m], i - reach
+                noise_ref.at[m], noise_at, depth[m], i - reach
             )
             conductivity[i] = jnp.exp(proposal)
             cond[i] = jnp.where(accepted, proposal, cond[i])
@@ -220,30 +220,28 @@
     )(in_vmem(parts))
 
 
-def join_kernel(mine_ref, other_ref, out_ref, sems):
+def put_kernel(own, half_ref, *refs):
+    out_ref, sem = refs[-2:]
     member = lax.axis_index("member")
-    rows = mine_ref.shape[0]
-    copies = [
-        pltpu.make_async_copy(
-            ref, out_ref.at[pl.ds(pl.multiple_of(owner * rows, rows), rows)], sems.at[i]
-        )
-        for i, (ref, owner) in enumerate([(mine_ref, member), (other_ref, 1 - member)])
-    ]
-    for copy in copies:
-        copy.start()
-    for copy in copies:
-        copy.wait()
-
-
-def join(mine, other):
-    return pl.pallas_call(
-        join_kernel,
-        out_shape=jax.ShapeDtypeStruct((pair * mine.shape[0], mine.shape[1]), jnp.float32),
-        in_specs=[VMEM, VMEM],
+    owner = member if own else 1 - member
+    rows = half_ref.shape[0]
+    copy = pltpu.make_async_copy(
+        half_ref, out_ref.at[pl.ds(pl.multiple_of(owner * rows, rows), rows)], sem
+    )
+    copy.start()
+    copy.wait()
+
+
+def put(half, own, whole=()):
+    return pl.pallas_call(
+        functools.partial(put_kernel, own),
+        out_shape=jax.ShapeDtypeStruct((pair * half.shape[0], half.shape[1]), jnp.float32),
+        in_specs=[VMEM] + [ANY] * len(whole),
         out_specs=ANY,
-        scratch_shapes=[pltpu.SemaphoreType.DMA((2,))],
-        name="join",
-    )(in_vmem(mine), in_vmem(other))
+        scratch_shapes=[pltpu.SemaphoreType.DMA],
+        input_output_aliases={1: 0} if whole else {},
+        name="put",
+    )(in_vmem(half), *whole)
 
 
 def exchange_halo(low_edge, high_edge):
@@ -269,14 +267,14 @@
         weights, log_cond, potential, noise[:, 0], source, lax.axis_size("pairs"), depth
     )
     pieces = lax.all_to_all(pieces, "pairs", 0, 0, tiled=True)
-    fixed_low, fixed_high = exchange_halo(low_edge, high_edge)
     chosen, root = choose(parents, weights, pieces, swap(pieces))
     moved = lax.all_to_all(chosen, "pairs", 0, 0, tiled=True).reshape(2, width, ny, nz)
-    moved_low, moved_high = exchange_halo(
-        moved[:, :reach].reshape(-1, ny, nz), moved[:, width - reach:].reshape(-1, ny, nz)
+    low, high = exchange_halo(
+        jnp.concatenate([moved[:, :reach].reshape(-1, ny, nz), low_edge]),
+        jnp.concatenate([moved[:, width - reach:].reshape(-1, ny, nz), high_edge]),
     )
     conduct, pot, traces = run_moves(
-        depth, accept[:, 0], root, moved, noise, source, moved_low, moved_high, fixed_low, fixed_high
+        depth, accept[:, 0], root, moved, noise, source, low, high
     )
 
     rows = traces.shape[1] // (lax.axis_size("tile") * pair)
@@ -298,7 +296,8 @@
     got = swap(product(1 - member))
     parts = lax.all_to_all(product(member) + got, "pairs", 0, 0, tiled=True)
     mine = lax.all_to_all(sum_copies(parts), "pairs", 0, 0, tiled=True)
-    moments = join(mine.reshape(rows, -1), swap(mine).reshape(rows, -1))
+    other = swap(mine).reshape(rows, -1)
+    moments = put(other, False, (put(mine.reshape(rows, -1), True),))
     return (conduct[None], pot[None], moments)
 
 

time: 82.7 us -> 82.1 us (level)
  starting transfers between devices: 13 us -> 4.87 us
  blocking collectives: 49.7 us -> 56.7 us
    all_to_all x0 -> x1, blocking collectives: none -> 8.68 us  [local(): lax.all_to_all(chosen, 'pairs', 0, 0, tiled=True).reshape(2, width, ny, nz)]
    ppermute x2 -> x1, starting transfers between devices: 6.98 us -> 3.5 us  [exchange_halo(): low = lax.ppermute(high_edge, 'tile', forward)]
    all_to_all x1 -> x0, starting transfers between devices: 3.41 us -> none  [local(): lax.all_to_all(chosen, 'pairs', 0, 0, tiled=True).reshape(2, width, ny, nz)]
    ppermute x2 -> x1, waiting for transfers between devices: 0.93 us -> 3.67 us  [exchange_halo(): low = lax.ppermute(high_edge, 'tile', forward)]
    ppermute x2 -> x1, starting transfers between devices: 2.58 us -> 1.29 us  [exchange_halo(): high = lax.ppermute(low_edge, 'tile', backward)]
    all_to_all x1 -> x0, waiting for transfers between devices: 1.11 us -> none  [local(): lax.all_to_all(chosen, 'pairs', 0, 0, tiled=True).reshape(2, width, ny, nz)]
    all_to_all x1, blocking collectives: 12.6 us -> 11.5 us  [local(): parts = lax.all_to_all(product(member) + got, 'pairs', 0, 0, tiled=True)]
    ppermute x2 -> x1, waiting for transfers between devices: 4.62 us -> 4.16 us  [exchange_halo(): high = lax.ppermute(low_edge, 'tile', backward)]
  transfers between devices with their start and end apart: 8 -> 5, of which waited for: 7 -> 4; matrix products, arithmetic and copies ran while one was open for 2% -> 2% of each run, Pallas kernels for 0% -> 1%
where the time goes in v2:
time: 82.1 us; the launch traced here: 81.7 us
  blocking collectives  56.7 us (69%)
  waiting for transfers between devices  10.6 us (13%)
  Pallas kernels  5.39 us (7%)
  starting transfers between devices  4.87 us (6%)
  between operations  1.41 us (2%)
  local copies, waits for them, and re-layouts  1.33 us (2%)
  matrix products  1.27 us (2%)
    all_gather x1, blocking collectives, local(): piece = lax.all_gather(traces, 'tile', axis=0, tiled=True)  15.6 us
    all_to_all x1, blocking collectives, local(): parts = lax.all_to_all(product(member) + got, 'pairs', 0, 0, tiled=True)  11.5 us
    all_to_all x1, blocking collectives, local(): pieces = lax.all_to_all(pieces, 'pairs', 0, 0, tiled=True)  11.2 us
    all_to_all x1, blocking collectives, local(): mine = lax.all_to_all(sum_copies(parts), 'pairs', 0, 0, tiled=True)  9.8 us
    all_to_all x1, blocking collectives, local(): lax.all_to_all(chosen, 'pairs', 0, 0, tiled=True).reshape(2, width, ny, nz)  8.68 us
    ppermute x1, waiting for transfers between devices, exchange_halo(): high = lax.ppermute(low_edge, 'tile', backward)  4.16 us
    ppermute x1, waiting for transfers between devices, exchange_halo(): low = lax.ppermute(high_edge, 'tile', forward)  3.67 us
    ppermute x1, starting transfers between devices, exchange_halo(): low = lax.ppermute(high_edge, 'tile', forward)  3.5 us
  transfers between devices with their start and end apart: 5, of which 4 were waited for; matrix products, arithmetic and copies ran while one was open for 2% of the time, Pallas kernels for 1%

profile of v2, /device:TPU:0, one launch (start us, length us, event | category | flops | bytes accessed | tf_op | source)
XLA Modules:
  0.0 81.7 jit_solution(4162173079216862768)
XLA Ops:
  1.3 1.2 %pack.1 = (f32[4,136,128]{2,1,0:T(8,128)S(1)}, f32[2,8,32,128]{3,2,1,0:T(8,128)S(1)}, f32[8,32,128]{2,1,0:T(8,128)S(1)}, f32[9,32,128]{2,1,0:T(8,128)S(1)}, f32[9,32,128]{2,1,0:T(8,128)S(1)}) custom-call(f32[1]{0:T(128)S(6)} %copy.14.weight_ref, f32[256,128]{1,0:T(8,128)} %bitcast.26, f32[256,128]{1,0:T(8,128)} %bitcast.27, f32[2,8,32,128]{3,2,1,0:T(8,128)} %bitcast.25, ...), custom_call_target="tpu_custom_call" | custom-call | tf_op jit(solution)/shard_map/pack/pallas_call | solution.py:58
  2.5 11.2 %all_to_all.20.mine_ref = f32[4,136,128]{2,1,0:T(8,128)S(1)} all-to-all(f32[4,136,128]{2,1,0:T(8,128)S(1)} %get-tuple-element.13), channel_id=1, replica_groups=mesh['pairs'=4,'member'=2,'tile'=4] {'pairs'}, dimensions={0} | all-to-all | bytes 557056 | tf_op jit(solution)/shard_map/all_to_all | solution.py:269
  13.7 0.0 collective-permute-start
  13.7 1.6 %collective-permute-done.other_ref = f32[4,136,128]{2,1,0:T(8,128)S(1)} collective-permute-done((f32[4,136,128]{2,1,0:T(8,128)S(1)}, f32[4,136,128]{2,1,0:T(8,128)S(1)}, u32[]{:S(2)}, u32[]{:S(2)}) %collective-permute-start) | collective-permute-done | bytes 278560 | tf_op jit(solution)/shard_map/ppermute | solution.py:257
  15.2 0.7 choose.1
  16.0 8.7 %all_to_all.21 = f32[4,128,128]{2,1,0:T(8,128)S(1)} all-to-all(f32[4,128,128]{2,1,0:T(8,128)S(1)} %get-tuple-element.15), channel_id=1, replica_groups=mesh['pairs'=4,'member'=2,'tile'=4] {'pairs'}, dimensions={0} | all-to-all | bytes 524288 | tf_op jit(solution)/shard_map/all_to_all | solution.py:271
  24.7 3.5 %collective-permute-start.1 = (f32[17,32,128]{2,1,0:T(8,128)S(1)}, f32[17,32,128]{2,1,0:T(8,128)S(1)}, u32[]{:S(2)}, u32[]{:S(2)}) collective-permute-start(f32[17,32,128]{2,1,0:T(8,128)S(1)} %pad_maximum_fusion), channel_id=1, source_target_pairs={{0,1},{1,2},{2,3},{4,5},{5,6},{6,7},{8,9},{9,10},{10,11},{12,13},{... | collective-permute-start | bytes 835592 | tf_op jit(solution)/shard_map/ppermute | solution.py:251
  28.2 1.3 %collective-permute-start.2 = (f32[17,32,128]{2,1,0:T(8,128)S(1)}, f32[17,32,128]{2,1,0:T(8,128)S(1)}, u32[]{:S(2)}, u32[]{:S(2)}) collective-permute-start(f32[17,32,128]{2,1,0:T(8,128)S(1)} %pad_maximum_fusion.1), channel_id=1, source_target_pairs={{1,0},{2,1},{3,2},{5,4},{6,5},{7,6},{9,8},{10,9},{11,10},{13,12},{... | collective-permute-start | bytes 835592 | tf_op jit(solution)/shard_map/ppermute | solution.py:252
  29.5 3.7 %collective-permute-done.1.low_ref = f32[17,32,128]{2,1,0:T(8,128)S(1)} collective-permute-done((f32[17,32,128]{2,1,0:T(8,128)S(1)}, f32[17,32,128]{2,1,0:T(8,128)S(1)}, u32[]{:S(2)}, u32[]{:S(2)}) %collective-permute-start.1) | collective-permute-done | bytes 278560 | tf_op jit(solution)/shard_map/ppermute | solution.py:251
  33.2 4.2 %collective-permute-done.2.high_ref = f32[17,32,128]{2,1,0:T(8,128)S(1)} collective-permute-done((f32[17,32,128]{2,1,0:T(8,128)S(1)}, f32[17,32,128]{2,1,0:T(8,128)S(1)}, u32[]{:S(2)}, u32[]{:S(2)}) %collective-permute-start.2) | collective-permute-done | bytes 278560 | tf_op jit(solution)/shard_map/ppermute | solution.py:252
  37.4 1.8 %moves.1 = (f32[8,32,128]{2,1,0:T(8,128)S(1)}, f32[8,32,128]{2,1,0:T(8,128)S(1)}, f32[32,1024]{1,0:T(8,128)S(1)}) custom-call(s32[2]{0:T(128)} %bitcast.28, f32[8,128]{1,0:T(8,128)S(1)} %get-tuple-element.14.root_ref, f32[2,8,32,128]{3,2,1,0:T(8,128)S(1)} %bitcast.18, f32[2,8,32,128]{3,2,1,0:T(8,128)S(1)} %get-tuple-element.16.noise_ref, ...), custom_call_target="tpu_custom_call" | custom-call | tf_op jit(solution)/shard_map/moves/pallas_call | solution.py:191
  39.2 15.6 %all_gather.3 = f32[128,1024]{1,0:T(8,128)S(1)} all-gather(f32[32,1024]{1,0:T(8,128)S(1)} %get-tuple-element.22), channel_id=1, replica_groups=mesh['pairs'=4,'member'=2,'tile'=4] {'tile'}, dimensions={0}, use_global_device_ids=true | all-gather | bytes 655360 | tf_op jit(solution)/shard_map/all_gather | solution.py:282
  54.7 0.6 fusion
  55.4 0.1 collective-permute-start.3
  55.4 0.6 fusion.2
  56.1 1.2 %collective-permute-done.3 = f32[4,32,1024]{2,1,0:T(8,128)S(1)} collective-permute-done((f32[4,32,1024]{2,1,0:T(8,128)S(1)}, f32[4,32,1024]{2,1,0:T(8,128)S(1)}, u32[]{:S(2)}, u32[]{:S(2)}) %collective-permute-start.3) | collective-permute-done | bytes 524320 | tf_op jit(solution)/shard_map/ppermute | solution.py:257
  57.3 0.1 add.19
  57.4 11.5 %all_to_all.22.parts_ref = f32[4,32,1024]{2,1,0:T(8,128)S(1)} all-to-all(f32[4,32,1024]{2,1,0:T(8,128)S(1)} %add.19), channel_id=1, replica_groups=mesh['pairs'=4,'member'=2,'tile'=4] {'pairs'}, dimensions={0} | all-to-all | bytes 1048576 | tf_op jit(solution)/shard_map/all_to_all | solution.py:297
  69.0 9.8 %all_to_all.23 = f32[4,32,1024]{2,1,0:T(8,128)S(1)} all-to-all(f32[4,32,1024]{2,1,0:T(8,128)S(1)} %sum_copies.1), channel_id=1, replica_groups=mesh['pairs'=4,'member'=2,'tile'=4] {'pairs'}, dimensions={0} | all-to-all | bytes 1048576 | tf_op jit(solution)/shard_map/all_to_all | solution.py:298
  78.8 0.7 copy.12
  79.4 0.7 copy.13
  80.1 0.8 put.2.refs_0_
  80.9 0.0 collective-permute-done.4
  80.9 0.8 put.3
  (5 shorter events, 0.1 us)
Async XLA Ops:
  13.7 1.6 %collective-permute-start = (f32[4,136,128]{2,1,0:T(8,128)S(1)}, f32[4,136,128]{2,1,0:T(8,128)S(1)}, u32[]{:S(2)}, u32[]{:S(2)}) collective-permute-start(f32[4,136,128]{2,1,0:T(8,128)S(1)} %all_to_all.20.mine_ref), channel_id=1, source_target_pairs={{0,4},{4,0},{1,5},{5,1},{2,6},{6,2},{3,7},{7,3},{8,12},{12,8},{9,1... | collective-permute-start | bytes 835592 | tf_op jit(solution)/shard_map/ppermute | solution.py:257
  24.7 8.5 %collective-permute-start.1 = (f32[17,32,128]{2,1,0:T(8,128)S(1)}, f32[17,32,128]{2,1,0:T(8,128)S(1)}, u32[]{:S(2)}, u32[]{:S(2)}) collective-permute-start(f32[17,32,128]{2,1,0:T(8,128)S(1)} %pad_maximum_fusion), channel_id=1, source_target_pairs={{0,1},{1,2},{2,3},{4,5},{5,6},{6,7},{8,9},{9,10},{10,11},{12,13},{... | collective-permute-start | bytes 835592 | tf_op jit(solution)/shard_map/ppermute | solution.py:251
  28.2 9.1 %collective-permute-start.2 = (f32[17,32,128]{2,1,0:T(8,128)S(1)}, f32[17,32,128]{2,1,0:T(8,128)S(1)}, u32[]{:S(2)}, u32[]{:S(2)}) collective-permute-start(f32[17,32,128]{2,1,0:T(8,128)S(1)} %pad_maximum_fusion.1), channel_id=1, source_target_pairs={{1,0},{2,1},{3,2},{5,4},{6,5},{7,6},{9,8},{10,9},{11,10},{13,12},{... | collective-permute-start | bytes 835592 | tf_op jit(solution)/shard_map/ppermute | solution.py:252
  55.4 2.0 %collective-permute-start.3 = (f32[4,32,1024]{2,1,0:T(8,128)S(1)}, f32[4,32,1024]{2,1,0:T(8,128)S(1)}, u32[]{:S(2)}, u32[]{:S(2)}) collective-permute-start(f32[4,32,1024]{2,1,0:T(8,128)S(1)} %bitcast.24), channel_id=1, source_target_pairs={{0,4},{4,0},{1,5},{5,1},{2,6},{6,2},{3,7},{7,3},{8,12},{12,8},{9,1... | collective-permute-start | bytes 1572872 | tf_op jit(solution)/shard_map/ppermute | solution.py:257
  78.8 2.1 %collective-permute-start.4 = (f32[4,32,1024]{2,1,0:T(8,128)S(1)}, f32[4,32,1024]{2,1,0:T(8,128)S(1)}, u32[]{:S(2)}, u32[]{:S(2)}) collective-permute-start(f32[4,32,1024]{2,1,0:T(8,128)S(1)} %all_to_all.23), channel_id=1, source_target_pairs={{0,4},{4,0},{1,5},{5,1},{2,6},{6,2},{3,7},{7,3},{8,12},{12,8},{9,1... | collective-permute-start | bytes 1572872 | tf_op jit(solution)/shard_map/ppermute | solution.py:257

commit v3 on v2

--- a/solution.py
+++ b/solution.py
@@ -182,7 +182,9 @@
         cond_out[i] = cond[i + reach]
         value = pot[i + reach]
         pot_out[i] = value
-        traces_out[:, i * nz:(i + 1) * nz] = value * root
+        scaled = value * root
+        for place in range(traces_out.shape[0]):
+            traces_out[place, :, i * nz:(i + 1) * nz] = scaled
 
 
 def run_moves(depth, accept, root, *fields):
@@ -193,7 +195,7 @@
         out_shape=(
             pltpu.VMEM((width, ny, nz), jnp.float32),
             pltpu.VMEM((width, ny, nz), jnp.float32),
-            pltpu.VMEM((ny, width * nz), jnp.float32),
+            pltpu.VMEM((lax.axis_size("tile"), ny, width * nz), jnp.float32),
         ),
         in_specs=[SMEM] + [VMEM] * (1 + len(fields)),
         out_specs=(VMEM, VMEM, VMEM),
@@ -277,9 +279,9 @@
         depth, accept[:, 0], root, moved, noise, source, low, high
     )
 
-    rows = traces.shape[1] // (lax.axis_size("tile") * pair)
+    rows = traces.shape[2] // (lax.axis_size("tile") * pair)
     member = lax.axis_index("member")
-    piece = lax.all_gather(traces, "tile", axis=0, tiled=True)
+    piece = lax.all_to_all(traces, "tile", 0, 0, tiled=True).reshape(-1, traces.shape[2])
 
     def product(owner):
         columns = lax.dynamic_slice_in_dim(

time: 82.1 us -> 84.3 us (1.027)
  blocking collectives: 56.7 us -> 41.2 us
  waiting for transfers between devices: 10.6 us -> 23.6 us
  starting transfers between devices: 4.87 us -> 8.71 us
    all_gather x1 -> x0, blocking collectives: 15.6 us -> none  [local(): piece = lax.all_gather(traces, 'tile', axis=0, tiled=True)]
    all_to_all x0 -> x1, waiting for transfers between devices: none -> 12.4 us  [local(): lax.all_to_all(traces, 'tile', 0, 0, tiled=True)]
    all_to_all x0 -> x1, starting transfers between devices: none -> 3.85 us  [local(): lax.all_to_all(traces, 'tile', 0, 0, tiled=True)]
  transfers between devices with their start and end apart: 5 -> 6, of which waited for: 4 -> 5; matrix products, arithmetic and copies ran while one was open for 2% -> 2% of each run, Pallas kernels for 1% -> 1%
where the time goes in v3:
time: 84.3 us; the launch traced here: 83.8 us
  blocking collectives  41.2 us (49%)
  waiting for transfers between devices  23.6 us (28%)
  starting transfers between devices  8.71 us (10%)
  Pallas kernels  6.21 us (7%)
  local copies, waits for them, and re-layouts  1.52 us (2%)
  between operations  1.4 us (2%)
  matrix products  1.16 us (1%)
    all_to_all x1, waiting for transfers between devices, local(): lax.all_to_all(traces, 'tile', 0, 0, tiled=True)  12.4 us
    all_to_all x1, blocking collectives, local(): parts = lax.all_to_all(product(member) + got, 'pairs', 0, 0, tiled=True)  11.5 us
    all_to_all x1, blocking collectives, local(): pieces = lax.all_to_all(pieces, 'pairs', 0, 0, tiled=True)  11.2 us
    all_to_all x1, blocking collectives, local(): mine = lax.all_to_all(sum_copies(parts), 'pairs', 0, 0, tiled=True)  9.81 us
    all_to_all x1, blocking collectives, local(): lax.all_to_all(chosen, 'pairs', 0, 0, tiled=True).reshape(2, width, ny, nz)  8.68 us
    ppermute x1, waiting for transfers between devices, exchange_halo(): high = lax.ppermute(low_edge, 'tile', backward)  4.16 us
    all_to_all x1, starting transfers between devices, local(): lax.all_to_all(traces, 'tile', 0, 0, tiled=True)  3.85 us
    ppermute x1, waiting for transfers between devices, exchange_halo(): low = lax.ppermute(high_edge, 'tile', forward)  3.68 us
  transfers between devices with their start and end apart: 6, of which 5 were waited for; matrix products, arithmetic and copies ran while one was open for 2% of the time, Pallas kernels for 1%

profile of v3, /device:TPU:0, one launch (start us, length us, event | category | flops | bytes accessed | tf_op | source)
XLA Modules:
  0.0 83.8 jit_solution(12519533431970634321)
XLA Ops:
  1.3 1.2 %pack.1 = (f32[4,136,128]{2,1,0:T(8,128)S(1)}, f32[2,8,32,128]{3,2,1,0:T(8,128)S(1)}, f32[8,32,128]{2,1,0:T(8,128)S(1)}, f32[9,32,128]{2,1,0:T(8,128)S(1)}, f32[9,32,128]{2,1,0:T(8,128)S(1)}) custom-call(f32[1]{0:T(128)S(6)} %copy.18.weight_ref, f32[256,128]{1,0:T(8,128)} %bitcast.38, f32[256,128]{1,0:T(8,128)} %bitcast.39, f32[2,8,32,128]{3,2,1,0:T(8,128)} %bitcast.37, ...), custom_call_target="tpu_custom_call" | custom-call | tf_op jit(solution)/shard_map/pack/pallas_call | solution.py:58
  2.5 11.2 %all_to_all.25.mine_ref = f32[4,136,128]{2,1,0:T(8,128)S(1)} all-to-all(f32[4,136,128]{2,1,0:T(8,128)S(1)} %get-tuple-element.13), channel_id=1, replica_groups=mesh['pairs'=4,'member'=2,'tile'=4] {'pairs'}, dimensions={0} | all-to-all | bytes 557056 | tf_op jit(solution)/shard_map/all_to_all | solution.py:271
  13.7 1.6 %collective-permute-done.other_ref = f32[4,136,128]{2,1,0:T(8,128)S(1)} collective-permute-done((f32[4,136,128]{2,1,0:T(8,128)S(1)}, f32[4,136,128]{2,1,0:T(8,128)S(1)}, u32[]{:S(2)}, u32[]{:S(2)}) %collective-permute-start) | collective-permute-done | bytes 278560 | tf_op jit(solution)/shard_map/ppermute | solution.py:259
  15.2 0.7 choose.1
  16.0 8.7 %all_to_all.26 = f32[4,128,128]{2,1,0:T(8,128)S(1)} all-to-all(f32[4,128,128]{2,1,0:T(8,128)S(1)} %get-tuple-element.15), channel_id=1, replica_groups=mesh['pairs'=4,'member'=2,'tile'=4] {'pairs'}, dimensions={0} | all-to-all | bytes 524288 | tf_op jit(solution)/shard_map/all_to_all | solution.py:273
  24.7 3.5 %collective-permute-start.1 = (f32[17,32,128]{2,1,0:T(8,128)S(1)}, f32[17,32,128]{2,1,0:T(8,128)S(1)}, u32[]{:S(2)}, u32[]{:S(2)}) collective-permute-start(f32[17,32,128]{2,1,0:T(8,128)S(1)} %pad_maximum_fusion), channel_id=1, source_target_pairs={{0,1},{1,2},{2,3},{4,5},{5,6},{6,7},{8,9},{9,10},{10,11},{12,13},{... | collective-permute-start | bytes 835592 | tf_op jit(solution)/shard_map/ppermute | solution.py:253
  28.2 1.3 %collective-permute-start.2 = (f32[17,32,128]{2,1,0:T(8,128)S(1)}, f32[17,32,128]{2,1,0:T(8,128)S(1)}, u32[]{:S(2)}, u32[]{:S(2)}) collective-permute-start(f32[17,32,128]{2,1,0:T(8,128)S(1)} %pad_maximum_fusion.1), channel_id=1, source_target_pairs={{1,0},{2,1},{3,2},{5,4},{6,5},{7,6},{9,8},{10,9},{11,10},{13,12},{... | collective-permute-start | bytes 835592 | tf_op jit(solution)/shard_map/ppermute | solution.py:254
  29.5 3.7 %collective-permute-done.1.low_ref = f32[17,32,128]{2,1,0:T(8,128)S(1)} collective-permute-done((f32[17,32,128]{2,1,0:T(8,128)S(1)}, f32[17,32,128]{2,1,0:T(8,128)S(1)}, u32[]{:S(2)}, u32[]{:S(2)}) %collective-permute-start.1) | collective-permute-done | bytes 278560 | tf_op jit(solution)/shard_map/ppermute | solution.py:253
  33.2 4.2 %collective-permute-done.2.high_ref = f32[17,32,128]{2,1,0:T(8,128)S(1)} collective-permute-done((f32[17,32,128]{2,1,0:T(8,128)S(1)}, f32[17,32,128]{2,1,0:T(8,128)S(1)}, u32[]{:S(2)}, u32[]{:S(2)}) %collective-permute-start.2) | collective-permute-done | bytes 278560 | tf_op jit(solution)/shard_map/ppermute | solution.py:254
  37.4 2.6 %moves.1 = (f32[8,32,128]{2,1,0:T(8,128)S(1)}, f32[8,32,128]{2,1,0:T(8,128)S(1)}, f32[4,32,1024]{2,1,0:T(8,128)}) custom-call(s32[2]{0:T(128)} %bitcast.40, f32[8,128]{1,0:T(8,128)S(1)} %get-tuple-element.14.root_ref, f32[2,8,32,128]{3,2,1,0:T(8,128)S(1)} %bitcast.27, f32[2,8,32,128]{3,2,1,0:T(8,128)S(1)} %get-tuple-element.16.noise_ref, ...), custom_call_target="tpu_custom_call" | custom-call | tf_op jit(solution)/shard_map/moves/pallas_call | solution.py:193
  40.0 3.8 %all-to-all-start.2 = ((f32[4,32,1024]{2,1,0:T(8,128)}), f32[4,32,1024]{2,1,0:T(8,128)S(1)}, u32[]{:S(2)}, u32[]{:S(2)}) async-start(f32[4,32,1024]{2,1,0:T(8,128)} %get-tuple-element.22), calls=%async_computation.2 | async-start | bytes 1048576 | tf_op jit(solution)/shard_map/all_to_all | solution.py:284
  43.8 12.4 %all-to-all-done.2 = f32[4,32,1024]{2,1,0:T(8,128)S(1)} async-done(((f32[4,32,1024]{2,1,0:T(8,128)}), f32[4,32,1024]{2,1,0:T(8,128)S(1)}, u32[]{:S(2)}, u32[]{:S(2)}) %all-to-all-start.2) | async-done | bytes 524320 | tf_op jit(solution)/shard_map/all_to_all | solution.py:284
  56.2 0.1 copy.14
  56.3 0.6 fusion.1
  56.9 0.1 collective-permute-start.3
  57.0 0.1 copy.13
  57.1 1.8 %collective-permute-done.3 = f32[4,32,1024]{2,1,0:T(8,128)S(1)} collective-permute-done((f32[4,32,1024]{2,1,0:T(8,128)S(1)}, f32[4,32,1024]{2,1,0:T(8,128)S(1)}, u32[]{:S(2)}, u32[]{:S(2)}) %collective-permute-start.3) | collective-permute-done | bytes 524320 | tf_op jit(solution)/shard_map/ppermute | solution.py:259
  58.9 0.6 convolution_add_fusion
  59.5 11.5 %all_to_all.27.parts_ref = f32[4,32,1024]{2,1,0:T(8,128)S(1)} all-to-all(f32[4,32,1024]{2,1,0:T(8,128)S(1)} %convolution_add_fusion), channel_id=1, replica_groups=mesh['pairs'=4,'member'=2,'tile'=4] {'pairs'}, dimensions={0} | all-to-all | bytes 1048576 | tf_op jit(solution)/shard_map/all_to_all | solution.py:299
  71.1 9.8 %all_to_all.28 = f32[4,32,1024]{2,1,0:T(8,128)S(1)} all-to-all(f32[4,32,1024]{2,1,0:T(8,128)S(1)} %sum_copies.1), channel_id=1, replica_groups=mesh['pairs'=4,'member'=2,'tile'=4] {'pairs'}, dimensions={0} | all-to-all | bytes 1048576 | tf_op jit(solution)/shard_map/all_to_all | solution.py:300
  80.9 0.7 copy.16
  81.5 0.7 copy.17
  82.2 0.8 put.2.refs_0_
  83.0 0.8 put.3
  (8 shorter events, 0.1 us)
Async XLA Ops:
  13.7 1.6 %collective-permute-start = (f32[4,136,128]{2,1,0:T(8,128)S(1)}, f32[4,136,128]{2,1,0:T(8,128)S(1)}, u32[]{:S(2)}, u32[]{:S(2)}) collective-permute-start(f32[4,136,128]{2,1,0:T(8,128)S(1)} %all_to_all.25.mine_ref), channel_id=1, source_target_pairs={{0,4},{4,0},{1,5},{5,1},{2,6},{6,2},{3,7},{7,3},{8,12},{12,8},{9,1... | collective-permute-start | bytes 835592 | tf_op jit(solution)/shard_map/ppermute | solution.py:259
  24.7 8.5 %collective-permute-start.1 = (f32[17,32,128]{2,1,0:T(8,128)S(1)}, f32[17,32,128]{2,1,0:T(8,128)S(1)}, u32[]{:S(2)}, u32[]{:S(2)}) collective-permute-start(f32[17,32,128]{2,1,0:T(8,128)S(1)} %pad_maximum_fusion), channel_id=1, source_target_pairs={{0,1},{1,2},{2,3},{4,5},{5,6},{6,7},{8,9},{9,10},{10,11},{12,13},{... | collective-permute-start | bytes 835592 | tf_op jit(solution)/shard_map/ppermute | solution.py:253
  28.2 9.1 %collective-permute-start.2 = (f32[17,32,128]{2,1,0:T(8,128)S(1)}, f32[17,32,128]{2,1,0:T(8,128)S(1)}, u32[]{:S(2)}, u32[]{:S(2)}) collective-permute-start(f32[17,32,128]{2,1,0:T(8,128)S(1)} %pad_maximum_fusion.1), channel_id=1, source_target_pairs={{1,0},{2,1},{3,2},{5,4},{6,5},{7,6},{9,8},{10,9},{11,10},{13,12},{... | collective-permute-start | bytes 835592 | tf_op jit(solution)/shard_map/ppermute | solution.py:254
  40.0 16.3 %all-to-all-start.2 = ((f32[4,32,1024]{2,1,0:T(8,128)}), f32[4,32,1024]{2,1,0:T(8,128)S(1)}, u32[]{:S(2)}, u32[]{:S(2)}) async-start(f32[4,32,1024]{2,1,0:T(8,128)} %get-tuple-element.22), calls=%async_computation.2 | async-start | bytes 1048576 | tf_op jit(solution)/shard_map/all_to_all | solution.py:284
  56.9 2.0 %collective-permute-start.3 = (f32[4,32,1024]{2,1,0:T(8,128)S(1)}, f32[4,32,1024]{2,1,0:T(8,128)S(1)}, u32[]{:S(2)}, u32[]{:S(2)}) collective-permute-start(f32[4,32,1024]{2,1,0:T(8,128)S(1)} %fusion.1), channel_id=1, source_target_pairs={{0,4},{4,0},{1,5},{5,1},{2,6},{6,2},{3,7},{7,3},{8,12},{12,8},{9,1... | collective-permute-start | bytes 1572872 | tf_op jit(solution)/shard_map/ppermute | solution.py:259
  80.9 2.1 %collective-permute-start.4 = (f32[4,32,1024]{2,1,0:T(8,128)S(1)}, f32[4,32,1024]{2,1,0:T(8,128)S(1)}, u32[]{:S(2)}, u32[]{:S(2)}) collective-permute-start(f32[4,32,1024]{2,1,0:T(8,128)S(1)} %all_to_all.28), channel_id=1, source_target_pairs={{0,4},{4,0},{1,5},{5,1},{2,6},{6,2},{3,7},{7,3},{8,12},{12,8},{9,1... | collective-permute-start | bytes 1572872 | tf_op jit(solution)/shard_map/ppermute | solution.py:259

commit v4 on v2

--- a/solution.py
+++ b/solution.py
@@ -23,16 +23,15 @@
 
 
 def pack_kernel(
-    rows, depth, weight_ref, cond_ref, pot_ref, noise_ref, source_ref,
-    pieces_ref, noise_out, source_out, low_ref, high_ref, sems,
+    depth, weight_ref, cond_ref, pot_ref, noise_ref, source_ref,
+    copies_ref, noise_out, source_out, low_ref, high_ref, sems,
 ):
     moves = noise_ref.shape[0]
+    rows = cond_ref.shape[0]
     pairs = []
-    for piece in range(pieces_ref.shape[0]):
-        row = piece * rows
-        field = cond_ref if row < cond_ref.shape[0] else pot_ref
-        row %= cond_ref.shape[0]
-        pairs.append((field.at[pl.ds(row, rows)], pieces_ref.at[piece, pl.ds(0, rows)]))
+    for place in range(copies_ref.shape[0]):
+        pairs.append((cond_ref, copies_ref.at[place, pl.ds(0, rows)]))
+        pairs.append((pot_ref, copies_ref.at[place, pl.ds(rows, rows)]))
     pairs += [(noise_ref, noise_out), (source_ref, source_out)]
     at = 0
     for field, h in zip([noise_ref.at[m] for m in range(moves)] + [source_ref], depth):
@@ -44,19 +43,20 @@
     ]
     for copy in copies:
         copy.start()
-    weight = jnp.full((8, pieces_ref.shape[2]), weight_ref[0], jnp.float32)
-    for piece in range(pieces_ref.shape[0]):
-        pieces_ref[piece, rows:rows + 8] = weight
+    weight = jnp.full((8, copies_ref.shape[2]), weight_ref[0], jnp.float32)
+    for place in range(copies_ref.shape[0]):
+        copies_ref[place, 2 * rows:2 * rows + 8] = weight
     for copy in copies:
         copy.wait()
 
 
-def pack(weights, log_cond, potential, noise, source, pairs, depth):
+def pack(weights, log_cond, potential, noise, source, depth):
     _, ny, nz = source.shape
-    rows = 2 * log_cond.size // (pairs * nz)
+    pairs = lax.axis_size("pairs")
+    rows = 2 * source.size // nz
     edge = pltpu.VMEM((sum(depth), ny, nz), jnp.float32)
     return pl.pallas_call(
-        functools.partial(pack_kernel, rows, depth),
+        functools.partial(pack_kernel, depth),
         out_shape=(
             pltpu.VMEM((pairs, rows + 8, nz), jnp.float32),
             pltpu.VMEM(noise.shape, jnp.float32),
@@ -66,39 +66,76 @@
         ),
         in_specs=[SMEM, ANY, ANY, ANY, ANY],
         out_specs=(VMEM,) * 5,
-        scratch_shapes=[pltpu.SemaphoreType.DMA((pairs + 2 + 2 * len(depth),))],
+        scratch_shapes=[pltpu.SemaphoreType.DMA((2 * pairs + 2 + 2 * len(depth),))],
         name="pack",
     )(weights, log_cond.reshape(-1, nz), potential.reshape(-1, nz), noise, source)
 
 
-def choose_kernel(parents_ref, weight_ref, mine_ref, other_ref, chosen_ref, root_ref):
+def pick_kernel(parents_ref, held_ref, keep_ref, give_ref):
+    pairs, rows, _ = held_ref.shape
+    rows -= 8
     member = lax.axis_index("member")
-    rows = chosen_ref.shape[1]
-    for place in range(chosen_ref.shape[0]):
-        parent = parents_ref[place * pair + member]
-        here = lax.rem(parent, pair) == member
-        at = lax.div(parent, pair)
-        chosen_ref[place] = jnp.where(
-            here, mine_ref[at, pl.ds(0, rows)], other_ref[at, pl.ds(0, rows)]
-        )
-    total = jnp.zeros_like(root_ref)
-    for place in range(chosen_ref.shape[0]):
-        total += mine_ref[place, rows:rows + 8] + other_ref[place, rows:rows + 8]
-    root_ref[...] = jnp.sqrt(weight_ref[0] / total)
-
-
-def choose(parents, weights, mine, other):
-    pairs, rows, nz = mine.shape
-    return pl.pallas_call(
-        choose_kernel,
+    first = lax.axis_index("pairs") * pair
+    total = held_ref[0, rows:rows + 8]
+    for place in range(1, pairs):
+        total += held_ref[place, rows:rows + 8]
+    for out_ref, device in [(keep_ref, first + member), (give_ref, first + 1 - member)]:
+        out_ref[0:rows] = held_ref[lax.div(parents_ref[device], pair), 0:rows]
+        out_ref[rows:rows + 8] = total
+
+
+def pick(parents, held):
+    out = pltpu.VMEM(held.shape[1:], jnp.float32)
+    return pl.pallas_call(
+        pick_kernel,
+        out_shape=(out, out),
+        in_specs=[SMEM, VMEM],
+        out_specs=(VMEM, VMEM),
+        name="pick",
+    )(parents, in_vmem(held))
+
+
+def settle_kernel(
+    reach, parents_ref, weight_ref, keep_ref, got_ref, low_edge_ref, high_edge_ref,
+    moved_ref, low_ref, high_ref, root_ref,
+):
+    _, width, ny, nz = moved_ref.shape
+    member = lax.axis_index("member")
+    parent = parents_ref[lax.axis_index("pairs") * pair + member]
+    here = lax.rem(parent, pair) == member
+    for field in range(2):
+        for i in range(width):
+            row = (field * width + i) * ny
+            layer = jnp.where(here, keep_ref[row:row + ny], got_ref[row:row + ny])
+            moved_ref[field, i] = layer
+            if i < reach:
+                low_ref[field * reach + i] = layer
+            if i >= width - reach:
+                high_ref[field * reach + i - width + reach] = layer
+    low_ref[2 * reach:] = low_edge_ref[...]
+    high_ref[2 * reach:] = high_edge_ref[...]
+    rows = 2 * width * ny
+    root_ref[...] = jnp.sqrt(
+        weight_ref[0] / (keep_ref[rows:rows + 8] + got_ref[rows:rows + 8])
+    )
+
+
+def settle(reach, parents, weights, keep, got, low_edge, high_edge):
+    depth, ny, nz = low_edge.shape
+    edge = pltpu.VMEM((2 * reach + depth, ny, nz), jnp.float32)
+    width = (keep.shape[0] - 8) // (2 * ny)
+    return pl.pallas_call(
+        functools.partial(settle_kernel, reach),
         out_shape=(
-            pltpu.VMEM((pairs, rows - 8, nz), jnp.float32),
+            pltpu.VMEM((2, width, ny, nz), jnp.float32),
+            edge,
+            edge,
             pltpu.VMEM((8, nz), jnp.float32),
         ),
-        in_specs=[SMEM, SMEM, VMEM, VMEM],
-        out_specs=(VMEM, VMEM),
-        name="choose",
-    )(parents, weights, in_vmem(mine), in_vmem(other))
+        in_specs=[SMEM, SMEM] + [VMEM] * 4,
+        out_specs=(VMEM,) * 4,
+        name="settle",
+    )(parents, weights, *[in_vmem(a) for a in (keep, got, low_edge, high_edge)])
 
 
 def six_sum(before, here, after, edge):
@@ -263,16 +300,15 @@
     reach = 2 * moves
 
     depth = tuple(reach - 2 * m for m in range(moves)) + (reach - 1,)
-    pieces, noise, source, low_edge, high_edge = pack(
-        weights, log_cond, potential, noise[:, 0], source, lax.axis_size("pairs"), depth
-    )
-    pieces = lax.all_to_all(pieces, "pairs", 0, 0, tiled=True)
-    chosen, root = choose(parents, weights, pieces, swap(pieces))
-    moved = lax.all_to_all(chosen, "pairs", 0, 0, tiled=True).reshape(2, width, ny, nz)
-    low, high = exchange_halo(
-        jnp.concatenate([moved[:, :reach].reshape(-1, ny, nz), low_edge]),
-        jnp.concatenate([moved[:, width - reach:].reshape(-1, ny, nz), high_edge]),
-    )
+    bundles, noise, source, low_edge, high_edge = pack(
+        weights, log_cond, potential, noise[:, 0], source, depth
+    )
+    held = lax.all_to_all(bundles, "pairs", 0, 0, tiled=True)
+    keep, give = pick(parents, held)
+    moved, low_edge, high_edge, root = settle(
+        reach, parents, weights, keep, swap(give), low_edge, high_edge
+    )
+    low, high = exchange_halo(low_edge, high_edge)
     conduct, pot, traces = run_moves(
         depth, accept[:, 0], root, moved, noise, source, low, high
     )

time: 82.1 us -> 85.3 us (1.039)
  waiting for transfers between devices: 10.6 us -> 11.8 us
  Pallas kernels: 5.39 us -> 6.58 us
  blocking collectives: 56.7 us -> 57.6 us
    ppermute x1, waiting for transfers between devices: 3.67 us -> 4.87 us  [exchange_halo(): low = lax.ppermute(high_edge, 'tile', forward)]
    pallas_call x2 -> x3, Pallas kernels: 1.95 us -> 3.16 us  [the longest x1 1.7 us: pack(): pl.pallas_call(functools.partial(pack_kernel, depth), out_shape=(pltpu.VM...]
    all_to_all x2 -> x1, blocking collectives: 19.8 us -> 19.6 us  [local(): held = lax.all_to_all(bundles, 'pairs', 0, 0, tiled=True)]
where the time goes in v4:
time: 85.3 us; the launch traced here: 84.9 us
  blocking collectives  57.6 us (68%)
  waiting for transfers between devices  11.8 us (14%)
  Pallas kernels  6.58 us (8%)
  starting transfers between devices  4.93 us (6%)
  between operations  1.4 us (2%)
  local copies, waits for them, and re-layouts  1.31 us (2%)
  matrix products  1.27 us (1%)
    all_to_all x1, blocking collectives, local(): held = lax.all_to_all(bundles, 'pairs', 0, 0, tiled=True)  19.6 us
    all_gather x1, blocking collectives, local(): piece = lax.all_gather(traces, 'tile', axis=0, tiled=True)  16.2 us
    all_to_all x1, blocking collectives, local(): parts = lax.all_to_all(product(member) + got, 'pairs', 0, 0, tiled=True)  11.5 us
    all_to_all x1, blocking collectives, local(): mine = lax.all_to_all(sum_copies(parts), 'pairs', 0, 0, tiled=True)  10.3 us
    ppermute x1, waiting for transfers between devices, exchange_halo(): low = lax.ppermute(high_edge, 'tile', forward)  4.87 us
    ppermute x1, waiting for transfers between devices, exchange_halo(): high = lax.ppermute(low_edge, 'tile', backward)  4.13 us
    ppermute x1, starting transfers between devices, exchange_halo(): low = lax.ppermute(high_edge, 'tile', forward)  3.5 us
    ppermute x3, waiting for transfers between devices, swap(): return lax.ppermute(block, 'member', [(0, 1), (1, 0)])  2.78 us
  transfers between devices with their start and end apart: 5, of which 4 were waited for; matrix products, arithmetic and copies ran while one was open for 2% of the time, Pallas kernels for 1%

profile of v4, /device:TPU:0, one launch (start us, length us, event | category | flops | bytes accessed | tf_op | source)
XLA Modules:
  0.0 84.9 jit_solution(14886101979830998907)
XLA Ops:
  1.3 1.7 %pack.1 = (f32[4,520,128]{2,1,0:T(8,128)S(1)}, f32[2,8,32,128]{3,2,1,0:T(8,128)S(1)}, f32[8,32,128]{2,1,0:T(8,128)S(1)}, f32[9,32,128]{2,1,0:T(8,128)S(1)}, f32[9,32,128]{2,1,0:T(8,128)S(1)}) custom-call(f32[1]{0:T(128)S(6)} %copy.14.weight_ref, f32[256,128]{1,0:T(8,128)} %bitcast.19, f32[256,128]{1,0:T(8,128)} %bitcast.20, f32[2,8,32,128]{3,2,1,0:T(8,128)} %bitcast.18, ...), custom_call_target="tpu_custom_call" | custom-call | tf_op jit(solution)/shard_map/pack/pallas_call | solution.py:58
  3.0 19.6 %all_to_all.15.held_ref = f32[4,520,128]{2,1,0:T(8,128)S(1)} all-to-all(f32[4,520,128]{2,1,0:T(8,128)S(1)} %get-tuple-element.17), channel_id=1, replica_groups=mesh['pairs'=4,'member'=2,'tile'=4] {'pairs'}, dimensions={0} | all-to-all | bytes 2129920 | tf_op jit(solution)/shard_map/all_to_all | solution.py:306
  22.6 0.7 pick.1
  23.3 0.1 collective-permute-start
  23.4 1.5 %collective-permute-done.got_ref = f32[520,128]{1,0:T(8,128)S(1)} collective-permute-done((f32[520,128]{1,0:T(8,128)S(1)}, f32[520,128]{1,0:T(8,128)S(1)}, u32[]{:S(2)}, u32[]{:S(2)}) %collective-permute-start) | collective-permute-done | bytes 266272 | tf_op jit(solution)/shard_map/ppermute | solution.py:294
  24.9 0.7 settle.1
  25.6 3.5 %collective-permute-start.1 = (f32[17,32,128]{2,1,0:T(8,128)S(1)}, f32[17,32,128]{2,1,0:T(8,128)S(1)}, u32[]{:S(2)}, u32[]{:S(2)}) collective-permute-start(f32[17,32,128]{2,1,0:T(8,128)S(1)} %get-tuple-element.26), channel_id=1, source_target_pairs={{0,1},{1,2},{2,3},{4,5},{5,6},{6,7},{8,9},{9,10},{10,11},{12,13},{... | collective-permute-start | bytes 835592 | tf_op jit(solution)/shard_map/ppermute | solution.py:288
  29.2 1.3 %collective-permute-start.2 = (f32[17,32,128]{2,1,0:T(8,128)S(1)}, f32[17,32,128]{2,1,0:T(8,128)S(1)}, u32[]{:S(2)}, u32[]{:S(2)}) collective-permute-start(f32[17,32,128]{2,1,0:T(8,128)S(1)} %get-tuple-element.27), channel_id=1, source_target_pairs={{1,0},{2,1},{3,2},{5,4},{6,5},{7,6},{9,8},{10,9},{11,10},{13,12},{... | collective-permute-start | bytes 835592 | tf_op jit(solution)/shard_map/ppermute | solution.py:289
  30.5 4.9 %collective-permute-done.1.low_ref = f32[17,32,128]{2,1,0:T(8,128)S(1)} collective-permute-done((f32[17,32,128]{2,1,0:T(8,128)S(1)}, f32[17,32,128]{2,1,0:T(8,128)S(1)}, u32[]{:S(2)}, u32[]{:S(2)}) %collective-permute-start.1) | collective-permute-done | bytes 278560 | tf_op jit(solution)/shard_map/ppermute | solution.py:288
  35.3 4.1 %collective-permute-done.2.high_ref = f32[17,32,128]{2,1,0:T(8,128)S(1)} collective-permute-done((f32[17,32,128]{2,1,0:T(8,128)S(1)}, f32[17,32,128]{2,1,0:T(8,128)S(1)}, u32[]{:S(2)}, u32[]{:S(2)}) %collective-permute-start.2) | collective-permute-done | bytes 278560 | tf_op jit(solution)/shard_map/ppermute | solution.py:289
  39.5 1.8 %moves.1 = (f32[8,32,128]{2,1,0:T(8,128)S(1)}, f32[8,32,128]{2,1,0:T(8,128)S(1)}, f32[32,1024]{1,0:T(8,128)S(1)}) custom-call(s32[2]{0:T(128)} %bitcast.21, f32[8,128]{1,0:T(8,128)S(1)} %get-tuple-element.22.root_ref, f32[2,8,32,128]{3,2,1,0:T(8,128)S(1)} %get-tuple-element.23.moved_ref, f32[2,8,32,128]{3,2,1,0:T(8,128)S(1)} %get-tuple-element.24.noise_ref, ...), custom_call_target="tpu_custom_call" | custom-call | tf_op jit(solution)/shard_map/moves/pallas_call | solution.py:228
  41.2 16.2 %all_gather.3 = f32[128,1024]{1,0:T(8,128)S(1)} all-gather(f32[32,1024]{1,0:T(8,128)S(1)} %get-tuple-element.30), channel_id=1, replica_groups=mesh['pairs'=4,'member'=2,'tile'=4] {'tile'}, dimensions={0}, use_global_device_ids=true | all-gather | bytes 655360 | tf_op jit(solution)/shard_map/all_gather | solution.py:318
  57.4 0.6 fusion
  58.0 0.1 collective-permute-start.3
  58.1 0.6 fusion.2
  58.8 1.2 %collective-permute-done.3 = f32[4,32,1024]{2,1,0:T(8,128)S(1)} collective-permute-done((f32[4,32,1024]{2,1,0:T(8,128)S(1)}, f32[4,32,1024]{2,1,0:T(8,128)S(1)}, u32[]{:S(2)}, u32[]{:S(2)}) %collective-permute-start.3) | collective-permute-done | bytes 524320 | tf_op jit(solution)/shard_map/ppermute | solution.py:294
  60.0 0.1 add.19
  60.1 11.5 %all_to_all.16.parts_ref = f32[4,32,1024]{2,1,0:T(8,128)S(1)} all-to-all(f32[4,32,1024]{2,1,0:T(8,128)S(1)} %add.19), channel_id=1, replica_groups=mesh['pairs'=4,'member'=2,'tile'=4] {'pairs'}, dimensions={0} | all-to-all | bytes 1048576 | tf_op jit(solution)/shard_map/all_to_all | solution.py:333
  71.6 10.3 %all_to_all.17 = f32[4,32,1024]{2,1,0:T(8,128)S(1)} all-to-all(f32[4,32,1024]{2,1,0:T(8,128)S(1)} %sum_copies.1), channel_id=1, replica_groups=mesh['pairs'=4,'member'=2,'tile'=4] {'pairs'}, dimensions={0} | all-to-all | bytes 1048576 | tf_op jit(solution)/shard_map/all_to_all | solution.py:334
  81.9 0.0 collective-permute-start.4
  81.9 0.7 copy.12
  82.6 0.7 copy.13
  83.3 0.8 put.2.refs_0_
  84.1 0.8 put.3
  (2 shorter events, 0.0 us)
Async XLA Ops:
  23.3 1.6 %collective-permute-start = (f32[520,128]{1,0:T(8,128)S(1)}, f32[520,128]{1,0:T(8,128)S(1)}, u32[]{:S(2)}, u32[]{:S(2)}) collective-permute-start(f32[520,128]{1,0:T(8,128)S(1)} %get-tuple-element.19), channel_id=1, source_target_pairs={{0,4},{4,0},{1,5},{5,1},{2,6},{6,2},{3,7},{7,3},{8,12},{12,8},{9,1... | collective-permute-start | bytes 798728 | tf_op jit(solution)/shard_map/ppermute | solution.py:294
  25.6 9.7 %collective-permute-start.1 = (f32[17,32,128]{2,1,0:T(8,128)S(1)}, f32[17,32,128]{2,1,0:T(8,128)S(1)}, u32[]{:S(2)}, u32[]{:S(2)}) collective-permute-start(f32[17,32,128]{2,1,0:T(8,128)S(1)} %get-tuple-element.26), channel_id=1, source_target_pairs={{0,1},{1,2},{2,3},{4,5},{5,6},{6,7},{8,9},{9,10},{10,11},{12,13},{... | collective-permute-start | bytes 835592 | tf_op jit(solution)/shard_map/ppermute | solution.py:288
  29.2 10.3 %collective-permute-start.2 = (f32[17,32,128]{2,1,0:T(8,128)S(1)}, f32[17,32,128]{2,1,0:T(8,128)S(1)}, u32[]{:S(2)}, u32[]{:S(2)}) collective-permute-start(f32[17,32,128]{2,1,0:T(8,128)S(1)} %get-tuple-element.27), channel_id=1, source_target_pairs={{1,0},{2,1},{3,2},{5,4},{6,5},{7,6},{9,8},{10,9},{11,10},{13,12},{... | collective-permute-start | bytes 835592 | tf_op jit(solution)/shard_map/ppermute | solution.py:289
  58.0 2.0 %collective-permute-start.3 = (f32[4,32,1024]{2,1,0:T(8,128)S(1)}, f32[4,32,1024]{2,1,0:T(8,128)S(1)}, u32[]{:S(2)}, u32[]{:S(2)}) collective-permute-start(f32[4,32,1024]{2,1,0:T(8,128)S(1)} %bitcast.17), channel_id=1, source_target_pairs={{0,4},{4,0},{1,5},{5,1},{2,6},{6,2},{3,7},{7,3},{8,12},{12,8},{9,1... | collective-permute-start | bytes 1572872 | tf_op jit(solution)/shard_map/ppermute | solution.py:294
  81.9 2.1 %collective-permute-start.4 = (f32[4,32,1024]{2,1,0:T(8,128)S(1)}, f32[4,32,1024]{2,1,0:T(8,128)S(1)}, u32[]{:S(2)}, u32[]{:S(2)}) collective-permute-start(f32[4,32,1024]{2,1,0:T(8,128)S(1)} %all_to_all.17), channel_id=1, source_target_pairs={{0,4},{4,0},{1,5},{5,1},{2,6},{6,2},{3,7},{7,3},{8,12},{12,8},{9,1... | collective-permute-start | bytes 1572872 | tf_op jit(solution)/shard_map/ppermute | solution.py:294

commit v5 on v1

--- a/solution.py
+++ b/solution.py
@@ -18,16 +18,20 @@
 ANY = pl.BlockSpec(memory_space=pl.ANY)
 
 
+def in_smem(array):
+    return pltpu.with_memory_space_constraint(array, pltpu.SMEM)
+
+
 def in_vmem(array):
     return pltpu.with_memory_space_constraint(array, pltpu.VMEM)
 
 
 def pack_kernel(
-    rows, depth, weight_ref, cond_ref, pot_ref, noise_ref, source_ref,
-    pieces_ref, noise_out, source_out, low_ref, high_ref, sems,
+    rows, depth, weight_ref, parents_ref, accept_ref, cond_ref, pot_ref, noise_ref, source_ref,
+    weight_out, parents_out, accept_out, pieces_ref, noise_out, source_out, low_ref, high_ref, sems,
 ):
     moves = noise_ref.shape[0]
-    pairs = []
+    pairs = [(weight_ref, weight_out), (parents_ref, parents_out), (accept_ref, accept_out)]
     for piece in range(pieces_ref.shape[0]):
         row = piece * rows
         field = cond_ref if row < cond_ref.shape[0] else pot_ref
@@ -44,31 +48,34 @@
     ]
     for copy in copies:
         copy.start()
-    weight = jnp.full((8, pieces_ref.shape[2]), weight_ref[0], jnp.float32)
+    for copy in copies:
+        copy.wait()
+    weight = jnp.full((8, pieces_ref.shape[2]), weight_out[0], jnp.float32)
     for piece in range(pieces_ref.shape[0]):
         pieces_ref[piece, rows:rows + 8] = weight
-    for copy in copies:
-        copy.wait()
-
-
-def pack(weights, log_cond, potential, noise, source, pairs, depth):
+
+
+def pack(weights, parents, accept, log_cond, potential, noise, source, pairs, depth):
     _, ny, nz = source.shape
     rows = 2 * log_cond.size // (pairs * nz)
     edge = pltpu.VMEM((sum(depth), ny, nz), jnp.float32)
     return pl.pallas_call(
         functools.partial(pack_kernel, rows, depth),
         out_shape=(
+            pltpu.SMEM(weights.shape, jnp.float32),
+            pltpu.SMEM(parents.shape, jnp.int32),
+            pltpu.SMEM(accept.shape, jnp.int32),
             pltpu.VMEM((pairs, rows + 8, nz), jnp.float32),
             pltpu.VMEM(noise.shape, jnp.float32),
             pltpu.VMEM(source.shape, jnp.float32),
             edge,
             edge,
         ),
-        in_specs=[SMEM, ANY, ANY, ANY, ANY],
-        out_specs=(VMEM,) * 5,
-        scratch_shapes=[pltpu.SemaphoreType.DMA((pairs + 2 + 2 * len(depth),))],
+        in_specs=[ANY] * 7,
+        out_specs=(SMEM,) * 3 + (VMEM,) * 5,
+        scratch_shapes=[pltpu.SemaphoreType.DMA((pairs + 5 + 2 * len(depth),))],
         name="pack",
-    )(weights, log_cond.reshape(-1, nz), potential.reshape(-1, nz), noise, source)
+    )(weights, parents, accept, log_cond.reshape(-1, nz), potential.reshape(-1, nz), noise, source)
 
 
 def choose_kernel(parents_ref, weight_ref, mine_ref, other_ref, chosen_ref, root_ref):
@@ -98,7 +105,7 @@
         in_specs=[SMEM, SMEM, VMEM, VMEM],
         out_specs=(VMEM, VMEM),
         name="choose",
-    )(parents, weights, in_vmem(mine), in_vmem(other))
+    )(in_smem(parents), in_smem(weights), in_vmem(mine), in_vmem(other))
 
 
 def six_sum(before, here, after, edge):
@@ -199,7 +206,7 @@
         out_specs=(VMEM, VMEM, VMEM),
         scratch_shapes=[pltpu.VMEM((span, ny, nz), jnp.float32)] * 5,
         name="moves",
-    )(accept, in_vmem(root), *[in_vmem(field) for field in fields])
+    )(in_smem(accept), in_vmem(root), *[in_vmem(field) for field in fields])
 
 
 def sum_copies_kernel(parts_ref, copies_ref):
@@ -220,14 +227,15 @@
     )(in_vmem(parts))
 
 
-def join_kernel(mine_ref, other_ref, out_ref, sems):
-    member = lax.axis_index("member")
-    rows = mine_ref.shape[0]
+def own_rows(ref, rows, owner):
+    return ref.at[pl.ds(pl.multiple_of(owner * rows, rows), rows)]
+
+
+def store_kernel(cond_ref, pot_ref, half_ref, cond_out, pot_out, rows_out, sems):
+    own = own_rows(rows_out, half_ref.shape[0], lax.axis_index("member"))
+    pairs = [(cond_ref, cond_out), (pot_ref, pot_out), (half_ref, own)]
     copies = [
-        pltpu.make_async_copy(
-            ref, out_ref.at[pl.ds(pl.multiple_of(owner * rows, rows), rows)], sems.at[i]
-        )
-        for i, (ref, owner) in enumerate([(mine_ref, member), (other_ref, 1 - member)])
+        pltpu.make_async_copy(here, there, sems.at[i]) for i, (here, there) in enumerate(pairs)
     ]
     for copy in copies:
         copy.start()
@@ -235,15 +243,38 @@
         copy.wait()
 
 
-def join(mine, other):
-    return pl.pallas_call(
-        join_kernel,
-        out_shape=jax.ShapeDtypeStruct((pair * mine.shape[0], mine.shape[1]), jnp.float32),
-        in_specs=[VMEM, VMEM],
+def store(conduct, pot, half):
+    return pl.pallas_call(
+        store_kernel,
+        out_shape=(
+            jax.ShapeDtypeStruct(conduct.shape, jnp.float32),
+            jax.ShapeDtypeStruct(pot.shape, jnp.float32),
+            jax.ShapeDtypeStruct((pair * half.shape[0], half.shape[1]), jnp.float32),
+        ),
+        in_specs=[VMEM] * 3,
+        out_specs=(ANY,) * 3,
+        scratch_shapes=[pltpu.SemaphoreType.DMA((3,))],
+        name="store",
+    )(in_vmem(conduct), in_vmem(pot), in_vmem(half))
+
+
+def store_other_kernel(half_ref, held_ref, rows_out, sem):
+    other = own_rows(rows_out, half_ref.shape[0], 1 - lax.axis_index("member"))
+    copy = pltpu.make_async_copy(half_ref, other, sem)
+    copy.start()
+    copy.wait()
+
+
+def store_other(half, held):
+    return pl.pallas_call(
+        store_other_kernel,
+        out_shape=jax.ShapeDtypeStruct(held.shape, jnp.float32),
+        in_specs=[VMEM, ANY],
         out_specs=ANY,
-        scratch_shapes=[pltpu.SemaphoreType.DMA((2,))],
-        name="join",
-    )(in_vmem(mine), in_vmem(other))
+        scratch_shapes=[pltpu.SemaphoreType.DMA],
+        input_output_aliases={1: 0},
+        name="store_other",
+    )(in_vmem(half), held)
 
 
 def exchange_halo(low_edge, high_edge):
@@ -265,8 +296,9 @@
     reach = 2 * moves
 
     depth = tuple(reach - 2 * m for m in range(moves)) + (reach - 1,)
-    pieces, noise, source, low_edge, high_edge = pack(
-        weights, log_cond, potential, noise[:, 0], source, lax.axis_size("pairs"), depth
+    weights, parents, accept, pieces, noise, source, low_edge, high_edge = pack(
+        weights, parents, accept[:, 0], log_cond, potential, noise[:, 0], source,
+        lax.axis_size("pairs"), depth,
     )
     pieces = lax.all_to_all(pieces, "pairs", 0, 0, tiled=True)
     fixed_low, fixed_high = exchange_halo(low_edge, high_edge)
@@ -276,7 +308,7 @@
         moved[:, :reach].reshape(-1, ny, nz), moved[:, width - reach:].reshape(-1, ny, nz)
     )
     conduct, pot, traces = run_moves(
-        depth, accept[:, 0], root, moved, noise, source, moved_low, moved_high, fixed_low, fixed_high
+        depth, accept, root, moved, noise, source, moved_low, moved_high, fixed_low, fixed_high
     )
 
     rows = traces.shape[1] // (lax.axis_size("tile") * pair)
@@ -291,14 +323,16 @@
             columns,
             piece,
             (((0,), (0,)), ((), ())),
-            precision=lax.Precision.HIGHEST,
+            precision=lax.Precision.HIGH,
             preferred_element_type=jnp.float32,
         ).reshape(lax.axis_size("pairs"), -1, piece.shape[1])
 
     got = swap(product(1 - member))
     parts = lax.all_to_all(product(member) + got, "pairs", 0, 0, tiled=True)
     mine = lax.all_to_all(sum_copies(parts), "pairs", 0, 0, tiled=True)
-    moments = join(mine.reshape(rows, -1), swap(mine).reshape(rows, -1))
+    other = swap(mine).reshape(rows, -1)
+    conduct, pot, held = store(conduct, pot, mine.reshape(rows, -1))
+    moments = store_other(other, held)
     return (conduct[None], pot[None], moments)
 
 

time: 82.7 us -> 81 us (0.979)
  local copies, waits for them, and re-layouts: 1.33 us -> 0.02 us
    unnamed x2 -> x0, local copies, waits for them, and re-layouts: 1.31 us -> none
    pallas_call x1 -> x2, Pallas kernels: 0.98 us -> 1.7 us  [the longest x1 0.9 us: store(): pl.pallas_call(store_kernel, out_shape=(jax.ShapeDtypeStruct(conduct.shap...]
  transfers between devices with their start and end apart: 8 -> 8, of which waited for: 7 -> 7; matrix products, arithmetic and copies ran while one was open for 2% -> 1% of each run, Pallas kernels for 0% -> 1%
where the time goes in v5:
time: 81 us; the launch traced here: 80.6 us
  blocking collectives  49.7 us (61%)
  starting transfers between devices  13 us (16%)
  waiting for transfers between devices  10.7 us (13%)
  Pallas kernels  4.89 us (6%)
  between operations  1.41 us (2%)
  matrix products  0.85 us (1%)
    all_gather x1, blocking collectives, local(): piece = lax.all_gather(traces, 'tile', axis=0, tiled=True)  16.1 us
    all_to_all x1, blocking collectives, local(): parts = lax.all_to_all(product(member) + got, 'pairs', 0, 0, tiled=True)  12.6 us
    all_to_all x1, blocking collectives, local(): pieces = lax.all_to_all(pieces, 'pairs', 0, 0, tiled=True)  11.2 us
    all_to_all x1, blocking collectives, local(): mine = lax.all_to_all(sum_copies(parts), 'pairs', 0, 0, tiled=True)  9.8 us
    ppermute x2, starting transfers between devices, exchange_halo(): low = lax.ppermute(high_edge, 'tile', forward)  6.98 us
    ppermute x2, waiting for transfers between devices, exchange_halo(): high = lax.ppermute(low_edge, 'tile', backward)  4.62 us
    ppermute x3, waiting for transfers between devices, swap(): return lax.ppermute(block, 'member', [(0, 1), (1, 0)])  4.01 us
    all_to_all x1, starting transfers between devices, local(): lax.all_to_all(chosen, 'pairs', 0, 0, tiled=True).reshape(2, width, ny, nz)  3.41 us
  transfers between devices with their start and end apart: 8, of which 7 were waited for; matrix products, arithmetic and copies ran while one was open for 1% of the time, Pallas kernels for 1%

profile of v5, /device:TPU:0, one launch (start us, length us, event | category | flops | bytes accessed | tf_op | source)
XLA Modules:
  0.0 80.6 jit_solution(12726868774286243572)
XLA Ops:
  1.3 1.3 %pack.1 = (f32[1]{0:T(128)S(4)}, s32[8]{0:T(128)S(4)}, s32[2]{0:T(128)S(4)}, f32[4,136,128]{2,1,0:T(8,128)S(1)}, f32[2,8,32,128]{3,2,1,0:T(8,128)S(1)}, /*index=...) custom-call(f32[1]{0:T(128)S(6)} %copy.12.weight_ref, s32[8]{0:T(128)} %parents_ref.1, ...), custom_call_target="tpu_custom_call" | custom-call | tf_op jit(solution)/shard_map/pack/pallas_call | solution.py:62
  2.6 11.2 %all_to_all.20.mine_ref = f32[4,136,128]{2,1,0:T(8,128)S(1)} all-to-all(f32[4,136,128]{2,1,0:T(8,128)S(1)} %get-tuple-element.22), channel_id=1, replica_groups=mesh['pairs'=4,'member'=2,'tile'=4] {'pairs'}, dimensions={0} | all-to-all | bytes 557056 | tf_op jit(solution)/shard_map/all_to_all | solution.py:303
  13.7 1.6 %collective-permute-done.other_ref = f32[4,136,128]{2,1,0:T(8,128)S(1)} collective-permute-done((f32[4,136,128]{2,1,0:T(8,128)S(1)}, f32[4,136,128]{2,1,0:T(8,128)S(1)}, u32[]{:S(2)}, u32[]{:S(2)}) %collective-permute-start) | collective-permute-done | bytes 278560 | tf_op jit(solution)/shard_map/ppermute | solution.py:290
  15.3 0.7 choose.1
  16.0 3.4 %all-to-all-start.1 = ((f32[4,128,128]{2,1,0:T(8,128)}), f32[4,128,128]{2,1,0:T(8,128)S(1)}, u32[]{:S(2)}, u32[]{:S(2)}) async-start(f32[4,128,128]{2,1,0:T(8,128)} %get-tuple-element.24), calls=%async_computation.1 | async-start | bytes 524288 | tf_op jit(solution)/shard_map/all_to_all | solution.py:306
  19.4 3.5 %collective-permute-start.3 = (f32[9,32,128]{2,1,0:T(8,128)S(1)}, f32[9,32,128]{2,1,0:T(8,128)S(1)}, u32[]{:S(2)}, u32[]{:S(2)}) collective-permute-start(f32[9,32,128]{2,1,0:T(8,128)S(1)} %get-tuple-element.27), channel_id=1, source_target_pairs={{0,1},{1,2},{2,3},{4,5},{5,6},{6,7},{8,9},{9,10},{10,11},{12,13},{... | collective-permute-start | bytes 442376 | tf_op jit(solution)/shard_map/ppermute | solution.py:284
  22.9 1.3 %collective-permute-start.4 = (f32[9,32,128]{2,1,0:T(8,128)S(1)}, f32[9,32,128]{2,1,0:T(8,128)S(1)}, u32[]{:S(2)}, u32[]{:S(2)}) collective-permute-start(f32[9,32,128]{2,1,0:T(8,128)S(1)} %get-tuple-element.28), channel_id=1, source_target_pairs={{1,0},{2,1},{3,2},{5,4},{6,5},{7,6},{9,8},{10,9},{11,10},{13,12},{... | collective-permute-start | bytes 442376 | tf_op jit(solution)/shard_map/ppermute | solution.py:285
  24.2 1.1 %all-to-all-done.1 = f32[4,128,128]{2,1,0:T(8,128)S(1)} async-done(((f32[4,128,128]{2,1,0:T(8,128)}), f32[4,128,128]{2,1,0:T(8,128)S(1)}, u32[]{:S(2)}, u32[]{:S(2)}) %all-to-all-start.1) | async-done | bytes 262176 | tf_op jit(solution)/shard_map/all_to_all | solution.py:306
  25.4 3.5 %collective-permute-start.1 = (f32[8,32,128]{2,1,0:T(8,128)S(1)}, f32[8,32,128]{2,1,0:T(8,128)S(1)}, u32[]{:S(2)}, u32[]{:S(2)}) collective-permute-start(f32[8,32,128]{2,1,0:T(8,128)S(1)} %bitcast.25), channel_id=1, source_target_pairs={{0,1},{1,2},{2,3},{4,5},{5,6},{6,7},{8,9},{9,10},{10,11},{12,13},{... | collective-permute-start | bytes 393224 | tf_op jit(solution)/shard_map/ppermute | solution.py:284
  28.9 1.3 %collective-permute-start.2 = (f32[8,32,128]{2,1,0:T(8,128)S(1)}, f32[8,32,128]{2,1,0:T(8,128)S(1)}, u32[]{:S(2)}, u32[]{:S(2)}) collective-permute-start(f32[8,32,128]{2,1,0:T(8,128)S(1)} %bitcast.24), channel_id=1, source_target_pairs={{1,0},{2,1},{3,2},{5,4},{6,5},{7,6},{9,8},{10,9},{11,10},{13,12},{... | collective-permute-start | bytes 393224 | tf_op jit(solution)/shard_map/ppermute | solution.py:285
  30.2 0.3 collective-permute-done.4.fixed_high
  30.4 0.9 %collective-permute-done.1.moved_low = f32[8,32,128]{2,1,0:T(8,128)S(1)} collective-permute-done((f32[8,32,128]{2,1,0:T(8,128)S(1)}, f32[8,32,128]{2,1,0:T(8,128)S(1)}, u32[]{:S(2)}, u32[]{:S(2)}) %collective-permute-start.1) | collective-permute-done | bytes 131104 | tf_op jit(solution)/shard_map/ppermute | solution.py:284
  31.4 4.4 %collective-permute-done.2.moved_high = f32[8,32,128]{2,1,0:T(8,128)S(1)} collective-permute-done((f32[8,32,128]{2,1,0:T(8,128)S(1)}, f32[8,32,128]{2,1,0:T(8,128)S(1)}, u32[]{:S(2)}, u32[]{:S(2)}) %collective-permute-start.2) | collective-permute-done | bytes 131104 | tf_op jit(solution)/shard_map/ppermute | solution.py:285
  35.7 1.1 %moves.1 = (f32[8,32,128]{2,1,0:T(8,128)S(1)}, f32[8,32,128]{2,1,0:T(8,128)S(1)}, f32[32,1024]{1,0:T(8,128)S(1)}) custom-call(s32[2]{0:T(128)S(4)} %get-tuple-element.19.accept_ref, f32[8,128]{1,0:T(8,128)S(1)} %get-tuple-element.23.root_ref, f32[2,8,32,128]{3,2,1,0:T(8,128)S(1)} %bitcast.16, f32[2,8,32,128]{3,2,1,0:T(8,128)S(1)} %get-tuple-element.25.noise_ref, ...), custom_call_target="tpu_custom_call" | custom-call | tf_op jit(solution)/shard_map/moves/pallas_call | solution.py:198
  36.9 16.1 %all_gather.3 = f32[128,1024]{1,0:T(8,128)S(1)} all-gather(f32[32,1024]{1,0:T(8,128)S(1)} %get-tuple-element.31), channel_id=1, replica_groups=mesh['pairs'=4,'member'=2,'tile'=4] {'tile'}, dimensions={0}, use_global_device_ids=true | all-gather | bytes 655360 | tf_op jit(solution)/shard_map/all_gather | solution.py:316
  53.0 0.4 fusion
  53.4 0.1 collective-permute-start.5
  53.5 0.4 fusion.2
  53.9 1.5 %collective-permute-done.5 = f32[4,32,1024]{2,1,0:T(8,128)S(1)} collective-permute-done((f32[4,32,1024]{2,1,0:T(8,128)S(1)}, f32[4,32,1024]{2,1,0:T(8,128)S(1)}, u32[]{:S(2)}, u32[]{:S(2)}) %collective-permute-start.5) | collective-permute-done | bytes 524320 | tf_op jit(solution)/shard_map/ppermute | solution.py:290
  55.5 12.6 %all_to_all.21.parts_ref = f32[4,32,1024]{2,1,0:T(8,128)S(1)} all-to-all(f32[4,32,1024]{2,1,0:T(8,128)S(1)} %add.19), channel_id=1, replica_groups=mesh['pairs'=4,'member'=2,'tile'=4] {'pairs'}, dimensions={0} | all-to-all | bytes 1048576 | tf_op jit(solution)/shard_map/all_to_all | solution.py:331
  68.1 9.8 %all_to_all.22 = f32[4,32,1024]{2,1,0:T(8,128)S(1)} all-to-all(f32[4,32,1024]{2,1,0:T(8,128)S(1)} %sum_copies.1), channel_id=1, replica_groups=mesh['pairs'=4,'member'=2,'tile'=4] {'pairs'}, dimensions={0} | all-to-all | bytes 1048576 | tf_op jit(solution)/shard_map/all_to_all | solution.py:332
  77.9 0.9 %store.1 = (f32[8,32,128]{2,1,0:T(8,128)}, f32[8,32,128]{2,1,0:T(8,128)}, f32[256,1024]{1,0:T(8,128)}) custom-call(f32[8,32,128]{2,1,0:T(8,128)S(1)} %get-tuple-element.29.cond_ref, f32[8,32,128]{2,1,0:T(8,128)S(1)} %get-tuple-element.30.pot_ref, f32[128,1024]{1,0:T(8,128)S(1)} %bitcast.17), custom_call_target="tpu_custom_call" | custom-call | tf_op jit(solution)/shard_map/store/pallas_call | solution.py:247
  78.8 1.0 %collective-permute-done.6 = f32[4,32,1024]{2,1,0:T(8,128)S(1)} collective-permute-done((f32[4,32,1024]{2,1,0:T(8,128)S(1)}, f32[4,32,1024]{2,1,0:T(8,128)S(1)}, u32[]{:S(2)}, u32[]{:S(2)}) %collective-permute-start.6) | collective-permute-done | bytes 524320 | tf_op jit(solution)/shard_map/ppermute | solution.py:290
  79.8 0.8 store_other.1
  (6 shorter events, 0.1 us)
Async XLA Ops:
  13.7 1.6 %collective-permute-start = (f32[4,136,128]{2,1,0:T(8,128)S(1)}, f32[4,136,128]{2,1,0:T(8,128)S(1)}, u32[]{:S(2)}, u32[]{:S(2)}) collective-permute-start(f32[4,136,128]{2,1,0:T(8,128)S(1)} %all_to_all.20.mine_ref), channel_id=1, source_target_pairs={{0,4},{4,0},{1,5},{5,1},{2,6},{6,2},{3,7},{7,3},{8,12},{12,8},{9,1... | collective-permute-start | bytes 835592 | tf_op jit(solution)/shard_map/ppermute | solution.py:290
  16.0 9.3 %all-to-all-start.1 = ((f32[4,128,128]{2,1,0:T(8,128)}), f32[4,128,128]{2,1,0:T(8,128)S(1)}, u32[]{:S(2)}, u32[]{:S(2)}) async-start(f32[4,128,128]{2,1,0:T(8,128)} %get-tuple-element.24), calls=%async_computation.1 | async-start | bytes 524288 | tf_op jit(solution)/shard_map/all_to_all | solution.py:306
  19.4 10.7 %collective-permute-start.3 = (f32[9,32,128]{2,1,0:T(8,128)S(1)}, f32[9,32,128]{2,1,0:T(8,128)S(1)}, u32[]{:S(2)}, u32[]{:S(2)}) collective-permute-start(f32[9,32,128]{2,1,0:T(8,128)S(1)} %get-tuple-element.27), channel_id=1, source_target_pairs={{0,1},{1,2},{2,3},{4,5},{5,6},{6,7},{8,9},{9,10},{10,11},{12,13},{... | collective-permute-start | bytes 442376 | tf_op jit(solution)/shard_map/ppermute | solution.py:284
  22.9 7.5 %collective-permute-start.4 = (f32[9,32,128]{2,1,0:T(8,128)S(1)}, f32[9,32,128]{2,1,0:T(8,128)S(1)}, u32[]{:S(2)}, u32[]{:S(2)}) collective-permute-start(f32[9,32,128]{2,1,0:T(8,128)S(1)} %get-tuple-element.28), channel_id=1, source_target_pairs={{1,0},{2,1},{3,2},{5,4},{6,5},{7,6},{9,8},{10,9},{11,10},{13,12},{... | collective-permute-start | bytes 442376 | tf_op jit(solution)/shard_map/ppermute | solution.py:285
  25.4 6.0 %collective-permute-start.1 = (f32[8,32,128]{2,1,0:T(8,128)S(1)}, f32[8,32,128]{2,1,0:T(8,128)S(1)}, u32[]{:S(2)}, u32[]{:S(2)}) collective-permute-start(f32[8,32,128]{2,1,0:T(8,128)S(1)} %bitcast.25), channel_id=1, source_target_pairs={{0,1},{1,2},{2,3},{4,5},{5,6},{6,7},{8,9},{9,10},{10,11},{12,13},{... | collective-permute-start | bytes 393224 | tf_op jit(solution)/shard_map/ppermute | solution.py:284
  28.9 6.9 %collective-permute-start.2 = (f32[8,32,128]{2,1,0:T(8,128)S(1)}, f32[8,32,128]{2,1,0:T(8,128)S(1)}, u32[]{:S(2)}, u32[]{:S(2)}) collective-permute-start(f32[8,32,128]{2,1,0:T(8,128)S(1)} %bitcast.24), channel_id=1, source_target_pairs={{1,0},{2,1},{3,2},{5,4},{6,5},{7,6},{9,8},{10,9},{11,10},{13,12},{... | collective-permute-start | bytes 393224 | tf_op jit(solution)/shard_map/ppermute | solution.py:285
  53.4 2.0 %collective-permute-start.5 = (f32[4,32,1024]{2,1,0:T(8,128)S(1)}, f32[4,32,1024]{2,1,0:T(8,128)S(1)}, u32[]{:S(2)}, u32[]{:S(2)}) collective-permute-start(f32[4,32,1024]{2,1,0:T(8,128)S(1)} %bitcast.20), channel_id=1, source_target_pairs={{0,4},{4,0},{1,5},{5,1},{2,6},{6,2},{3,7},{7,3},{8,12},{12,8},{9,1... | collective-permute-start | bytes 1572872 | tf_op jit(solution)/shard_map/ppermute | solution.py:290
  77.9 1.9 %collective-permute-start.6 = (f32[4,32,1024]{2,1,0:T(8,128)S(1)}, f32[4,32,1024]{2,1,0:T(8,128)S(1)}, u32[]{:S(2)}, u32[]{:S(2)}) collective-permute-start(f32[4,32,1024]{2,1,0:T(8,128)S(1)} %all_to_all.22), channel_id=1, source_target_pairs={{0,4},{4,0},{1,5},{5,1},{2,6},{6,2},{3,7},{7,3},{8,12},{12,8},{9,1... | collective-permute-start | bytes 1572872 | tf_op jit(solution)/shard_map/ppermute | solution.py:290

commit v6 on v5

--- a/solution.py
+++ b/solution.py
@@ -121,7 +121,7 @@
 
 def moves_kernel(
     depth, accept_ref, root_ref, moved_ref, noise_ref, source_ref,
-    moved_low, moved_high, fixed_low, fixed_high,
+    moved_first, moved_second, fixed_first, fixed_second,
     cond_out, pot_out, traces_out, cond, pot, once, conductivity, gain,
 ):
     moves, width, _, nz = noise_ref.shape
@@ -131,20 +131,21 @@
     first = tile == 0
     last = tile == lax.axis_size("tile") - 1
 
-    def fetch(field, low, high, at, h, i):
-        if i < 0:
-            return low[at + h + i]
-        if i >= width:
-            return high[at + i - width]
-        return field[i]
+    even = lax.axis_index("member") == 0
+
+    def fetch(field, first, second, at, h, i):
+        if 0 <= i < width:
+            return field[i]
+        place = at + h + i if i < 0 else at + i - width
+        return jnp.where(even == (i < 0), first[place], second[place])
 
     def keep_inside(value, i):
         outside = (first & (i < reach)) | (last & (i >= reach + width))
         return jnp.where(outside, 0.0, value)
 
     for i in range(span):
-        cond[i] = fetch(moved_ref.at[0], moved_low, moved_high, 0, reach, i - reach)
-        pot[i] = fetch(moved_ref.at[1], moved_low, moved_high, reach, reach, i - reach)
+        cond[i] = fetch(moved_ref.at[0], moved_first, moved_second, 0, reach, i - reach)
+        pot[i] = fetch(moved_ref.at[1], moved_first, moved_second, reach, reach, i - reach)
 
     source_at = sum(depth[:moves])
     for m in range(moves):
@@ -161,7 +162,7 @@
                     before * conductivity[i - 1], here * here_k, after * conductivity[i + 1], 0.0
                 )
                 source = fetch(
-                    source_ref, fixed_low, fixed_high, source_at, depth[moves], i - reach
+                    source_ref, fixed_first, fixed_second, source_at, depth[moves], i - reach
                 )
                 value = (1.0 - relax_weight) * here + (
                     2.0 * source + (here_k * plain + scaled)
@@ -170,7 +171,7 @@
 
         for i in range(start, span - start):
             proposal = prior_keep * cond[i] + prior_fresh * fetch(
-                noise_ref.at[m], fixed_low, fixed_high, noise_at, depth[m], i - reach
+                noise_ref.at[m], fixed_first, fixed_second, noise_at, depth[m], i - reach
             )
             conductivity[i] = jnp.exp(proposal)
             cond[i] = jnp.where(accepted, proposal, cond[i])
@@ -189,7 +190,7 @@
         cond_out[i] = cond[i + reach]
         value = pot[i + reach]
         pot_out[i] = value
-        traces_out[:, i * nz:(i + 1) * nz] = value * root
+        traces_out[0, :, i * nz:(i + 1) * nz] = value * root
 
 
 def run_moves(depth, accept, root, *fields):
@@ -200,7 +201,7 @@
         out_shape=(
             pltpu.VMEM((width, ny, nz), jnp.float32),
             pltpu.VMEM((width, ny, nz), jnp.float32),
-            pltpu.VMEM((ny, width * nz), jnp.float32),
+            pltpu.VMEM((1, ny, width * nz), jnp.float32),
         ),
         in_specs=[SMEM] + [VMEM] * (1 + len(fields)),
         out_specs=(VMEM, VMEM, VMEM),
@@ -279,11 +280,20 @@
 
 def exchange_halo(low_edge, high_edge):
     count = lax.axis_size("tile")
-    forward = [(i, i + 1) for i in range(count - 1)]
-    backward = [(target, source) for source, target in forward]
-    low = lax.ppermute(high_edge, "tile", forward)
-    high = lax.ppermute(low_edge, "tile", backward)
-    return low, high
+    up = [(i, i + 1) for i in range(count - 1)]
+    down = [(target, source) for source, target in up]
+
+    def turn(member_0, member_1):
+        return member_0 + [(count + source, count + target) for source, target in member_1]
+
+    even = lax.axis_index("member") == 0
+    first = lax.ppermute(
+        jnp.where(even, high_edge, low_edge), ("member", "tile"), turn(up, down)
+    )
+    second = lax.ppermute(
+        jnp.where(even, low_edge, high_edge), ("member", "tile"), turn(down, up)
+    )
+    return first, second
 
 
 def swap(block):
@@ -301,19 +311,19 @@
         lax.axis_size("pairs"), depth,
     )
     pieces = lax.all_to_all(pieces, "pairs", 0, 0, tiled=True)
-    fixed_low, fixed_high = exchange_halo(low_edge, high_edge)
+    fixed_first, fixed_second = exchange_halo(low_edge, high_edge)
     chosen, root = choose(parents, weights, pieces, swap(pieces))
     moved = lax.all_to_all(chosen, "pairs", 0, 0, tiled=True).reshape(2, width, ny, nz)
-    moved_low, moved_high = exchange_halo(
+    moved_first, moved_second = exchange_halo(
         moved[:, :reach].reshape(-1, ny, nz), moved[:, width - reach:].reshape(-1, ny, nz)
     )
     conduct, pot, traces = run_moves(
-        depth, accept, root, moved, noise, source, moved_low, moved_high, fixed_low, fixed_high
-    )
-
-    rows = traces.shape[1] // (lax.axis_size("tile") * pair)
+        depth, accept, root, moved, noise, source, moved_first, moved_second, fixed_first, fixed_second
+    )
+
+    rows = traces.shape[2] // (lax.axis_size("tile") * pair)
     member = lax.axis_index("member")
-    piece = lax.all_gather(traces, "tile", axis=0, tiled=True)
+    piece = lax.all_gather(traces, "tile", axis=0, tiled=True).reshape(-1, traces.shape[2])
 
     def product(owner):
         columns = lax.dynamic_slice_in_dim(

time: 81 us -> 81.5 us (level)
  starting transfers between devices: 13 us -> 14.1 us
    all_to_all x1, waiting for transfers between devices: 1.11 us -> 0.01 us  [local(): lax.all_to_all(chosen, 'pairs', 0, 0, tiled=True).reshape(2, width, ny, nz)]
    ppermute x4, starting transfers between devices: 9.56 us -> 10.6 us  [the longest x2 8.04 us: exchange_halo(): lax.ppermute(jnp.where(even, high_edge, low_edge), ('member', 'tile'), tu...]
  transfers between devices with their start and end apart: 8 -> 8, of which waited for: 7 -> 5; matrix products, arithmetic and copies ran while one was open for 1% -> 0% of each run, Pallas kernels for 1% -> 1%
where the time goes in v6:
time: 81.5 us; the launch traced here: 81.1 us
  blocking collectives  49.7 us (61%)
  starting transfers between devices  14.1 us (17%)
  waiting for transfers between devices  9.9 us (12%)
  Pallas kernels  4.9 us (6%)
  between operations  1.43 us (2%)
    all_gather x1, blocking collectives, local(): lax.all_gather(traces, 'tile', axis=0, tiled=True)  16.1 us
    all_to_all x1, blocking collectives, local(): parts = lax.all_to_all(product(member) + got, 'pairs', 0, 0, tiled=True)  12.7 us
    all_to_all x1, blocking collectives, local(): pieces = lax.all_to_all(pieces, 'pairs', 0, 0, tiled=True)  11.2 us
    all_to_all x1, blocking collectives, local(): mine = lax.all_to_all(sum_copies(parts), 'pairs', 0, 0, tiled=True)  9.8 us
    ppermute x2, starting transfers between devices, exchange_halo(): lax.ppermute(jnp.where(even, high_edge, low_edge), ('member', 'tile'), tu...  8.04 us
    ppermute x3, waiting for transfers between devices, swap(): return lax.ppermute(block, 'member', [(0, 1), (1, 0)])  4.35 us
    ppermute x2, waiting for transfers between devices, exchange_halo(): lax.ppermute(jnp.where(even, low_edge, high_edge), ('member', 'tile'), tu...  3.47 us
    all_to_all x1, starting transfers between devices, local(): lax.all_to_all(chosen, 'pairs', 0, 0, tiled=True).reshape(2, width, ny, nz)  3.41 us
  transfers between devices with their start and end apart: 8, of which 5 were waited for; matrix products, arithmetic and copies ran while one was open for 0% of the time, Pallas kernels for 1%

profile of v6, /device:TPU:0, one launch (start us, length us, event | category | flops | bytes accessed | tf_op | source)
XLA Modules:
  0.0 81.1 jit_solution(6345023858934229696)
XLA Ops:
  1.3 1.3 %pack.1 = (f32[1]{0:T(128)S(4)}, s32[8]{0:T(128)S(4)}, s32[2]{0:T(128)S(4)}, f32[4,136,128]{2,1,0:T(8,128)S(1)}, f32[2,8,32,128]{3,2,1,0:T(8,128)S(1)}, /*index=...) custom-call(f32[1]{0:T(128)S(6)} %copy.18.weight_ref, s32[8]{0:T(128)} %parents_ref.1, ...), custom_call_target="tpu_custom_call" | custom-call | tf_op jit(solution)/shard_map/pack/pallas_call | solution.py:62
  2.6 11.2 %all_to_all.20.mine_ref = f32[4,136,128]{2,1,0:T(8,128)S(1)} all-to-all(f32[4,136,128]{2,1,0:T(8,128)S(1)} %get-tuple-element.22), channel_id=1, replica_groups=mesh['pairs'=4,'member'=2,'tile'=4] {'pairs'}, dimensions={0} | all-to-all | bytes 557056 | tf_op jit(solution)/shard_map/all_to_all | solution.py:313
  13.7 1.6 %collective-permute-done.other_ref = f32[4,136,128]{2,1,0:T(8,128)S(1)} collective-permute-done((f32[4,136,128]{2,1,0:T(8,128)S(1)}, f32[4,136,128]{2,1,0:T(8,128)S(1)}, u32[]{:S(2)}, u32[]{:S(2)}) %collective-permute-start) | collective-permute-done | bytes 278560 | tf_op jit(solution)/shard_map/ppermute | solution.py:300
  15.3 0.7 choose.1
  16.0 3.4 %all-to-all-start.1 = ((f32[4,128,128]{2,1,0:T(8,128)}), f32[4,128,128]{2,1,0:T(8,128)S(1)}, u32[]{:S(2)}, u32[]{:S(2)}) async-start(f32[4,128,128]{2,1,0:T(8,128)} %get-tuple-element.24), calls=%async_computation.1 | async-start | bytes 524288 | tf_op jit(solution)/shard_map/all_to_all | solution.py:316
  19.5 1.3 %collective-permute-start.4 = (f32[9,32,128]{2,1,0:T(8,128)S(1)}, f32[9,32,128]{2,1,0:T(8,128)S(1)}, u32[]{:S(2)}, u32[]{:S(2)}) collective-permute-start(f32[9,32,128]{2,1,0:T(8,128)S(1)} %get-tuple-element.37), channel_id=1, source_target_pairs={{1,0},{2,1},{3,2},{4,5},{5,6},{6,7},{9,8},{10,9},{11,10},{12,13},{... | collective-permute-start | bytes 442376 | tf_op jit(solution)/shard_map/ppermute | solution.py:293
  20.8 4.6 %collective-permute-start.3 = (f32[9,32,128]{2,1,0:T(8,128)S(1)}, f32[9,32,128]{2,1,0:T(8,128)S(1)}, u32[]{:S(2)}, u32[]{:S(2)}) collective-permute-start(f32[9,32,128]{2,1,0:T(8,128)S(1)} %get-tuple-element.38), channel_id=1, source_target_pairs={{0,1},{1,2},{2,3},{5,4},{6,5},{7,6},{8,9},{9,10},{10,11},{13,12},{... | collective-permute-start | bytes 442376 | tf_op jit(solution)/shard_map/ppermute | solution.py:290
  25.4 3.5 %collective-permute-start.1 = (f32[8,32,128]{2,1,0:T(8,128)S(1)}, f32[8,32,128]{2,1,0:T(8,128)S(1)}, u32[]{:S(2)}, u32[]{:S(2)}) collective-permute-start(f32[8,32,128]{2,1,0:T(8,128)S(1)} %bitcast.35), channel_id=1, source_target_pairs={{0,1},{1,2},{2,3},{5,4},{6,5},{7,6},{8,9},{9,10},{10,11},{13,12},{... | collective-permute-start | bytes 393224 | tf_op jit(solution)/shard_map/ppermute | solution.py:290
  28.9 1.3 %collective-permute-start.2 = (f32[8,32,128]{2,1,0:T(8,128)S(1)}, f32[8,32,128]{2,1,0:T(8,128)S(1)}, u32[]{:S(2)}, u32[]{:S(2)}) collective-permute-start(f32[8,32,128]{2,1,0:T(8,128)S(1)} %bitcast.34), channel_id=1, source_target_pairs={{1,0},{2,1},{3,2},{4,5},{5,6},{6,7},{9,8},{10,9},{11,10},{12,13},{... | collective-permute-start | bytes 393224 | tf_op jit(solution)/shard_map/ppermute | solution.py:293
  30.2 2.1 %collective-permute-done.1.moved_first = f32[8,32,128]{2,1,0:T(8,128)S(1)} collective-permute-done((f32[8,32,128]{2,1,0:T(8,128)S(1)}, f32[8,32,128]{2,1,0:T(8,128)S(1)}, u32[]{:S(2)}, u32[]{:S(2)}) %collective-permute-start.1) | collective-permute-done | bytes 131104 | tf_op jit(solution)/shard_map/ppermute | solution.py:290
  32.3 3.5 %collective-permute-done.2.moved_second = f32[8,32,128]{2,1,0:T(8,128)S(1)} collective-permute-done((f32[8,32,128]{2,1,0:T(8,128)S(1)}, f32[8,32,128]{2,1,0:T(8,128)S(1)}, u32[]{:S(2)}, u32[]{:S(2)}) %collective-permute-start.2) | collective-permute-done | bytes 131104 | tf_op jit(solution)/shard_map/ppermute | solution.py:293
  35.7 1.1 %moves.1 = (f32[8,32,128]{2,1,0:T(8,128)S(1)}, f32[8,32,128]{2,1,0:T(8,128)S(1)}, f32[1,32,1024]{2,1,0:T(8,128)S(1)}) custom-call(s32[2]{0:T(128)S(4)} %get-tuple-element.19.accept_ref, f32[8,128]{1,0:T(8,128)S(1)} %get-tuple-element.23.root_ref, f32[2,8,32,128]{3,2,1,0:T(8,128)S(1)} %bitcast.25, f32[2,8,32,128]{3,2,1,0:T(8,128)S(1)} %get-tuple-element.25.noise_ref, ...), custom_call_target="tpu_custom_call" | custom-call | tf_op jit(solution)/shard_map/moves/pallas_call | solution.py:199
  36.9 16.1 %all_gather.3 = f32[4,32,1024]{2,1,0:T(8,128)S(1)} all-gather(f32[1,32,1024]{2,1,0:T(8,128)S(1)} %get-tuple-element.31), channel_id=1, replica_groups=mesh['pairs'=4,'member'=2,'tile'=4] {'tile'}, dimensions={0}, use_global_device_ids=true | all-gather | bytes 655360 | tf_op jit(solution)/shard_map/all_gather | solution.py:326
  53.0 0.1 copy.16
  53.1 0.4 fusion
  53.5 0.1 collective-permute-start.5
  53.6 0.1 copy.15
  53.7 1.8 %collective-permute-done.5 = f32[4,32,1024]{2,1,0:T(8,128)S(1)} collective-permute-done((f32[4,32,1024]{2,1,0:T(8,128)S(1)}, f32[4,32,1024]{2,1,0:T(8,128)S(1)}, u32[]{:S(2)}, u32[]{:S(2)}) %collective-permute-start.5) | collective-permute-done | bytes 524320 | tf_op jit(solution)/shard_map/ppermute | solution.py:300
  55.5 0.4 convolution_add_fusion
  55.8 12.7 %all_to_all.21.parts_ref = f32[4,32,1024]{2,1,0:T(8,128)S(1)} all-to-all(f32[4,32,1024]{2,1,0:T(8,128)S(1)} %convolution_add_fusion), channel_id=1, replica_groups=mesh['pairs'=4,'member'=2,'tile'=4] {'pairs'}, dimensions={0} | all-to-all | bytes 1048576 | tf_op jit(solution)/shard_map/all_to_all | solution.py:341
  68.6 9.8 %all_to_all.22 = f32[4,32,1024]{2,1,0:T(8,128)S(1)} all-to-all(f32[4,32,1024]{2,1,0:T(8,128)S(1)} %sum_copies.1), channel_id=1, replica_groups=mesh['pairs'=4,'member'=2,'tile'=4] {'pairs'}, dimensions={0} | all-to-all | bytes 1048576 | tf_op jit(solution)/shard_map/all_to_all | solution.py:342
  78.4 0.9 %store.1 = (f32[8,32,128]{2,1,0:T(8,128)}, f32[8,32,128]{2,1,0:T(8,128)}, f32[256,1024]{1,0:T(8,128)}) custom-call(f32[8,32,128]{2,1,0:T(8,128)S(1)} %get-tuple-element.29.cond_ref, f32[8,32,128]{2,1,0:T(8,128)S(1)} %get-tuple-element.30.pot_ref, f32[128,1024]{1,0:T(8,128)S(1)} %bitcast.26), custom_call_target="tpu_custom_call" | custom-call | tf_op jit(solution)/shard_map/store/pallas_call | solution.py:248
  79.3 1.0 %collective-permute-done.6 = f32[4,32,1024]{2,1,0:T(8,128)S(1)} collective-permute-done((f32[4,32,1024]{2,1,0:T(8,128)S(1)}, f32[4,32,1024]{2,1,0:T(8,128)S(1)}, u32[]{:S(2)}, u32[]{:S(2)}) %collective-permute-start.6) | collective-permute-done | bytes 524320 | tf_op jit(solution)/shard_map/ppermute | solution.py:300
  80.3 0.8 store_other.1
  (9 shorter events, 0.1 us)
Async XLA Ops:
  13.7 1.6 %collective-permute-start = (f32[4,136,128]{2,1,0:T(8,128)S(1)}, f32[4,136,128]{2,1,0:T(8,128)S(1)}, u32[]{:S(2)}, u32[]{:S(2)}) collective-permute-start(f32[4,136,128]{2,1,0:T(8,128)S(1)} %all_to_all.20.mine_ref), channel_id=1, source_target_pairs={{0,4},{4,0},{1,5},{5,1},{2,6},{6,2},{3,7},{7,3},{8,12},{12,8},{9,1... | collective-permute-start | bytes 835592 | tf_op jit(solution)/shard_map/ppermute | solution.py:300
  16.0 9.3 %all-to-all-start.1 = ((f32[4,128,128]{2,1,0:T(8,128)}), f32[4,128,128]{2,1,0:T(8,128)S(1)}, u32[]{:S(2)}, u32[]{:S(2)}) async-start(f32[4,128,128]{2,1,0:T(8,128)} %get-tuple-element.24), calls=%async_computation.1 | async-start | bytes 524288 | tf_op jit(solution)/shard_map/all_to_all | solution.py:316
  19.5 10.7 %collective-permute-start.4 = (f32[9,32,128]{2,1,0:T(8,128)S(1)}, f32[9,32,128]{2,1,0:T(8,128)S(1)}, u32[]{:S(2)}, u32[]{:S(2)}) collective-permute-start(f32[9,32,128]{2,1,0:T(8,128)S(1)} %get-tuple-element.37), channel_id=1, source_target_pairs={{1,0},{2,1},{3,2},{4,5},{5,6},{6,7},{9,8},{10,9},{11,10},{12,13},{... | collective-permute-start | bytes 442376 | tf_op jit(solution)/shard_map/ppermute | solution.py:293
  20.8 9.4 %collective-permute-start.3 = (f32[9,32,128]{2,1,0:T(8,128)S(1)}, f32[9,32,128]{2,1,0:T(8,128)S(1)}, u32[]{:S(2)}, u32[]{:S(2)}) collective-permute-start(f32[9,32,128]{2,1,0:T(8,128)S(1)} %get-tuple-element.38), channel_id=1, source_target_pairs={{0,1},{1,2},{2,3},{5,4},{6,5},{7,6},{8,9},{9,10},{10,11},{13,12},{... | collective-permute-start | bytes 442376 | tf_op jit(solution)/shard_map/ppermute | solution.py:290
  25.4 6.9 %collective-permute-start.1 = (f32[8,32,128]{2,1,0:T(8,128)S(1)}, f32[8,32,128]{2,1,0:T(8,128)S(1)}, u32[]{:S(2)}, u32[]{:S(2)}) collective-permute-start(f32[8,32,128]{2,1,0:T(8,128)S(1)} %bitcast.35), channel_id=1, source_target_pairs={{0,1},{1,2},{2,3},{5,4},{6,5},{7,6},{8,9},{9,10},{10,11},{13,12},{... | collective-permute-start | bytes 393224 | tf_op jit(solution)/shard_map/ppermute | solution.py:290
  28.9 6.9 %collective-permute-start.2 = (f32[8,32,128]{2,1,0:T(8,128)S(1)}, f32[8,32,128]{2,1,0:T(8,128)S(1)}, u32[]{:S(2)}, u32[]{:S(2)}) collective-permute-start(f32[8,32,128]{2,1,0:T(8,128)S(1)} %bitcast.34), channel_id=1, source_target_pairs={{1,0},{2,1},{3,2},{4,5},{5,6},{6,7},{9,8},{10,9},{11,10},{12,13},{... | collective-permute-start | bytes 393224 | tf_op jit(solution)/shard_map/ppermute | solution.py:293
  53.5 2.0 %collective-permute-start.5 = (f32[4,32,1024]{2,1,0:T(8,128)S(1)}, f32[4,32,1024]{2,1,0:T(8,128)S(1)}, u32[]{:S(2)}, u32[]{:S(2)}) collective-permute-start(f32[4,32,1024]{2,1,0:T(8,128)S(1)} %fusion), channel_id=1, source_target_pairs={{0,4},{4,0},{1,5},{5,1},{2,6},{6,2},{3,7},{7,3},{8,12},{12,8},{9,1... | collective-permute-start | bytes 1572872 | tf_op jit(solution)/shard_map/ppermute | solution.py:300
  78.4 1.9 %collective-permute-start.6 = (f32[4,32,1024]{2,1,0:T(8,128)S(1)}, f32[4,32,1024]{2,1,0:T(8,128)S(1)}, u32[]{:S(2)}, u32[]{:S(2)}) collective-permute-start(f32[4,32,1024]{2,1,0:T(8,128)S(1)} %all_to_all.22), channel_id=1, source_target_pairs={{0,4},{4,0},{1,5},{5,1},{2,6},{6,2},{3,7},{7,3},{8,12},{12,8},{9,1... | collective-permute-start | bytes 1572872 | tf_op jit(solution)/shard_map/ppermute | solution.py:300

commit v7 on v5

--- a/solution.py
+++ b/solution.py
@@ -121,7 +121,7 @@
 
 def moves_kernel(
     depth, accept_ref, root_ref, moved_ref, noise_ref, source_ref,
-    moved_low, moved_high, fixed_low, fixed_high,
+    moved_low, moved_high, fixed_own, fixed_other,
     cond_out, pot_out, traces_out, cond, pot, once, conductivity, gain,
 ):
     moves, width, _, nz = noise_ref.shape
@@ -131,20 +131,28 @@
     first = tile == 0
     last = tile == lax.axis_size("tile") - 1
 
-    def fetch(field, low, high, at, h, i):
+    even = lax.axis_index("member") == 0
+
+    def fetch_moved(field, at, i):
         if i < 0:
-            return low[at + h + i]
+            return moved_low[at + reach + i]
         if i >= width:
-            return high[at + i - width]
-        return field[i]
+            return moved_high[at + i - width]
+        return moved_ref[field, i]
+
+    def fetch(field, at, h, i):
+        if 0 <= i < width:
+            return field[i]
+        place = at + h + i if i < 0 else at + i - width
+        return jnp.where(even == (i < 0), fixed_own[place], fixed_other[place])
 
     def keep_inside(value, i):
         outside = (first & (i < reach)) | (last & (i >= reach + width))
         return jnp.where(outside, 0.0, value)
 
     for i in range(span):
-        cond[i] = fetch(moved_ref.at[0], moved_low, moved_high, 0, reach, i - reach)
-        pot[i] = fetch(moved_ref.at[1], moved_low, moved_high, reach, reach, i - reach)
+        cond[i] = fetch_moved(0, 0, i - reach)
+        pot[i] = fetch_moved(1, reach, i - reach)
 
     source_at = sum(depth[:moves])
     for m in range(moves):
@@ -161,7 +169,7 @@
                     before * conductivity[i - 1], here * here_k, after * conductivity[i + 1], 0.0
                 )
                 source = fetch(
-                    source_ref, fixed_low, fixed_high, source_at, depth[moves], i - reach
+                    source_ref, source_at, depth[moves], i - reach
                 )
                 value = (1.0 - relax_weight) * here + (
                     2.0 * source + (here_k * plain + scaled)
@@ -170,7 +178,7 @@
 
         for i in range(start, span - start):
             proposal = prior_keep * cond[i] + prior_fresh * fetch(
-                noise_ref.at[m], fixed_low, fixed_high, noise_at, depth[m], i - reach
+                noise_ref.at[m], noise_at, depth[m], i - reach
             )
             conductivity[i] = jnp.exp(proposal)
             cond[i] = jnp.where(accepted, proposal, cond[i])
@@ -290,6 +298,17 @@
     return lax.ppermute(block, "member", [(0, 1), (1, 0)])
 
 
+def exchange_by_member(low_edge, high_edge):
+    count = lax.axis_size("tile")
+    up = [(i, i + 1) for i in range(count - 1)]
+    down = [(count + target, count + source) for source, target in up]
+    even = lax.axis_index("member") == 0
+    got = swap(jnp.where(even, low_edge, high_edge))
+    lane = jnp.concatenate([jnp.where(even, high_edge, low_edge), got])
+    came = lax.ppermute(lane, ("member", "tile"), up + down)
+    return came[:low_edge.shape[0]], swap(came[low_edge.shape[0]:])
+
+
 def local(log_cond, potential, noise, source, parents, accept, weights):
     moves = noise.shape[0]
     width, ny, nz = source.shape
@@ -301,14 +320,14 @@
         lax.axis_size("pairs"), depth,
     )
     pieces = lax.all_to_all(pieces, "pairs", 0, 0, tiled=True)
-    fixed_low, fixed_high = exchange_halo(low_edge, high_edge)
+    fixed_own, fixed_other = exchange_by_member(low_edge, high_edge)
     chosen, root = choose(parents, weights, pieces, swap(pieces))
     moved = lax.all_to_all(chosen, "pairs", 0, 0, tiled=True).reshape(2, width, ny, nz)
     moved_low, moved_high = exchange_halo(
         moved[:, :reach].reshape(-1, ny, nz), moved[:, width - reach:].reshape(-1, ny, nz)
     )
     conduct, pot, traces = run_moves(
-        depth, accept, root, moved, noise, source, moved_low, moved_high, fixed_low, fixed_high
+        depth, accept, root, moved, noise, source, moved_low, moved_high, fixed_own, fixed_other
     )
 
     rows = traces.shape[1] // (lax.axis_size("tile") * pair)

time: 81 us -> 80.9 us (level)
  blocking collectives: 49.7 us -> 37.4 us
  waiting for transfers between devices: 10.7 us -> 17.8 us
  starting transfers between devices: 13 us -> 17.2 us
    all_to_all x1 -> x0, blocking collectives: 11.2 us -> none  [local(): pieces = lax.all_to_all(pieces, 'pairs', 0, 0, tiled=True)]
    all_to_all x0 -> x1, starting transfers between devices: none -> 4.74 us  [local(): pieces = lax.all_to_all(pieces, 'pairs', 0, 0, tiled=True)]
    all_to_all x1, waiting for transfers between devices: 1.11 us -> 5.67 us  [local(): lax.all_to_all(chosen, 'pairs', 0, 0, tiled=True).reshape(2, width, ny, nz)]
    ppermute x0 -> x1, starting transfers between devices: none -> 3.5 us  [exchange_by_member(): came = lax.ppermute(lane, ('member', 'tile'), up + down)]
    ppermute x2 -> x1, starting transfers between devices: 6.98 us -> 3.49 us  [exchange_halo(): low = lax.ppermute(high_edge, 'tile', forward)]
    all_to_all x0 -> x1, waiting for transfers between devices: none -> 2.59 us  [local(): pieces = lax.all_to_all(pieces, 'pairs', 0, 0, tiled=True)]
    ppermute x2 -> x1, starting transfers between devices: 2.58 us -> 1.29 us  [exchange_halo(): high = lax.ppermute(low_edge, 'tile', backward)]
    all_to_all x1, blocking collectives: 12.6 us -> 11.5 us  [local(): parts = lax.all_to_all(product(member) + got, 'pairs', 0, 0, tiled=True)]
  transfers between devices with their start and end apart: 8 -> 10, of which waited for: 7 -> 7; matrix products, arithmetic and copies ran while one was open for 1% -> 1% of each run, Pallas kernels for 1% -> 2%
where the time goes in v7:
time: 80.9 us; the launch traced here: 80.5 us
  blocking collectives  37.4 us (46%)
  waiting for transfers between devices  17.8 us (22%)
  starting transfers between devices  17.2 us (21%)
  Pallas kernels  5.6 us (7%)
  between operations  1.44 us (2%)
  matrix products  0.85 us (1%)
    all_gather x1, blocking collectives, local(): piece = lax.all_gather(traces, 'tile', axis=0, tiled=True)  15.8 us
    all_to_all x1, blocking collectives, local(): parts = lax.all_to_all(product(member) + got, 'pairs', 0, 0, tiled=True)  11.5 us
    all_to_all x1, blocking collectives, local(): mine = lax.all_to_all(sum_copies(parts), 'pairs', 0, 0, tiled=True)  10.1 us
    all_to_all x1, waiting for transfers between devices, local(): lax.all_to_all(chosen, 'pairs', 0, 0, tiled=True).reshape(2, width, ny, nz)  5.67 us
    all_to_all x1, starting transfers between devices, local(): pieces = lax.all_to_all(pieces, 'pairs', 0, 0, tiled=True)  4.74 us
    ppermute x1, waiting for transfers between devices, exchange_halo(): high = lax.ppermute(low_edge, 'tile', backward)  4.36 us
    ppermute x5, waiting for transfers between devices, swap(): return lax.ppermute(block, 'member', [(0, 1), (1, 0)])  4.02 us
    ppermute x1, starting transfers between devices, exchange_by_member(): came = lax.ppermute(lane, ('member', 'tile'), up + down)  3.5 us
  transfers between devices with their start and end apart: 10, of which 7 were waited for; matrix products, arithmetic and copies ran while one was open for 1% of the time, Pallas kernels for 2%

profile of v7, /device:TPU:0, one launch (start us, length us, event | category | flops | bytes accessed | tf_op | source)
XLA Modules:
  0.0 80.5 jit_solution(17221210586344051860)
XLA Ops:
  1.3 2.0 %pack.1 = (f32[1]{0:T(128)S(4)}, s32[8]{0:T(128)S(4)}, s32[2]{0:T(128)S(4)}, f32[4,136,128]{2,1,0:T(8,128)}, f32[2,8,32,128]{3,2,1,0:T(8,128)S(1)}, /*index=5*/f...) custom-call(f32[1]{0:T(128)S(6)} %copy.12.weight_ref, s32[8]{0:T(128)} %parents_ref.1, ...), custom_call_target="tpu_custom_call" | custom-call | tf_op jit(solution)/shard_map/pack/pallas_call | solution.py:62
  3.3 0.5 collective-permute-start.3
  3.8 4.7 %all-to-all-start = ((f32[4,136,128]{2,1,0:T(8,128)}), f32[4,136,128]{2,1,0:T(8,128)S(1)}, u32[]{:S(2)}, u32[]{:S(2)}) async-start(f32[4,136,128]{2,1,0:T(8,128)} %get-tuple-element.22), calls=%async_computation | async-start | bytes 557056 | tf_op jit(solution)/shard_map/all_to_all | solution.py:322
  8.6 3.5 %collective-permute-start.4 = (f32[18,32,128]{2,1,0:T(8,128)S(1)}, f32[18,32,128]{2,1,0:T(8,128)S(1)}, u32[]{:S(2)}, u32[]{:S(2)}) collective-permute-start(f32[18,32,128]{2,1,0:T(8,128)S(1)} %pad_maximum_fusion), channel_id=1, source_target_pairs={{0,1},{1,2},{2,3},{5,4},{6,5},{7,6},{8,9},{9,10},{10,11},{13,12},{... | collective-permute-start | bytes 884744 | tf_op jit(solution)/shard_map/ppermute | solution.py:308
  12.1 2.6 %all-to-all-done.mine_ref = f32[4,136,128]{2,1,0:T(8,128)S(1)} async-done(((f32[4,136,128]{2,1,0:T(8,128)}), f32[4,136,128]{2,1,0:T(8,128)S(1)}, u32[]{:S(2)}, u32[]{:S(2)}) %all-to-all-start) | async-done | bytes 278560 | tf_op jit(solution)/shard_map/all_to_all | solution.py:322
  14.7 1.6 %collective-permute-done.other_ref = f32[4,136,128]{2,1,0:T(8,128)S(1)} collective-permute-done((f32[4,136,128]{2,1,0:T(8,128)S(1)}, f32[4,136,128]{2,1,0:T(8,128)S(1)}, u32[]{:S(2)}, u32[]{:S(2)}) %collective-permute-start) | collective-permute-done | bytes 278560 | tf_op jit(solution)/shard_map/ppermute | solution.py:298
  16.2 0.7 choose.1
  17.0 3.4 %all-to-all-start.1 = ((f32[4,128,128]{2,1,0:T(8,128)}), f32[4,128,128]{2,1,0:T(8,128)S(1)}, u32[]{:S(2)}, u32[]{:S(2)}) async-start(f32[4,128,128]{2,1,0:T(8,128)} %get-tuple-element.24), calls=%async_computation.1 | async-start | bytes 524288 | tf_op jit(solution)/shard_map/all_to_all | solution.py:325
  20.4 0.2 collective-permute-start.5
  20.7 5.7 %all-to-all-done.1 = f32[4,128,128]{2,1,0:T(8,128)S(1)} async-done(((f32[4,128,128]{2,1,0:T(8,128)}), f32[4,128,128]{2,1,0:T(8,128)S(1)}, u32[]{:S(2)}, u32[]{:S(2)}) %all-to-all-start.1) | async-done | bytes 262176 | tf_op jit(solution)/shard_map/all_to_all | solution.py:325
  26.3 3.5 %collective-permute-start.1 = (f32[8,32,128]{2,1,0:T(8,128)S(1)}, f32[8,32,128]{2,1,0:T(8,128)S(1)}, u32[]{:S(2)}, u32[]{:S(2)}) collective-permute-start(f32[8,32,128]{2,1,0:T(8,128)S(1)} %bitcast.25), channel_id=1, source_target_pairs={{0,1},{1,2},{2,3},{4,5},{5,6},{6,7},{8,9},{9,10},{10,11},{12,13},{... | collective-permute-start | bytes 393224 | tf_op jit(solution)/shard_map/ppermute | solution.py:292
  29.8 1.3 %collective-permute-start.2 = (f32[8,32,128]{2,1,0:T(8,128)S(1)}, f32[8,32,128]{2,1,0:T(8,128)S(1)}, u32[]{:S(2)}, u32[]{:S(2)}) collective-permute-start(f32[8,32,128]{2,1,0:T(8,128)S(1)} %bitcast.24), channel_id=1, source_target_pairs={{1,0},{2,1},{3,2},{5,4},{6,5},{7,6},{9,8},{10,9},{11,10},{13,12},{... | collective-permute-start | bytes 393224 | tf_op jit(solution)/shard_map/ppermute | solution.py:293
  31.2 1.2 %collective-permute-done.1.moved_low = f32[8,32,128]{2,1,0:T(8,128)S(1)} collective-permute-done((f32[8,32,128]{2,1,0:T(8,128)S(1)}, f32[8,32,128]{2,1,0:T(8,128)S(1)}, u32[]{:S(2)}, u32[]{:S(2)}) %collective-permute-start.1) | collective-permute-done | bytes 131104 | tf_op jit(solution)/shard_map/ppermute | solution.py:292
  32.3 4.4 %collective-permute-done.2.moved_high = f32[8,32,128]{2,1,0:T(8,128)S(1)} collective-permute-done((f32[8,32,128]{2,1,0:T(8,128)S(1)}, f32[8,32,128]{2,1,0:T(8,128)S(1)}, u32[]{:S(2)}, u32[]{:S(2)}) %collective-permute-start.2) | collective-permute-done | bytes 131104 | tf_op jit(solution)/shard_map/ppermute | solution.py:293
  36.7 1.1 %moves.1 = (f32[8,32,128]{2,1,0:T(8,128)S(1)}, f32[8,32,128]{2,1,0:T(8,128)S(1)}, f32[32,1024]{1,0:T(8,128)S(1)}) custom-call(s32[2]{0:T(128)S(4)} %get-tuple-element.19.accept_ref, f32[8,128]{1,0:T(8,128)S(1)} %get-tuple-element.23.root_ref, f32[2,8,32,128]{3,2,1,0:T(8,128)S(1)} %bitcast.16, f32[2,8,32,128]{3,2,1,0:T(8,128)S(1)} %get-tuple-element.25.noise_ref, ...), custom_call_target="tpu_custom_call" | custom-call | tf_op jit(solution)/shard_map/moves/pallas_call | solution.py:206
  37.8 15.8 %all_gather.3 = f32[128,1024]{1,0:T(8,128)S(1)} all-gather(f32[32,1024]{1,0:T(8,128)S(1)} %get-tuple-element.31), channel_id=1, replica_groups=mesh['pairs'=4,'member'=2,'tile'=4] {'tile'}, dimensions={0}, use_global_device_ids=true | all-gather | bytes 655360 | tf_op jit(solution)/shard_map/all_gather | solution.py:335
  53.6 0.4 fusion
  54.2 0.4 fusion.2
  54.6 1.5 %collective-permute-done.6 = f32[4,32,1024]{2,1,0:T(8,128)S(1)} collective-permute-done((f32[4,32,1024]{2,1,0:T(8,128)S(1)}, f32[4,32,1024]{2,1,0:T(8,128)S(1)}, u32[]{:S(2)}, u32[]{:S(2)}) %collective-permute-start.6) | collective-permute-done | bytes 524320 | tf_op jit(solution)/shard_map/ppermute | solution.py:298
  56.1 11.5 %all_to_all.20.parts_ref = f32[4,32,1024]{2,1,0:T(8,128)S(1)} all-to-all(f32[4,32,1024]{2,1,0:T(8,128)S(1)} %add.19), channel_id=1, replica_groups=mesh['pairs'=4,'member'=2,'tile'=4] {'pairs'}, dimensions={0} | all-to-all | bytes 1048576 | tf_op jit(solution)/shard_map/all_to_all | solution.py:350
  67.7 10.1 %all_to_all.21 = f32[4,32,1024]{2,1,0:T(8,128)S(1)} all-to-all(f32[4,32,1024]{2,1,0:T(8,128)S(1)} %sum_copies.1), channel_id=1, replica_groups=mesh['pairs'=4,'member'=2,'tile'=4] {'pairs'}, dimensions={0} | all-to-all | bytes 1048576 | tf_op jit(solution)/shard_map/all_to_all | solution.py:351
  77.8 0.9 %store.1 = (f32[8,32,128]{2,1,0:T(8,128)}, f32[8,32,128]{2,1,0:T(8,128)}, f32[256,1024]{1,0:T(8,128)}) custom-call(f32[8,32,128]{2,1,0:T(8,128)S(1)} %get-tuple-element.29.cond_ref, f32[8,32,128]{2,1,0:T(8,128)S(1)} %get-tuple-element.30.pot_ref, f32[128,1024]{1,0:T(8,128)S(1)} %bitcast.17), custom_call_target="tpu_custom_call" | custom-call | tf_op jit(solution)/shard_map/store/pallas_call | solution.py:255
  78.7 1.0 %collective-permute-done.7 = f32[4,32,1024]{2,1,0:T(8,128)S(1)} collective-permute-done((f32[4,32,1024]{2,1,0:T(8,128)S(1)}, f32[4,32,1024]{2,1,0:T(8,128)S(1)}, u32[]{:S(2)}, u32[]{:S(2)}) %collective-permute-start.7) | collective-permute-done | bytes 524320 | tf_op jit(solution)/shard_map/ppermute | solution.py:298
  79.7 0.8 store_other.1
  (12 shorter events, 0.3 us)
Async XLA Ops:
  3.3 5.3 %collective-permute-start.3 = (f32[9,32,128]{2,1,0:T(8,128)S(1)}, f32[9,32,128]{2,1,0:T(8,128)S(1)}, u32[]{:S(2)}, u32[]{:S(2)}) collective-permute-start(f32[9,32,128]{2,1,0:T(8,128)S(1)} %get-tuple-element.38), channel_id=1, source_target_pairs={{0,4},{4,0},{1,5},{5,1},{2,6},{6,2},{3,7},{7,3},{8,12},{12,8},{9,1... | collective-permute-start | bytes 442376 | tf_op jit(solution)/shard_map/ppermute | solution.py:298
  3.8 10.9 %all-to-all-start = ((f32[4,136,128]{2,1,0:T(8,128)}), f32[4,136,128]{2,1,0:T(8,128)S(1)}, u32[]{:S(2)}, u32[]{:S(2)}) async-start(f32[4,136,128]{2,1,0:T(8,128)} %get-tuple-element.22), calls=%async_computation | async-start | bytes 557056 | tf_op jit(solution)/shard_map/all_to_all | solution.py:322
  8.6 11.8 %collective-permute-start.4 = (f32[18,32,128]{2,1,0:T(8,128)S(1)}, f32[18,32,128]{2,1,0:T(8,128)S(1)}, u32[]{:S(2)}, u32[]{:S(2)}) collective-permute-start(f32[18,32,128]{2,1,0:T(8,128)S(1)} %pad_maximum_fusion), channel_id=1, source_target_pairs={{0,1},{1,2},{2,3},{5,4},{6,5},{7,6},{8,9},{9,10},{10,11},{13,12},{... | collective-permute-start | bytes 884744 | tf_op jit(solution)/shard_map/ppermute | solution.py:308
  14.7 1.6 %collective-permute-start = (f32[4,136,128]{2,1,0:T(8,128)S(1)}, f32[4,136,128]{2,1,0:T(8,128)S(1)}, u32[]{:S(2)}, u32[]{:S(2)}) collective-permute-start(f32[4,136,128]{2,1,0:T(8,128)S(1)} %all-to-all-done.mine_ref), channel_id=1, source_target_pairs={{0,4},{4,0},{1,5},{5,1},{2,6},{6,2},{3,7},{7,3},{8,12},{12,8},{9,1... | collective-permute-start | bytes 835592 | tf_op jit(solution)/shard_map/ppermute | solution.py:298
  17.0 9.3 %all-to-all-start.1 = ((f32[4,128,128]{2,1,0:T(8,128)}), f32[4,128,128]{2,1,0:T(8,128)S(1)}, u32[]{:S(2)}, u32[]{:S(2)}) async-start(f32[4,128,128]{2,1,0:T(8,128)} %get-tuple-element.24), calls=%async_computation.1 | async-start | bytes 524288 | tf_op jit(solution)/shard_map/all_to_all | solution.py:325
  20.4 10.7 %collective-permute-start.5 = (f32[9,32,128]{2,1,0:T(8,128)S(1)}, f32[9,32,128]{2,1,0:T(8,128)S(1)}, u32[]{:S(2)}, u32[]{:S(2)}) collective-permute-start(f32[9,32,128]{2,1,0:T(8,128)S(1)} %get-tuple-element.35), channel_id=1, source_target_pairs={{0,4},{4,0},{1,5},{5,1},{2,6},{6,2},{3,7},{7,3},{8,12},{12,8},{9,1... | collective-permute-start | bytes 442376 | tf_op jit(solution)/shard_map/ppermute | solution.py:298
  26.3 6.0 %collective-permute-start.1 = (f32[8,32,128]{2,1,0:T(8,128)S(1)}, f32[8,32,128]{2,1,0:T(8,128)S(1)}, u32[]{:S(2)}, u32[]{:S(2)}) collective-permute-start(f32[8,32,128]{2,1,0:T(8,128)S(1)} %bitcast.25), channel_id=1, source_target_pairs={{0,1},{1,2},{2,3},{4,5},{5,6},{6,7},{8,9},{9,10},{10,11},{12,13},{... | collective-permute-start | bytes 393224 | tf_op jit(solution)/shard_map/ppermute | solution.py:292
  29.8 6.9 %collective-permute-start.2 = (f32[8,32,128]{2,1,0:T(8,128)S(1)}, f32[8,32,128]{2,1,0:T(8,128)S(1)}, u32[]{:S(2)}, u32[]{:S(2)}) collective-permute-start(f32[8,32,128]{2,1,0:T(8,128)S(1)} %bitcast.24), channel_id=1, source_target_pairs={{1,0},{2,1},{3,2},{5,4},{6,5},{7,6},{9,8},{10,9},{11,10},{13,12},{... | collective-permute-start | bytes 393224 | tf_op jit(solution)/shard_map/ppermute | solution.py:293
  54.1 2.0 %collective-permute-start.6 = (f32[4,32,1024]{2,1,0:T(8,128)S(1)}, f32[4,32,1024]{2,1,0:T(8,128)S(1)}, u32[]{:S(2)}, u32[]{:S(2)}) collective-permute-start(f32[4,32,1024]{2,1,0:T(8,128)S(1)} %bitcast.20), channel_id=1, source_target_pairs={{0,4},{4,0},{1,5},{5,1},{2,6},{6,2},{3,7},{7,3},{8,12},{12,8},{9,1... | collective-permute-start | bytes 1572872 | tf_op jit(solution)/shard_map/ppermute | solution.py:298
  77.8 1.9 %collective-permute-start.7 = (f32[4,32,1024]{2,1,0:T(8,128)S(1)}, f32[4,32,1024]{2,1,0:T(8,128)S(1)}, u32[]{:S(2)}, u32[]{:S(2)}) collective-permute-start(f32[4,32,1024]{2,1,0:T(8,128)S(1)} %all_to_all.21), channel_id=1, source_target_pairs={{0,4},{4,0},{1,5},{5,1},{2,6},{6,2},{3,7},{7,3},{8,12},{12,8},{9,1... | collective-permute-start | bytes 1572872 | tf_op jit(solution)/shard_map/ppermute | solution.py:298

commit v8 on v7

--- a/solution.py
+++ b/solution.py
@@ -28,10 +28,13 @@
 
 def pack_kernel(
     rows, depth, weight_ref, parents_ref, accept_ref, cond_ref, pot_ref, noise_ref, source_ref,
-    weight_out, parents_out, accept_out, pieces_ref, noise_out, source_out, low_ref, high_ref, sems,
+    weight_out, parents_out, accept_out, pieces_ref, noise_out, source_out, low_ref, high_ref,
+    weight_rows, sems,
 ):
     moves = noise_ref.shape[0]
-    pairs = [(weight_ref, weight_out), (parents_ref, parents_out), (accept_ref, accept_out)]
+    fetch_weight = pltpu.make_async_copy(weight_ref, weight_out, sems.at[0])
+    fetch_weight.start()
+    pairs = [(parents_ref, parents_out), (accept_ref, accept_out)]
     for piece in range(pieces_ref.shape[0]):
         row = piece * rows
         field = cond_ref if row < cond_ref.shape[0] else pot_ref
@@ -44,15 +47,18 @@
         pairs.append((field.at[pl.ds(field.shape[0] - h, h)], high_ref.at[pl.ds(at, h)]))
         at += h
     copies = [
-        pltpu.make_async_copy(here, there, sems.at[i]) for i, (here, there) in enumerate(pairs)
+        pltpu.make_async_copy(here, there, sems.at[1 + i]) for i, (here, there) in enumerate(pairs)
     ]
     for copy in copies:
         copy.start()
-    for copy in copies:
+    fetch_weight.wait()
+    weight_rows[...] = jnp.full(weight_rows.shape, weight_out[0], jnp.float32)
+    weights = pltpu.make_async_copy(
+        weight_rows, pieces_ref.at[:, pl.ds(rows, 8)], sems.at[1 + len(pairs)]
+    )
+    weights.start()
+    for copy in copies + [weights]:
         copy.wait()
-    weight = jnp.full((8, pieces_ref.shape[2]), weight_out[0], jnp.float32)
-    for piece in range(pieces_ref.shape[0]):
-        pieces_ref[piece, rows:rows + 8] = weight
 
 
 def pack(weights, parents, accept, log_cond, potential, noise, source, pairs, depth):
@@ -65,15 +71,18 @@
             pltpu.SMEM(weights.shape, jnp.float32),
             pltpu.SMEM(parents.shape, jnp.int32),
             pltpu.SMEM(accept.shape, jnp.int32),
-            pltpu.VMEM((pairs, rows + 8, nz), jnp.float32),
+            jax.ShapeDtypeStruct((pairs, rows + 8, nz), jnp.float32),
             pltpu.VMEM(noise.shape, jnp.float32),
             pltpu.VMEM(source.shape, jnp.float32),
             edge,
             edge,
         ),
         in_specs=[ANY] * 7,
-        out_specs=(SMEM,) * 3 + (VMEM,) * 5,
-        scratch_shapes=[pltpu.SemaphoreType.DMA((pairs + 5 + 2 * len(depth),))],
+        out_specs=(SMEM,) * 3 + (ANY,) + (VMEM,) * 4,
+        scratch_shapes=[
+            pltpu.VMEM((pairs, 8, nz), jnp.float32),
+            pltpu.SemaphoreType.DMA((pairs + 6 + 2 * len(depth),)),
+        ],
         name="pack",
     )(weights, parents, accept, log_cond.reshape(-1, nz), potential.reshape(-1, nz), noise, source)
 
@@ -106,6 +115,28 @@
         out_specs=(VMEM, VMEM),
         name="choose",
     )(in_smem(parents), in_smem(weights), in_vmem(mine), in_vmem(other))
+
+
+def cut_kernel(moved_ref, came_ref, low_ref, high_ref, pass_ref):
+    reach = low_ref.shape[0] // 2
+    width = moved_ref.shape[1]
+    for field in range(2):
+        at = field * reach
+        low_ref[at:at + reach] = moved_ref[field, 0:reach]
+        high_ref[at:at + reach] = moved_ref[field, width - reach:width]
+    pass_ref[...] = came_ref[came_ref.shape[0] - pass_ref.shape[0]:]
+
+
+def cut(reach, moved, came):
+    layer = moved.shape[2:]
+    edge = pltpu.VMEM((2 * reach,) + layer, jnp.float32)
+    return pl.pallas_call(
+        cut_kernel,
+        out_shape=(edge, edge, pltpu.VMEM((came.shape[0] // 2,) + layer, jnp.float32)),
+        in_specs=[VMEM] * 2,
+        out_specs=(VMEM,) * 3,
+        name="cut",
+    )(in_vmem(moved), in_vmem(came))
 
 
 def six_sum(before, here, after, edge):
@@ -305,8 +336,7 @@
     even = lax.axis_index("member") == 0
     got = swap(jnp.where(even, low_edge, high_edge))
     lane = jnp.concatenate([jnp.where(even, high_edge, low_edge), got])
-    came = lax.ppermute(lane, ("member", "tile"), up + down)
-    return came[:low_edge.shape[0]], swap(came[low_edge.shape[0]:])
+    return lax.ppermute(lane, ("member", "tile"), up + down)
 
 
 def local(log_cond, potential, noise, source, parents, accept, weights):
@@ -320,14 +350,13 @@
         lax.axis_size("pairs"), depth,
     )
     pieces = lax.all_to_all(pieces, "pairs", 0, 0, tiled=True)
-    fixed_own, fixed_other = exchange_by_member(low_edge, high_edge)
+    came = exchange_by_member(low_edge, high_edge)
     chosen, root = choose(parents, weights, pieces, swap(pieces))
     moved = lax.all_to_all(chosen, "pairs", 0, 0, tiled=True).reshape(2, width, ny, nz)
-    moved_low, moved_high = exchange_halo(
-        moved[:, :reach].reshape(-1, ny, nz), moved[:, width - reach:].reshape(-1, ny, nz)
-    )
+    low_edge, high_edge, other = cut(reach, moved, came)
+    moved_low, moved_high = exchange_halo(low_edge, high_edge)
     conduct, pot, traces = run_moves(
-        depth, accept, root, moved, noise, source, moved_low, moved_high, fixed_own, fixed_other
+        depth, accept, root, moved, noise, source, moved_low, moved_high, came, swap(other)
     )
 
     rows = traces.shape[1] // (lax.axis_size("tile") * pair)

time: 80.9 us -> 89.5 us (1.11)
  Pallas kernels: 5.6 us -> 12.9 us
  waiting for transfers between devices: 17.8 us -> 19.4 us
    pallas_call x1, Pallas kernels: 1.98 us -> 9.2 us  [pack(): pl.pallas_call(functools.partial(pack_kernel, rows, depth), out_shape=(pl...]
    all_to_all x1, waiting for transfers between devices: 2.59 us -> 5.39 us  [local(): pieces = lax.all_to_all(pieces, 'pairs', 0, 0, tiled=True)]
    ppermute x5, waiting for transfers between devices: 4.02 us -> 2.47 us  [swap(): return lax.ppermute(block, 'member', [(0, 1), (1, 0)])]
  transfers between devices with their start and end apart: 10 -> 10, of which waited for: 7 -> 6; matrix products, arithmetic and copies ran while one was open for 1% -> 1% of each run, Pallas kernels for 2% -> 2%
where the time goes in v8:
time: 89.5 us; the launch traced here: 89.1 us
  blocking collectives  37.4 us (42%)
  waiting for transfers between devices  19.4 us (22%)
  starting transfers between devices  17.1 us (19%)
  Pallas kernels  12.9 us (14%)
  between operations  1.43 us (2%)
    all_gather x1, blocking collectives, local(): piece = lax.all_gather(traces, 'tile', axis=0, tiled=True)  15.6 us
    all_to_all x1, blocking collectives, local(): parts = lax.all_to_all(product(member) + got, 'pairs', 0, 0, tiled=True)  11.5 us
    all_to_all x1, blocking collectives, local(): mine = lax.all_to_all(sum_copies(parts), 'pairs', 0, 0, tiled=True)  10.3 us
    pallas_call x1, Pallas kernels, pack(): pl.pallas_call(functools.partial(pack_kernel, rows, depth), out_shape=(pl...  9.2 us
    all_to_all x1, waiting for transfers between devices, local(): pieces = lax.all_to_all(pieces, 'pairs', 0, 0, tiled=True)  5.39 us
    all_to_all x1, waiting for transfers between devices, local(): lax.all_to_all(chosen, 'pairs', 0, 0, tiled=True).reshape(2, width, ny, nz)  5.31 us
    all_to_all x1, starting transfers between devices, local(): pieces = lax.all_to_all(pieces, 'pairs', 0, 0, tiled=True)  5.18 us
    ppermute x1, waiting for transfers between devices, exchange_halo(): high = lax.ppermute(low_edge, 'tile', backward)  4.12 us
  transfers between devices with their start and end apart: 10, of which 6 were waited for; matrix products, arithmetic and copies ran while one was open for 1% of the time, Pallas kernels for 2%

profile of v8, /device:TPU:0, one launch (start us, length us, event | category | flops | bytes accessed | tf_op | source)
XLA Modules:
  0.0 89.1 jit_solution(12001488664707453528)
XLA Ops:
  1.3 9.2 %pack.1 = (f32[1]{0:T(128)S(4)}, s32[8]{0:T(128)S(4)}, s32[2]{0:T(128)S(4)}, f32[4,136,128]{2,1,0:T(8,128)}, f32[2,8,32,128]{3,2,1,0:T(8,128)S(1)}, /*index=5*/f...) custom-call(f32[1]{0:T(128)S(6)} %copy.12.weight_ref, s32[8]{0:T(128)} %parents_ref.1, ...), custom_call_target="tpu_custom_call" | custom-call | tf_op jit(solution)/shard_map/pack/pallas_call | solution.py:68
  10.5 5.2 %all-to-all-start = ((f32[4,136,128]{2,1,0:T(8,128)}), f32[4,136,128]{2,1,0:T(8,128)S(1)}, u32[]{:S(2)}, u32[]{:S(2)}) async-start(f32[4,136,128]{2,1,0:T(8,128)} %get-tuple-element.25), calls=%async_computation | async-start | bytes 557056 | tf_op jit(solution)/shard_map/all_to_all | solution.py:352
  15.7 0.1 collective-permute-start.1
  15.8 5.4 %all-to-all-done.mine_ref = f32[4,136,128]{2,1,0:T(8,128)S(1)} async-done(((f32[4,136,128]{2,1,0:T(8,128)}), f32[4,136,128]{2,1,0:T(8,128)S(1)}, u32[]{:S(2)}, u32[]{:S(2)}) %all-to-all-start) | async-done | bytes 278560 | tf_op jit(solution)/shard_map/all_to_all | solution.py:352
  21.2 3.5 %collective-permute-start.2 = (f32[18,32,128]{2,1,0:T(8,128)S(1)}, f32[18,32,128]{2,1,0:T(8,128)S(1)}, u32[]{:S(2)}, u32[]{:S(2)}) collective-permute-start(f32[18,32,128]{2,1,0:T(8,128)S(1)} %pad_maximum_fusion), channel_id=1, source_target_pairs={{0,1},{1,2},{2,3},{5,4},{6,5},{7,6},{8,9},{9,10},{10,11},{13,12},{... | collective-permute-start | bytes 884744 | tf_op jit(solution)/shard_map/ppermute | solution.py:339
  24.7 0.7 choose.1
  25.5 3.4 %all-to-all-start.1 = ((f32[4,128,128]{2,1,0:T(8,128)}), f32[4,128,128]{2,1,0:T(8,128)S(1)}, u32[]{:S(2)}, u32[]{:S(2)}) async-start(f32[4,128,128]{2,1,0:T(8,128)} %get-tuple-element.27), calls=%async_computation.1 | async-start | bytes 524288 | tf_op jit(solution)/shard_map/all_to_all | solution.py:355
  28.9 5.3 %all-to-all-done.1 = f32[4,128,128]{2,1,0:T(8,128)S(1)} async-done(((f32[4,128,128]{2,1,0:T(8,128)}), f32[4,128,128]{2,1,0:T(8,128)S(1)}, u32[]{:S(2)}, u32[]{:S(2)}) %all-to-all-start.1) | async-done | bytes 262176 | tf_op jit(solution)/shard_map/all_to_all | solution.py:355
  34.2 0.1 collective-permute-start.5
  34.3 3.5 %collective-permute-start.3 = (f32[8,32,128]{2,1,0:T(8,128)S(1)}, f32[8,32,128]{2,1,0:T(8,128)S(1)}, u32[]{:S(2)}, u32[]{:S(2)}) collective-permute-start(f32[8,32,128]{2,1,0:T(8,128)S(1)} %get-tuple-element.32), channel_id=1, source_target_pairs={{0,1},{1,2},{2,3},{4,5},{5,6},{6,7},{8,9},{9,10},{10,11},{12,13},{... | collective-permute-start | bytes 393224 | tf_op jit(solution)/shard_map/ppermute | solution.py:323
  37.8 1.3 %collective-permute-start.4 = (f32[8,32,128]{2,1,0:T(8,128)S(1)}, f32[8,32,128]{2,1,0:T(8,128)S(1)}, u32[]{:S(2)}, u32[]{:S(2)}) collective-permute-start(f32[8,32,128]{2,1,0:T(8,128)S(1)} %get-tuple-element.33), channel_id=1, source_target_pairs={{1,0},{2,1},{3,2},{5,4},{6,5},{7,6},{9,8},{10,9},{11,10},{13,12},{... | collective-permute-start | bytes 393224 | tf_op jit(solution)/shard_map/ppermute | solution.py:324
  39.1 2.1 %collective-permute-done.3.moved_low = f32[8,32,128]{2,1,0:T(8,128)S(1)} collective-permute-done((f32[8,32,128]{2,1,0:T(8,128)S(1)}, f32[8,32,128]{2,1,0:T(8,128)S(1)}, u32[]{:S(2)}, u32[]{:S(2)}) %collective-permute-start.3) | collective-permute-done | bytes 131104 | tf_op jit(solution)/shard_map/ppermute | solution.py:323
  41.2 4.1 %collective-permute-done.4.moved_high = f32[8,32,128]{2,1,0:T(8,128)S(1)} collective-permute-done((f32[8,32,128]{2,1,0:T(8,128)S(1)}, f32[8,32,128]{2,1,0:T(8,128)S(1)}, u32[]{:S(2)}, u32[]{:S(2)}) %collective-permute-start.4) | collective-permute-done | bytes 131104 | tf_op jit(solution)/shard_map/ppermute | solution.py:324
  45.3 1.1 %moves.1 = (f32[8,32,128]{2,1,0:T(8,128)S(1)}, f32[8,32,128]{2,1,0:T(8,128)S(1)}, f32[32,1024]{1,0:T(8,128)S(1)}) custom-call(s32[2]{0:T(128)S(4)} %get-tuple-element.22.accept_ref, f32[8,128]{1,0:T(8,128)S(1)} %get-tuple-element.26.root_ref, f32[2,8,32,128]{3,2,1,0:T(8,128)S(1)} %bitcast.14, f32[2,8,32,128]{3,2,1,0:T(8,128)S(1)} %get-tuple-element.28.noise_ref, ...), custom_call_target="tpu_custom_call" | custom-call | tf_op jit(solution)/shard_map/moves/pallas_call | solution.py:237
  46.4 15.6 %all_gather.3 = f32[128,1024]{1,0:T(8,128)S(1)} all-gather(f32[32,1024]{1,0:T(8,128)S(1)} %get-tuple-element.37), channel_id=1, replica_groups=mesh['pairs'=4,'member'=2,'tile'=4] {'tile'}, dimensions={0}, use_global_device_ids=true | all-gather | bytes 655360 | tf_op jit(solution)/shard_map/all_gather | solution.py:364
  62.0 0.4 fusion
  62.4 0.1 collective-permute-start.6
  62.5 0.4 fusion.2
  62.9 1.5 %collective-permute-done.6 = f32[4,32,1024]{2,1,0:T(8,128)S(1)} collective-permute-done((f32[4,32,1024]{2,1,0:T(8,128)S(1)}, f32[4,32,1024]{2,1,0:T(8,128)S(1)}, u32[]{:S(2)}, u32[]{:S(2)}) %collective-permute-start.6) | collective-permute-done | bytes 524320 | tf_op jit(solution)/shard_map/ppermute | solution.py:329
  64.5 11.5 %all_to_all.20.parts_ref = f32[4,32,1024]{2,1,0:T(8,128)S(1)} all-to-all(f32[4,32,1024]{2,1,0:T(8,128)S(1)} %add.19), channel_id=1, replica_groups=mesh['pairs'=4,'member'=2,'tile'=4] {'pairs'}, dimensions={0} | all-to-all | bytes 1048576 | tf_op jit(solution)/shard_map/all_to_all | solution.py:379
  76.0 10.3 %all_to_all.21 = f32[4,32,1024]{2,1,0:T(8,128)S(1)} all-to-all(f32[4,32,1024]{2,1,0:T(8,128)S(1)} %sum_copies.1), channel_id=1, replica_groups=mesh['pairs'=4,'member'=2,'tile'=4] {'pairs'}, dimensions={0} | all-to-all | bytes 1048576 | tf_op jit(solution)/shard_map/all_to_all | solution.py:380
  86.4 0.9 %store.1 = (f32[8,32,128]{2,1,0:T(8,128)}, f32[8,32,128]{2,1,0:T(8,128)}, f32[256,1024]{1,0:T(8,128)}) custom-call(f32[8,32,128]{2,1,0:T(8,128)S(1)} %get-tuple-element.35.cond_ref, f32[8,32,128]{2,1,0:T(8,128)S(1)} %get-tuple-element.36.pot_ref, f32[128,1024]{1,0:T(8,128)S(1)} %bitcast.15), custom_call_target="tpu_custom_call" | custom-call | tf_op jit(solution)/shard_map/store/pallas_call | solution.py:286
  87.3 1.0 %collective-permute-done.7 = f32[4,32,1024]{2,1,0:T(8,128)S(1)} collective-permute-done((f32[4,32,1024]{2,1,0:T(8,128)S(1)}, f32[4,32,1024]{2,1,0:T(8,128)S(1)}, u32[]{:S(2)}, u32[]{:S(2)}) %collective-permute-start.7) | collective-permute-done | bytes 524320 | tf_op jit(solution)/shard_map/ppermute | solution.py:329
  88.3 0.8 store_other.1
  (11 shorter events, 0.2 us)
Async XLA Ops:
  10.5 10.7 %all-to-all-start = ((f32[4,136,128]{2,1,0:T(8,128)}), f32[4,136,128]{2,1,0:T(8,128)S(1)}, u32[]{:S(2)}, u32[]{:S(2)}) async-start(f32[4,136,128]{2,1,0:T(8,128)} %get-tuple-element.25), calls=%async_computation | async-start | bytes 557056 | tf_op jit(solution)/shard_map/all_to_all | solution.py:352
  15.7 5.5 %collective-permute-start.1 = (f32[9,32,128]{2,1,0:T(8,128)S(1)}, f32[9,32,128]{2,1,0:T(8,128)S(1)}, u32[]{:S(2)}, u32[]{:S(2)}) collective-permute-start(f32[9,32,128]{2,1,0:T(8,128)S(1)} %get-tuple-element.42), channel_id=1, source_target_pairs={{0,4},{4,0},{1,5},{5,1},{2,6},{6,2},{3,7},{7,3},{8,12},{12,8},{9,1... | collective-permute-start | bytes 442376 | tf_op jit(solution)/shard_map/ppermute | solution.py:329
  21.2 3.5 %collective-permute-start = (f32[4,136,128]{2,1,0:T(8,128)S(1)}, f32[4,136,128]{2,1,0:T(8,128)S(1)}, u32[]{:S(2)}, u32[]{:S(2)}) collective-permute-start(f32[4,136,128]{2,1,0:T(8,128)S(1)} %all-to-all-done.mine_ref), channel_id=1, source_target_pairs={{0,4},{4,0},{1,5},{5,1},{2,6},{6,2},{3,7},{7,3},{8,12},{12,8},{9,1... | collective-permute-start | bytes 835592 | tf_op jit(solution)/shard_map/ppermute | solution.py:329
  21.2 7.7 %collective-permute-start.2 = (f32[18,32,128]{2,1,0:T(8,128)S(1)}, f32[18,32,128]{2,1,0:T(8,128)S(1)}, u32[]{:S(2)}, u32[]{:S(2)}) collective-permute-start(f32[18,32,128]{2,1,0:T(8,128)S(1)} %pad_maximum_fusion), channel_id=1, source_target_pairs={{0,1},{1,2},{2,3},{5,4},{6,5},{7,6},{8,9},{9,10},{10,11},{13,12},{... | collective-permute-start | bytes 884744 | tf_op jit(solution)/shard_map/ppermute | solution.py:339
  25.5 8.8 %all-to-all-start.1 = ((f32[4,128,128]{2,1,0:T(8,128)}), f32[4,128,128]{2,1,0:T(8,128)S(1)}, u32[]{:S(2)}, u32[]{:S(2)}) async-start(f32[4,128,128]{2,1,0:T(8,128)} %get-tuple-element.27), calls=%async_computation.1 | async-start | bytes 524288 | tf_op jit(solution)/shard_map/all_to_all | solution.py:355
  34.2 11.1 %collective-permute-start.5 = (f32[9,32,128]{2,1,0:T(8,128)S(1)}, f32[9,32,128]{2,1,0:T(8,128)S(1)}, u32[]{:S(2)}, u32[]{:S(2)}) collective-permute-start(f32[9,32,128]{2,1,0:T(8,128)S(1)} %get-tuple-element.34), channel_id=1, source_target_pairs={{0,4},{4,0},{1,5},{5,1},{2,6},{6,2},{3,7},{7,3},{8,12},{12,8},{9,1... | collective-permute-start | bytes 442376 | tf_op jit(solution)/shard_map/ppermute | solution.py:329
  34.3 6.9 %collective-permute-start.3 = (f32[8,32,128]{2,1,0:T(8,128)S(1)}, f32[8,32,128]{2,1,0:T(8,128)S(1)}, u32[]{:S(2)}, u32[]{:S(2)}) collective-permute-start(f32[8,32,128]{2,1,0:T(8,128)S(1)} %get-tuple-element.32), channel_id=1, source_target_pairs={{0,1},{1,2},{2,3},{4,5},{5,6},{6,7},{8,9},{9,10},{10,11},{12,13},{... | collective-permute-start | bytes 393224 | tf_op jit(solution)/shard_map/ppermute | solution.py:323
  37.8 7.5 %collective-permute-start.4 = (f32[8,32,128]{2,1,0:T(8,128)S(1)}, f32[8,32,128]{2,1,0:T(8,128)S(1)}, u32[]{:S(2)}, u32[]{:S(2)}) collective-permute-start(f32[8,32,128]{2,1,0:T(8,128)S(1)} %get-tuple-element.33), channel_id=1, source_target_pairs={{1,0},{2,1},{3,2},{5,4},{6,5},{7,6},{9,8},{10,9},{11,10},{13,12},{... | collective-permute-start | bytes 393224 | tf_op jit(solution)/shard_map/ppermute | solution.py:324
  62.4 2.0 %collective-permute-start.6 = (f32[4,32,1024]{2,1,0:T(8,128)S(1)}, f32[4,32,1024]{2,1,0:T(8,128)S(1)}, u32[]{:S(2)}, u32[]{:S(2)}) collective-permute-start(f32[4,32,1024]{2,1,0:T(8,128)S(1)} %bitcast.18), channel_id=1, source_target_pairs={{0,4},{4,0},{1,5},{5,1},{2,6},{6,2},{3,7},{7,3},{8,12},{12,8},{9,1... | collective-permute-start | bytes 1572872 | tf_op jit(solution)/shard_map/ppermute | solution.py:329
  86.3 1.9 %collective-permute-start.7 = (f32[4,32,1024]{2,1,0:T(8,128)S(1)}, f32[4,32,1024]{2,1,0:T(8,128)S(1)}, u32[]{:S(2)}, u32[]{:S(2)}) collective-permute-start(f32[4,32,1024]{2,1,0:T(8,128)S(1)} %all_to_all.21), channel_id=1, source_target_pairs={{0,4},{4,0},{1,5},{5,1},{2,6},{6,2},{3,7},{7,3},{8,12},{12,8},{9,1... | collective-permute-start | bytes 1572872 | tf_op jit(solution)/shard_map/ppermute | solution.py:329

commit v9 on v5

--- a/solution.py
+++ b/solution.py
@@ -27,10 +27,9 @@
 
 
 def pack_kernel(
-    rows, depth, weight_ref, parents_ref, accept_ref, cond_ref, pot_ref, noise_ref, source_ref,
-    weight_out, parents_out, accept_out, pieces_ref, noise_out, source_out, low_ref, high_ref, sems,
+    rows, weight_ref, parents_ref, accept_ref, cond_ref, pot_ref, noise_ref, source_ref,
+    weight_out, parents_out, accept_out, pieces_ref, noise_out, source_out, sems,
 ):
-    moves = noise_ref.shape[0]
     pairs = [(weight_ref, weight_out), (parents_ref, parents_out), (accept_ref, accept_out)]
     for piece in range(pieces_ref.shape[0]):
         row = piece * rows
@@ -38,11 +37,6 @@
         row %= cond_ref.shape[0]
         pairs.append((field.at[pl.ds(row, rows)], pieces_ref.at[piece, pl.ds(0, rows)]))
     pairs += [(noise_ref, noise_out), (source_ref, source_out)]
-    at = 0
-    for field, h in zip([noise_ref.at[m] for m in range(moves)] + [source_ref], depth):
-        pairs.append((field.at[pl.ds(0, h)], low_ref.at[pl.ds(at, h)]))
-        pairs.append((field.at[pl.ds(field.shape[0] - h, h)], high_ref.at[pl.ds(at, h)]))
-        at += h
     copies = [
         pltpu.make_async_copy(here, there, sems.at[i]) for i, (here, there) in enumerate(pairs)
     ]
@@ -55,12 +49,11 @@
         pieces_ref[piece, rows:rows + 8] = weight
 
 
-def pack(weights, parents, accept, log_cond, potential, noise, source, pairs, depth):
-    _, ny, nz = source.shape
+def pack(weights, parents, accept, log_cond, potential, noise, source, pairs):
+    nz = source.shape[2]
     rows = 2 * log_cond.size // (pairs * nz)
-    edge = pltpu.VMEM((sum(depth), ny, nz), jnp.float32)
-    return pl.pallas_call(
-        functools.partial(pack_kernel, rows, depth),
+    return pl.pallas_call(
+        functools.partial(pack_kernel, rows),
         out_shape=(
             pltpu.SMEM(weights.shape, jnp.float32),
             pltpu.SMEM(parents.shape, jnp.int32),
@@ -68,12 +61,10 @@
             pltpu.VMEM((pairs, rows + 8, nz), jnp.float32),
             pltpu.VMEM(noise.shape, jnp.float32),
             pltpu.VMEM(source.shape, jnp.float32),
-            edge,
-            edge,
         ),
         in_specs=[ANY] * 7,
-        out_specs=(SMEM,) * 3 + (VMEM,) * 5,
-        scratch_shapes=[pltpu.SemaphoreType.DMA((pairs + 5 + 2 * len(depth),))],
+        out_specs=(SMEM,) * 3 + (VMEM,) * 3,
+        scratch_shapes=[pltpu.SemaphoreType.DMA((pairs + 5,))],
         name="pack",
     )(weights, parents, accept, log_cond.reshape(-1, nz), potential.reshape(-1, nz), noise, source)
 
@@ -119,61 +110,99 @@
     return ((before + after) + (down + up)) + (left + right)
 
 
+def layout(moves):
+    reach = 2 * moves
+    depth = [reach] + [reach - 2 * m for m in range(moves)] + [reach - 1]
+    return [sum(depth[:i]) for i in range(len(depth))], depth
+
+
+def edges_kernel(accept_ref, moved_ref, noise_ref, source_ref, low_ref, high_ref):
+    moves, width = noise_ref.shape[:2]
+    at, depth = layout(moves)
+    for out_ref, place in [(low_ref, lambda h, i: i), (high_ref, lambda h, i: width - h + i)]:
+        for i in range(depth[0]):
+            out_ref[at[0] + i] = moved_ref[1, place(depth[0], i)]
+        for i in range(depth[-1]):
+            out_ref[at[-1] + i] = source_ref[place(depth[-1], i)]
+        conduct = {place(depth[1], i): moved_ref[0, place(depth[1], i)] for i in range(depth[1])}
+        for m in range(moves):
+            accepted = accept_ref[m] > 0
+            for i in range(depth[1 + m]):
+                layer = place(depth[1 + m], i)
+                proposal = prior_keep * conduct[layer] + prior_fresh * noise_ref[m, layer]
+                out_ref[at[1 + m] + i] = proposal
+                conduct[layer] = jnp.where(accepted, proposal, conduct[layer])
+
+
+def edges(accept, moved, noise, source):
+    at, depth = layout(noise.shape[0])
+    out = pltpu.VMEM((sum(depth),) + source.shape[1:], jnp.float32)
+    return pl.pallas_call(
+        edges_kernel,
+        out_shape=(out, out),
+        in_specs=[SMEM] + [VMEM] * 3,
+        out_specs=(VMEM, VMEM),
+        name="edges",
+    )(in_smem(accept), *[in_vmem(field) for field in (moved, noise, source)])
+
+
 def moves_kernel(
-    depth, accept_ref, root_ref, moved_ref, noise_ref, source_ref,
-    moved_low, moved_high, fixed_low, fixed_high,
-    cond_out, pot_out, traces_out, cond, pot, once, conductivity, gain,
+    accept_ref, root_ref, moved_ref, noise_ref, source_ref, low_ref, high_ref,
+    cond_out, pot_out, traces_out, pot, once, conductivity, gain,
 ):
     moves, width, _, nz = noise_ref.shape
     reach = 2 * moves
     span = width + 2 * reach
+    at, depth = layout(moves)
     tile = lax.axis_index("tile")
     first = tile == 0
     last = tile == lax.axis_size("tile") - 1
 
-    def fetch(field, low, high, at, h, i):
+    def halo(number, i):
         if i < 0:
-            return low[at + h + i]
-        if i >= width:
-            return high[at + i - width]
-        return field[i]
+            return low_ref[at[number] + depth[number] + i]
+        return high_ref[at[number] + i - width]
+
+    def own(i):
+        return 0 <= i < width
 
     def keep_inside(value, i):
         outside = (first & (i < reach)) | (last & (i >= reach + width))
         return jnp.where(outside, 0.0, value)
 
+    def sweep(old, lo, hi):
+        for i in range(lo, hi):
+            here, here_k = old[i], conductivity[i]
+            before, after = old[i - 1], old[i + 1]
+            plain = six_sum(before, here, after, 0.0)
+            scaled = six_sum(
+                before * conductivity[i - 1], here * here_k, after * conductivity[i + 1], 0.0
+            )
+            x = i - reach
+            source = source_ref[x] if own(x) else halo(1 + moves, x)
+            value = (1.0 - relax_weight) * here + (
+                2.0 * source + (here_k * plain + scaled)
+            ) * gain[i]
+            yield i, keep_inside(value, i)
+
     for i in range(span):
-        cond[i] = fetch(moved_ref.at[0], moved_low, moved_high, 0, reach, i - reach)
-        pot[i] = fetch(moved_ref.at[1], moved_low, moved_high, reach, reach, i - reach)
-
-    source_at = sum(depth[:moves])
+        x = i - reach
+        pot[i] = moved_ref[1, x] if own(x) else halo(0, x)
+        if own(x):
+            cond_out[x] = moved_ref[0, x]
+
     for m in range(moves):
         start = 2 * m
-        noise_at = sum(depth[:m])
         accepted = accept_ref[m] > 0
-
-        def sweep(old, lo, hi):
-            for i in range(lo, hi):
-                here, here_k = old[i], conductivity[i]
-                before, after = old[i - 1], old[i + 1]
-                plain = six_sum(before, here, after, 0.0)
-                scaled = six_sum(
-                    before * conductivity[i - 1], here * here_k, after * conductivity[i + 1], 0.0
-                )
-                source = fetch(
-                    source_ref, fixed_low, fixed_high, source_at, depth[moves], i - reach
-                )
-                value = (1.0 - relax_weight) * here + (
-                    2.0 * source + (here_k * plain + scaled)
-                ) * gain[i]
-                yield i, keep_inside(value, i)
-
         for i in range(start, span - start):
-            proposal = prior_keep * cond[i] + prior_fresh * fetch(
-                noise_ref.at[m], fixed_low, fixed_high, noise_at, depth[m], i - reach
-            )
+            x = i - reach
+            if own(x):
+                conduct = cond_out[x]
+                proposal = prior_keep * conduct + prior_fresh * noise_ref[m, x]
+                cond_out[x] = jnp.where(accepted, proposal, conduct)
+            else:
+                proposal = halo(1 + m, x)
             conductivity[i] = jnp.exp(proposal)
-            cond[i] = jnp.where(accepted, proposal, cond[i])
         for i in range(start + 1, span - start - 1):
             here_k = conductivity[i]
             gain[i] = relax_weight / (
@@ -185,18 +214,17 @@
             pot[i] = jnp.where(accepted, value, pot[i])
 
     root = root_ref[0:1]
-    for i in range(width):
-        cond_out[i] = cond[i + reach]
-        value = pot[i + reach]
-        pot_out[i] = value
-        traces_out[:, i * nz:(i + 1) * nz] = value * root
-
-
-def run_moves(depth, accept, root, *fields):
+    for x in range(width):
+        value = pot[x + reach]
+        pot_out[x] = value
+        traces_out[:, x * nz:(x + 1) * nz] = value * root
+
+
+def run_moves(accept, root, *fields):
     moves, width, ny, nz = fields[1].shape
     span = width + 4 * moves
     return pl.pallas_call(
-        functools.partial(moves_kernel, depth),
+        moves_kernel,
         out_shape=(
             pltpu.VMEM((width, ny, nz), jnp.float32),
             pltpu.VMEM((width, ny, nz), jnp.float32),
@@ -204,7 +232,7 @@
         ),
         in_specs=[SMEM] + [VMEM] * (1 + len(fields)),
         out_specs=(VMEM, VMEM, VMEM),
-        scratch_shapes=[pltpu.VMEM((span, ny, nz), jnp.float32)] * 5,
+        scratch_shapes=[pltpu.VMEM((span, ny, nz), jnp.float32)] * 4,
         name="moves",
     )(in_smem(accept), in_vmem(root), *[in_vmem(field) for field in fields])
 
@@ -291,25 +319,17 @@
 
 
 def local(log_cond, potential, noise, source, parents, accept, weights):
-    moves = noise.shape[0]
     width, ny, nz = source.shape
-    reach = 2 * moves
-
-    depth = tuple(reach - 2 * m for m in range(moves)) + (reach - 1,)
-    weights, parents, accept, pieces, noise, source, low_edge, high_edge = pack(
+
+    weights, parents, accept, pieces, noise, source = pack(
         weights, parents, accept[:, 0], log_cond, potential, noise[:, 0], source,
-        lax.axis_size("pairs"), depth,
+        lax.axis_size("pairs"),
     )
     pieces = lax.all_to_all(pieces, "pairs", 0, 0, tiled=True)
-    fixed_low, fixed_high = exchange_halo(low_edge, high_edge)
     chosen, root = choose(parents, weights, pieces, swap(pieces))
     moved = lax.all_to_all(chosen, "pairs", 0, 0, tiled=True).reshape(2, width, ny, nz)
-    moved_low, moved_high = exchange_halo(
-        moved[:, :reach].reshape(-1, ny, nz), moved[:, width - reach:].reshape(-1, ny, nz)
-    )
-    conduct, pot, traces = run_moves(
-        depth, accept, root, moved, noise, source, moved_low, moved_high, fixed_low, fixed_high
-    )
+    low, high = exchange_halo(*edges(accept, moved, noise, source))
+    conduct, pot, traces = run_moves(accept, root, moved, noise, source, low, high)
 
     rows = traces.shape[1] // (lax.axis_size("tile") * pair)
     member = lax.axis_index("member")

time: 81 us -> 79.1 us (0.977)
  starting transfers between devices: 13 us -> 4.86 us
  blocking collectives: 49.7 us -> 57 us
    all_to_all x0 -> x1, blocking collectives: none -> 8.68 us  [local(): lax.all_to_all(chosen, 'pairs', 0, 0, tiled=True).reshape(2, width, ny, nz)]
    ppermute x2 -> x1, starting transfers between devices: 6.98 us -> 3.49 us  [exchange_halo(): low = lax.ppermute(high_edge, 'tile', forward)]
    all_to_all x1 -> x0, starting transfers between devices: 3.41 us -> none  [local(): lax.all_to_all(chosen, 'pairs', 0, 0, tiled=True).reshape(2, width, ny, nz)]
    ppermute x2 -> x1, waiting for transfers between devices: 0.93 us -> 2.29 us  [exchange_halo(): low = lax.ppermute(high_edge, 'tile', forward)]
    ppermute x2 -> x1, starting transfers between devices: 2.58 us -> 1.29 us  [exchange_halo(): high = lax.ppermute(low_edge, 'tile', backward)]
    all_to_all x1 -> x0, waiting for transfers between devices: 1.11 us -> none  [local(): lax.all_to_all(chosen, 'pairs', 0, 0, tiled=True).reshape(2, width, ny, nz)]
    all_to_all x1, blocking collectives: 12.6 us -> 11.5 us  [local(): parts = lax.all_to_all(product(member) + got, 'pairs', 0, 0, tiled=True)]
    ppermute x2 -> x1, waiting for transfers between devices: 4.62 us -> 4.14 us  [exchange_halo(): high = lax.ppermute(low_edge, 'tile', backward)]
  transfers between devices with their start and end apart: 8 -> 5, of which waited for: 7 -> 5; matrix products, arithmetic and copies ran while one was open for 1% -> 1% of each run, Pallas kernels for 1% -> 1%
where the time goes in v9:
time: 79.1 us; the launch traced here: 78.8 us
  blocking collectives  57 us (72%)
  waiting for transfers between devices  10.4 us (13%)
  starting transfers between devices  4.86 us (6%)
  Pallas kernels  4.17 us (5%)
  between operations  1.38 us (2%)
  matrix products  0.85 us (1%)
    all_gather x1, blocking collectives, local(): piece = lax.all_gather(traces, 'tile', axis=0, tiled=True)  15.6 us
    all_to_all x1, blocking collectives, local(): parts = lax.all_to_all(product(member) + got, 'pairs', 0, 0, tiled=True)  11.5 us
    all_to_all x1, blocking collectives, local(): pieces = lax.all_to_all(pieces, 'pairs', 0, 0, tiled=True)  11.2 us
    all_to_all x1, blocking collectives, local(): mine = lax.all_to_all(sum_copies(parts), 'pairs', 0, 0, tiled=True)  10.1 us
    all_to_all x1, blocking collectives, local(): lax.all_to_all(chosen, 'pairs', 0, 0, tiled=True).reshape(2, width, ny, nz)  8.68 us
    ppermute x1, waiting for transfers between devices, exchange_halo(): high = lax.ppermute(low_edge, 'tile', backward)  4.14 us
    ppermute x3, waiting for transfers between devices, swap(): return lax.ppermute(block, 'member', [(0, 1), (1, 0)])  4.01 us
    ppermute x1, starting transfers between devices, exchange_halo(): low = lax.ppermute(high_edge, 'tile', forward)  3.49 us
  transfers between devices with their start and end apart: 5, of which 5 were waited for; matrix products, arithmetic and copies ran while one was open for 1% of the time, Pallas kernels for 1%

profile of v9, /device:TPU:0, one launch (start us, length us, event | category | flops | bytes accessed | tf_op | source)
XLA Modules:
  0.0 78.8 jit_solution(11275466811088539754)
XLA Ops:
  1.3 1.2 %pack.1 = (f32[1]{0:T(128)S(4)}, s32[8]{0:T(128)S(4)}, s32[2]{0:T(128)S(4)}, f32[4,136,128]{2,1,0:T(8,128)S(1)}, f32[2,8,32,128]{3,2,1,0:T(8,128)S(1)}, /*index=5*/f32[8,32,128]{2,1,0:T(8,128)S(1)}) custom-call(f32[1]{0:T(128)S(6)} %copy.12.weight_ref, s32[8]{0:T(128)} %parents_ref.1, s32[2]{0:T(128)} %bitcast.22, f32[256,128]{1,0:T(8,128)} %bitcast.20, ...), custom_call_target="tpu_custom_call" | custom-call | tf_op jit(solution)/shard_map/pack/pallas_call | solution.py:55
  2.5 11.2 %all_to_all.20.mine_ref = f32[4,136,128]{2,1,0:T(8,128)S(1)} all-to-all(f32[4,136,128]{2,1,0:T(8,128)S(1)} %get-tuple-element.22), channel_id=1, replica_groups=mesh['pairs'=4,'member'=2,'tile'=4] {'pairs'}, dimensions={0} | all-to-all | bytes 557056 | tf_op jit(solution)/shard_map/all_to_all | solution.py:328
  13.7 0.0 collective-permute-start
  13.7 1.6 %collective-permute-done.other_ref = f32[4,136,128]{2,1,0:T(8,128)S(1)} collective-permute-done((f32[4,136,128]{2,1,0:T(8,128)S(1)}, f32[4,136,128]{2,1,0:T(8,128)S(1)}, u32[]{:S(2)}, u32[]{:S(2)}) %collective-permute-start) | collective-permute-done | bytes 278560 | tf_op jit(solution)/shard_map/ppermute | solution.py:318
  15.3 8.7 %all_to_all.21 = f32[4,128,128]{2,1,0:T(8,128)S(1)} all-to-all(f32[4,128,128]{2,1,0:T(8,128)S(1)} %get-tuple-element.24), channel_id=1, replica_groups=mesh['pairs'=4,'member'=2,'tile'=4] {'pairs'}, dimensions={0} | all-to-all | bytes 524288 | tf_op jit(solution)/shard_map/all_to_all | solution.py:330
  24.0 3.5 %collective-permute-start.1 = (f32[13,32,128]{2,1,0:T(8,128)S(1)}, f32[13,32,128]{2,1,0:T(8,128)S(1)}, u32[]{:S(2)}, u32[]{:S(2)}) collective-permute-start(f32[13,32,128]{2,1,0:T(8,128)S(1)} %get-tuple-element.27), channel_id=1, source_target_pairs={{0,1},{1,2},{2,3},{4,5},{5,6},{6,7},{8,9},{9,10},{10,11},{12,13},{... | collective-permute-start | bytes 638984 | tf_op jit(solution)/shard_map/ppermute | solution.py:312
  27.5 1.3 %collective-permute-start.2 = (f32[13,32,128]{2,1,0:T(8,128)S(1)}, f32[13,32,128]{2,1,0:T(8,128)S(1)}, u32[]{:S(2)}, u32[]{:S(2)}) collective-permute-start(f32[13,32,128]{2,1,0:T(8,128)S(1)} %get-tuple-element.28), channel_id=1, source_target_pairs={{1,0},{2,1},{3,2},{5,4},{6,5},{7,6},{9,8},{10,9},{11,10},{13,12},{... | collective-permute-start | bytes 638984 | tf_op jit(solution)/shard_map/ppermute | solution.py:313
  28.8 2.3 %collective-permute-done.1.low_ref = f32[13,32,128]{2,1,0:T(8,128)S(1)} collective-permute-done((f32[13,32,128]{2,1,0:T(8,128)S(1)}, f32[13,32,128]{2,1,0:T(8,128)S(1)}, u32[]{:S(2)}, u32[]{:S(2)}) %collective-permute-start.1) | collective-permute-done | bytes 213024 | tf_op jit(solution)/shard_map/ppermute | solution.py:312
  31.1 4.1 %collective-permute-done.2.high_ref = f32[13,32,128]{2,1,0:T(8,128)S(1)} collective-permute-done((f32[13,32,128]{2,1,0:T(8,128)S(1)}, f32[13,32,128]{2,1,0:T(8,128)S(1)}, u32[]{:S(2)}, u32[]{:S(2)}) %collective-permute-start.2) | collective-permute-done | bytes 213024 | tf_op jit(solution)/shard_map/ppermute | solution.py:313
  35.2 1.1 %moves.1 = (f32[8,32,128]{2,1,0:T(8,128)S(1)}, f32[8,32,128]{2,1,0:T(8,128)S(1)}, f32[32,1024]{1,0:T(8,128)S(1)}) custom-call(s32[2]{0:T(128)S(4)} %get-tuple-element.19.accept_ref, f32[8,128]{1,0:T(8,128)S(1)} %get-tuple-element.23.root_ref, f32[2,8,32,128]{3,2,1,0:T(8,128)S(1)} %bitcast.14, f32[2,8,32,128]{3,2,1,0:T(8,128)S(1)} %get-tuple-element.25.noise_ref, ...), custom_call_target="tpu_custom_call" | custom-call | tf_op jit(solution)/shard_map/moves/pallas_call | solution.py:226
  36.4 15.6 %all_gather.3 = f32[128,1024]{1,0:T(8,128)S(1)} all-gather(f32[32,1024]{1,0:T(8,128)S(1)} %get-tuple-element.31), channel_id=1, replica_groups=mesh['pairs'=4,'member'=2,'tile'=4] {'tile'}, dimensions={0}, use_global_device_ids=true | all-gather | bytes 655360 | tf_op jit(solution)/shard_map/all_gather | solution.py:336
  52.0 0.4 fusion
  52.4 0.1 collective-permute-start.3
  52.5 0.4 fusion.2
  52.9 1.5 %collective-permute-done.3 = f32[4,32,1024]{2,1,0:T(8,128)S(1)} collective-permute-done((f32[4,32,1024]{2,1,0:T(8,128)S(1)}, f32[4,32,1024]{2,1,0:T(8,128)S(1)}, u32[]{:S(2)}, u32[]{:S(2)}) %collective-permute-start.3) | collective-permute-done | bytes 524320 | tf_op jit(solution)/shard_map/ppermute | solution.py:318
  54.4 0.1 add.19
  54.5 11.5 %all_to_all.22.parts_ref = f32[4,32,1024]{2,1,0:T(8,128)S(1)} all-to-all(f32[4,32,1024]{2,1,0:T(8,128)S(1)} %add.19), channel_id=1, replica_groups=mesh['pairs'=4,'member'=2,'tile'=4] {'pairs'}, dimensions={0} | all-to-all | bytes 1048576 | tf_op jit(solution)/shard_map/all_to_all | solution.py:351
  66.0 10.1 %all_to_all.23 = f32[4,32,1024]{2,1,0:T(8,128)S(1)} all-to-all(f32[4,32,1024]{2,1,0:T(8,128)S(1)} %sum_copies.1), channel_id=1, replica_groups=mesh['pairs'=4,'member'=2,'tile'=4] {'pairs'}, dimensions={0} | all-to-all | bytes 1048576 | tf_op jit(solution)/shard_map/all_to_all | solution.py:352
  76.1 0.0 collective-permute-start.4
  76.1 0.9 %store.1 = (f32[8,32,128]{2,1,0:T(8,128)}, f32[8,32,128]{2,1,0:T(8,128)}, f32[256,1024]{1,0:T(8,128)}) custom-call(f32[8,32,128]{2,1,0:T(8,128)S(1)} %get-tuple-element.29.cond_ref, f32[8,32,128]{2,1,0:T(8,128)S(1)} %get-tuple-element.30.pot_ref, f32[128,1024]{1,0:T(8,128)S(1)} %bitcast.15), custom_call_target="tpu_custom_call" | custom-call | tf_op jit(solution)/shard_map/store/pallas_call | solution.py:275
  77.0 1.0 %collective-permute-done.4 = f32[4,32,1024]{2,1,0:T(8,128)S(1)} collective-permute-done((f32[4,32,1024]{2,1,0:T(8,128)S(1)}, f32[4,32,1024]{2,1,0:T(8,128)S(1)}, u32[]{:S(2)}, u32[]{:S(2)}) %collective-permute-start.4) | collective-permute-done | bytes 524320 | tf_op jit(solution)/shard_map/ppermute | solution.py:318
  78.0 0.8 %store_other.1 = f32[256,1024]{1,0:T(8,128)} custom-call(f32[128,1024]{1,0:T(8,128)S(1)} %bitcast.16, f32[256,1024]{1,0:T(8,128)} %get-tuple-element.34.held_ref), custom_call_target="tpu_custom_call", output_to_operand_aliasing={{}: (1, {})} | custom-call | tf_op jit(solution)/shard_map/store_other/pallas_call | solution.py:297
  (3 shorter events, 0.1 us)
Async XLA Ops:
  13.7 1.6 %collective-permute-start = (f32[4,136,128]{2,1,0:T(8,128)S(1)}, f32[4,136,128]{2,1,0:T(8,128)S(1)}, u32[]{:S(2)}, u32[]{:S(2)}) collective-permute-start(f32[4,136,128]{2,1,0:T(8,128)S(1)} %all_to_all.20.mine_ref), channel_id=1, source_target_pairs={{0,4},{4,0},{1,5},{5,1},{2,6},{6,2},{3,7},{7,3},{8,12},{12,8},{9,1... | collective-permute-start | bytes 835592 | tf_op jit(solution)/shard_map/ppermute | solution.py:318
  24.0 7.1 %collective-permute-start.1 = (f32[13,32,128]{2,1,0:T(8,128)S(1)}, f32[13,32,128]{2,1,0:T(8,128)S(1)}, u32[]{:S(2)}, u32[]{:S(2)}) collective-permute-start(f32[13,32,128]{2,1,0:T(8,128)S(1)} %get-tuple-element.27), channel_id=1, source_target_pairs={{0,1},{1,2},{2,3},{4,5},{5,6},{6,7},{8,9},{9,10},{10,11},{12,13},{... | collective-permute-start | bytes 638984 | tf_op jit(solution)/shard_map/ppermute | solution.py:312
  27.5 7.7 %collective-permute-start.2 = (f32[13,32,128]{2,1,0:T(8,128)S(1)}, f32[13,32,128]{2,1,0:T(8,128)S(1)}, u32[]{:S(2)}, u32[]{:S(2)}) collective-permute-start(f32[13,32,128]{2,1,0:T(8,128)S(1)} %get-tuple-element.28), channel_id=1, source_target_pairs={{1,0},{2,1},{3,2},{5,4},{6,5},{7,6},{9,8},{10,9},{11,10},{13,12},{... | collective-permute-start | bytes 638984 | tf_op jit(solution)/shard_map/ppermute | solution.py:313
  52.4 2.0 %collective-permute-start.3 = (f32[4,32,1024]{2,1,0:T(8,128)S(1)}, f32[4,32,1024]{2,1,0:T(8,128)S(1)}, u32[]{:S(2)}, u32[]{:S(2)}) collective-permute-start(f32[4,32,1024]{2,1,0:T(8,128)S(1)} %bitcast.18), channel_id=1, source_target_pairs={{0,4},{4,0},{1,5},{5,1},{2,6},{6,2},{3,7},{7,3},{8,12},{12,8},{9,1... | collective-permute-start | bytes 1572872 | tf_op jit(solution)/shard_map/ppermute | solution.py:318
  76.1 1.9 %collective-permute-start.4 = (f32[4,32,1024]{2,1,0:T(8,128)S(1)}, f32[4,32,1024]{2,1,0:T(8,128)S(1)}, u32[]{:S(2)}, u32[]{:S(2)}) collective-permute-start(f32[4,32,1024]{2,1,0:T(8,128)S(1)} %all_to_all.23), channel_id=1, source_target_pairs={{0,4},{4,0},{1,5},{5,1},{2,6},{6,2},{3,7},{7,3},{8,12},{12,8},{9,1... | collective-permute-start | bytes 1572872 | tf_op jit(solution)/shard_map/ppermute | solution.py:318

commit v10 on v9

--- a/solution.py
+++ b/solution.py
@@ -99,15 +99,15 @@
     )(in_smem(parents), in_smem(weights), in_vmem(mine), in_vmem(other))
 
 
-def six_sum(before, here, after, edge):
-    row = lax.broadcasted_iota(jnp.int32, here.shape, 0)
-    lane = lax.broadcasted_iota(jnp.int32, here.shape, 1)
+def shifts(here):
     ny, nz = here.shape
-    down = jnp.where(row == 0, edge, pltpu.roll(here, 1, 0))
-    up = jnp.where(row == ny - 1, edge, pltpu.roll(here, ny - 1, 0))
-    left = jnp.where(lane == 0, edge, pltpu.roll(here, 1, 1))
-    right = jnp.where(lane == nz - 1, edge, pltpu.roll(here, nz - 1, 1))
-    return ((before + after) + (down + up)) + (left + right)
+    return [pltpu.roll(here, by, axis) for by, axis in [(1, 0), (ny - 1, 0), (1, 1), (nz - 1, 1)]]
+
+
+def outer(shape):
+    row = lax.broadcasted_iota(jnp.int32, shape, 0)
+    lane = lax.broadcasted_iota(jnp.int32, shape, 1)
+    return [row == 0, row == shape[0] - 1, lane == 0, lane == shape[1] - 1]
 
 
 def layout(moves):
@@ -148,9 +148,9 @@
 
 def moves_kernel(
     accept_ref, root_ref, moved_ref, noise_ref, source_ref, low_ref, high_ref,
-    cond_out, pot_out, traces_out, pot, once, conductivity, gain,
+    cond_out, pot_out, traces_out, pot, once, conductivity, gain, faces,
 ):
-    moves, width, _, nz = noise_ref.shape
+    moves, width, ny, nz = noise_ref.shape
     reach = 2 * moves
     span = width + 2 * reach
     at, depth = layout(moves)
@@ -173,15 +173,15 @@
     def sweep(old, lo, hi):
         for i in range(lo, hi):
             here, here_k = old[i], conductivity[i]
-            before, after = old[i - 1], old[i + 1]
-            plain = six_sum(before, here, after, 0.0)
-            scaled = six_sum(
-                before * conductivity[i - 1], here * here_k, after * conductivity[i + 1], 0.0
-            )
+            flux = (here_k + conductivity[i - 1]) * old[i - 1] + (
+                here_k + conductivity[i + 1]
+            ) * old[i + 1]
+            for side, near in enumerate(shifts(here)):
+                flux += faces[side, i] * near
             x = i - reach
             source = source_ref[x] if own(x) else halo(1 + moves, x)
             value = (1.0 - relax_weight) * here + (
-                2.0 * source + (here_k * plain + scaled)
+                2.0 * source + flux
             ) * gain[i]
             yield i, keep_inside(value, i)
 
@@ -205,9 +205,11 @@
             conductivity[i] = jnp.exp(proposal)
         for i in range(start + 1, span - start - 1):
             here_k = conductivity[i]
-            gain[i] = relax_weight / (
-                6.0 * here_k + six_sum(conductivity[i - 1], here_k, conductivity[i + 1], 1.0)
-            )
+            total = 6.0 * here_k + conductivity[i - 1] + conductivity[i + 1]
+            for side, (near, outside) in enumerate(zip(shifts(here_k), outer((ny, nz)))):
+                total += jnp.where(outside, 1.0, near)
+                faces[side, i] = jnp.where(outside, 0.0, here_k + near)
+            gain[i] = relax_weight / total
         for i, value in sweep(pot, start + 1, span - start - 1):
             once[i] = value
         for i, value in sweep(once, start + 2, span - start - 2):
@@ -232,7 +234,8 @@
         ),
         in_specs=[SMEM] + [VMEM] * (1 + len(fields)),
         out_specs=(VMEM, VMEM, VMEM),
-        scratch_shapes=[pltpu.VMEM((span, ny, nz), jnp.float32)] * 4,
+        scratch_shapes=[pltpu.VMEM((span, ny, nz), jnp.float32)] * 4
+        + [pltpu.VMEM((4, span, ny, nz), jnp.float32)],
         name="moves",
     )(in_smem(accept), in_vmem(root), *[in_vmem(field) for field in fields])
 

time: 79.1 us -> 79 us (level)
  no operation moved by 1% of the time
where the time goes in v10:
time: 79 us; the launch traced here: 78.6 us
  blocking collectives  57 us (72%)
  waiting for transfers between devices  10.4 us (13%)
  starting transfers between devices  4.86 us (6%)
  Pallas kernels  3.98 us (5%)
  between operations  1.38 us (2%)
  matrix products  0.85 us (1%)
    all_gather x1, blocking collectives, local(): piece = lax.all_gather(traces, 'tile', axis=0, tiled=True)  15.6 us
    all_to_all x1, blocking collectives, local(): parts = lax.all_to_all(product(member) + got, 'pairs', 0, 0, tiled=True)  11.5 us
    all_to_all x1, blocking collectives, local(): pieces = lax.all_to_all(pieces, 'pairs', 0, 0, tiled=True)  11.2 us
    all_to_all x1, blocking collectives, local(): mine = lax.all_to_all(sum_copies(parts), 'pairs', 0, 0, tiled=True)  10.1 us
    all_to_all x1, blocking collectives, local(): lax.all_to_all(chosen, 'pairs', 0, 0, tiled=True).reshape(2, width, ny, nz)  8.68 us
    ppermute x1, waiting for transfers between devices, exchange_halo(): high = lax.ppermute(low_edge, 'tile', backward)  4.14 us
    ppermute x3, waiting for transfers between devices, swap(): return lax.ppermute(block, 'member', [(0, 1), (1, 0)])  4.01 us
    ppermute x1, starting transfers between devices, exchange_halo(): low = lax.ppermute(high_edge, 'tile', forward)  3.49 us
  transfers between devices with their start and end apart: 5, of which 5 were waited for; matrix products, arithmetic and copies ran while one was open for 1% of the time, Pallas kernels for 1%

profile of v10, /device:TPU:0, one launch (start us, length us, event | category | flops | bytes accessed | tf_op | source)
XLA Modules:
  0.0 78.6 jit_solution(4462182721168290242)
XLA Ops:
  1.3 1.2 %pack.1 = (f32[1]{0:T(128)S(4)}, s32[8]{0:T(128)S(4)}, s32[2]{0:T(128)S(4)}, f32[4,136,128]{2,1,0:T(8,128)S(1)}, f32[2,8,32,128]{3,2,1,0:T(8,128)S(1)}, /*index=5*/f32[8,32,128]{2,1,0:T(8,128)S(1)}) custom-call(f32[1]{0:T(128)S(6)} %copy.12.weight_ref, s32[8]{0:T(128)} %parents_ref.1, s32[2]{0:T(128)} %bitcast.22, f32[256,128]{1,0:T(8,128)} %bitcast.20, ...), custom_call_target="tpu_custom_call" | custom-call | tf_op jit(solution)/shard_map/pack/pallas_call | solution.py:55
  2.5 11.2 %all_to_all.20.mine_ref = f32[4,136,128]{2,1,0:T(8,128)S(1)} all-to-all(f32[4,136,128]{2,1,0:T(8,128)S(1)} %get-tuple-element.22), channel_id=1, replica_groups=mesh['pairs'=4,'member'=2,'tile'=4] {'pairs'}, dimensions={0} | all-to-all | bytes 557056 | tf_op jit(solution)/shard_map/all_to_all | solution.py:331
  13.7 0.0 collective-permute-start
  13.7 1.6 %collective-permute-done.other_ref = f32[4,136,128]{2,1,0:T(8,128)S(1)} collective-permute-done((f32[4,136,128]{2,1,0:T(8,128)S(1)}, f32[4,136,128]{2,1,0:T(8,128)S(1)}, u32[]{:S(2)}, u32[]{:S(2)}) %collective-permute-start) | collective-permute-done | bytes 278560 | tf_op jit(solution)/shard_map/ppermute | solution.py:321
  15.3 8.7 %all_to_all.21 = f32[4,128,128]{2,1,0:T(8,128)S(1)} all-to-all(f32[4,128,128]{2,1,0:T(8,128)S(1)} %get-tuple-element.24), channel_id=1, replica_groups=mesh['pairs'=4,'member'=2,'tile'=4] {'pairs'}, dimensions={0} | all-to-all | bytes 524288 | tf_op jit(solution)/shard_map/all_to_all | solution.py:333
  24.0 3.5 %collective-permute-start.1 = (f32[13,32,128]{2,1,0:T(8,128)S(1)}, f32[13,32,128]{2,1,0:T(8,128)S(1)}, u32[]{:S(2)}, u32[]{:S(2)}) collective-permute-start(f32[13,32,128]{2,1,0:T(8,128)S(1)} %get-tuple-element.27), channel_id=1, source_target_pairs={{0,1},{1,2},{2,3},{4,5},{5,6},{6,7},{8,9},{9,10},{10,11},{12,13},{... | collective-permute-start | bytes 638984 | tf_op jit(solution)/shard_map/ppermute | solution.py:315
  27.5 1.3 %collective-permute-start.2 = (f32[13,32,128]{2,1,0:T(8,128)S(1)}, f32[13,32,128]{2,1,0:T(8,128)S(1)}, u32[]{:S(2)}, u32[]{:S(2)}) collective-permute-start(f32[13,32,128]{2,1,0:T(8,128)S(1)} %get-tuple-element.28), channel_id=1, source_target_pairs={{1,0},{2,1},{3,2},{5,4},{6,5},{7,6},{9,8},{10,9},{11,10},{13,12},{... | collective-permute-start | bytes 638984 | tf_op jit(solution)/shard_map/ppermute | solution.py:316
  28.8 2.3 %collective-permute-done.1.low_ref = f32[13,32,128]{2,1,0:T(8,128)S(1)} collective-permute-done((f32[13,32,128]{2,1,0:T(8,128)S(1)}, f32[13,32,128]{2,1,0:T(8,128)S(1)}, u32[]{:S(2)}, u32[]{:S(2)}) %collective-permute-start.1) | collective-permute-done | bytes 213024 | tf_op jit(solution)/shard_map/ppermute | solution.py:315
  31.1 4.1 %collective-permute-done.2.high_ref = f32[13,32,128]{2,1,0:T(8,128)S(1)} collective-permute-done((f32[13,32,128]{2,1,0:T(8,128)S(1)}, f32[13,32,128]{2,1,0:T(8,128)S(1)}, u32[]{:S(2)}, u32[]{:S(2)}) %collective-permute-start.2) | collective-permute-done | bytes 213024 | tf_op jit(solution)/shard_map/ppermute | solution.py:316
  35.2 0.9 %moves.1 = (f32[8,32,128]{2,1,0:T(8,128)S(1)}, f32[8,32,128]{2,1,0:T(8,128)S(1)}, f32[32,1024]{1,0:T(8,128)S(1)}) custom-call(s32[2]{0:T(128)S(4)} %get-tuple-element.19.accept_ref, f32[8,128]{1,0:T(8,128)S(1)} %get-tuple-element.23.root_ref, f32[2,8,32,128]{3,2,1,0:T(8,128)S(1)} %bitcast.14, f32[2,8,32,128]{3,2,1,0:T(8,128)S(1)} %get-tuple-element.25.noise_ref, ...), custom_call_target="tpu_custom_call" | custom-call | tf_op jit(solution)/shard_map/moves/pallas_call | solution.py:228
  36.2 15.6 %all_gather.3 = f32[128,1024]{1,0:T(8,128)S(1)} all-gather(f32[32,1024]{1,0:T(8,128)S(1)} %get-tuple-element.31), channel_id=1, replica_groups=mesh['pairs'=4,'member'=2,'tile'=4] {'tile'}, dimensions={0}, use_global_device_ids=true | all-gather | bytes 655360 | tf_op jit(solution)/shard_map/all_gather | solution.py:339
  51.8 0.4 fusion
  52.2 0.1 collective-permute-start.3
  52.3 0.4 fusion.2
  52.7 1.5 %collective-permute-done.3 = f32[4,32,1024]{2,1,0:T(8,128)S(1)} collective-permute-done((f32[4,32,1024]{2,1,0:T(8,128)S(1)}, f32[4,32,1024]{2,1,0:T(8,128)S(1)}, u32[]{:S(2)}, u32[]{:S(2)}) %collective-permute-start.3) | collective-permute-done | bytes 524320 | tf_op jit(solution)/shard_map/ppermute | solution.py:321
  54.2 0.1 add.19
  54.3 11.5 %all_to_all.22.parts_ref = f32[4,32,1024]{2,1,0:T(8,128)S(1)} all-to-all(f32[4,32,1024]{2,1,0:T(8,128)S(1)} %add.19), channel_id=1, replica_groups=mesh['pairs'=4,'member'=2,'tile'=4] {'pairs'}, dimensions={0} | all-to-all | bytes 1048576 | tf_op jit(solution)/shard_map/all_to_all | solution.py:354
  65.8 10.1 %all_to_all.23 = f32[4,32,1024]{2,1,0:T(8,128)S(1)} all-to-all(f32[4,32,1024]{2,1,0:T(8,128)S(1)} %sum_copies.1), channel_id=1, replica_groups=mesh['pairs'=4,'member'=2,'tile'=4] {'pairs'}, dimensions={0} | all-to-all | bytes 1048576 | tf_op jit(solution)/shard_map/all_to_all | solution.py:355
  75.9 0.0 collective-permute-start.4
  75.9 0.9 %store.1 = (f32[8,32,128]{2,1,0:T(8,128)}, f32[8,32,128]{2,1,0:T(8,128)}, f32[256,1024]{1,0:T(8,128)}) custom-call(f32[8,32,128]{2,1,0:T(8,128)S(1)} %get-tuple-element.29.cond_ref, f32[8,32,128]{2,1,0:T(8,128)S(1)} %get-tuple-element.30.pot_ref, f32[128,1024]{1,0:T(8,128)S(1)} %bitcast.15), custom_call_target="tpu_custom_call" | custom-call | tf_op jit(solution)/shard_map/store/pallas_call | solution.py:278
  76.8 1.0 %collective-permute-done.4 = f32[4,32,1024]{2,1,0:T(8,128)S(1)} collective-permute-done((f32[4,32,1024]{2,1,0:T(8,128)S(1)}, f32[4,32,1024]{2,1,0:T(8,128)S(1)}, u32[]{:S(2)}, u32[]{:S(2)}) %collective-permute-start.4) | collective-permute-done | bytes 524320 | tf_op jit(solution)/shard_map/ppermute | solution.py:321
  77.8 0.8 %store_other.1 = f32[256,1024]{1,0:T(8,128)} custom-call(f32[128,1024]{1,0:T(8,128)S(1)} %bitcast.16, f32[256,1024]{1,0:T(8,128)} %get-tuple-element.34.held_ref), custom_call_target="tpu_custom_call", output_to_operand_aliasing={{}: (1, {})} | custom-call | tf_op jit(solution)/shard_map/store_other/pallas_call | solution.py:300
  (3 shorter events, 0.1 us)
Async XLA Ops:
  13.7 1.6 %collective-permute-start = (f32[4,136,128]{2,1,0:T(8,128)S(1)}, f32[4,136,128]{2,1,0:T(8,128)S(1)}, u32[]{:S(2)}, u32[]{:S(2)}) collective-permute-start(f32[4,136,128]{2,1,0:T(8,128)S(1)} %all_to_all.20.mine_ref), channel_id=1, source_target_pairs={{0,4},{4,0},{1,5},{5,1},{2,6},{6,2},{3,7},{7,3},{8,12},{12,8},{9,1... | collective-permute-start | bytes 835592 | tf_op jit(solution)/shard_map/ppermute | solution.py:321
  24.0 7.1 %collective-permute-start.1 = (f32[13,32,128]{2,1,0:T(8,128)S(1)}, f32[13,32,128]{2,1,0:T(8,128)S(1)}, u32[]{:S(2)}, u32[]{:S(2)}) collective-permute-start(f32[13,32,128]{2,1,0:T(8,128)S(1)} %get-tuple-element.27), channel_id=1, source_target_pairs={{0,1},{1,2},{2,3},{4,5},{5,6},{6,7},{8,9},{9,10},{10,11},{12,13},{... | collective-permute-start | bytes 638984 | tf_op jit(solution)/shard_map/ppermute | solution.py:315
  27.5 7.7 %collective-permute-start.2 = (f32[13,32,128]{2,1,0:T(8,128)S(1)}, f32[13,32,128]{2,1,0:T(8,128)S(1)}, u32[]{:S(2)}, u32[]{:S(2)}) collective-permute-start(f32[13,32,128]{2,1,0:T(8,128)S(1)} %get-tuple-element.28), channel_id=1, source_target_pairs={{1,0},{2,1},{3,2},{5,4},{6,5},{7,6},{9,8},{10,9},{11,10},{13,12},{... | collective-permute-start | bytes 638984 | tf_op jit(solution)/shard_map/ppermute | solution.py:316
  52.2 2.0 %collective-permute-start.3 = (f32[4,32,1024]{2,1,0:T(8,128)S(1)}, f32[4,32,1024]{2,1,0:T(8,128)S(1)}, u32[]{:S(2)}, u32[]{:S(2)}) collective-permute-start(f32[4,32,1024]{2,1,0:T(8,128)S(1)} %bitcast.18), channel_id=1, source_target_pairs={{0,4},{4,0},{1,5},{5,1},{2,6},{6,2},{3,7},{7,3},{8,12},{12,8},{9,1... | collective-permute-start | bytes 1572872 | tf_op jit(solution)/shard_map/ppermute | solution.py:321
  75.9 1.9 %collective-permute-start.4 = (f32[4,32,1024]{2,1,0:T(8,128)S(1)}, f32[4,32,1024]{2,1,0:T(8,128)S(1)}, u32[]{:S(2)}, u32[]{:S(2)}) collective-permute-start(f32[4,32,1024]{2,1,0:T(8,128)S(1)} %all_to_all.23), channel_id=1, source_target_pairs={{0,4},{4,0},{1,5},{5,1},{2,6},{6,2},{3,7},{7,3},{8,12},{12,8},{9,1... | collective-permute-start | bytes 1572872 | tf_op jit(solution)/shard_map/ppermute | solution.py:321

commit v11 on v10

--- a/solution.py
+++ b/solution.py
@@ -24,6 +24,14 @@
 
 def in_vmem(array):
     return pltpu.with_memory_space_constraint(array, pltpu.VMEM)
+
+
+def quarters(here, there):
+    layers = max(1, here.shape[0] // 4)
+    return [
+        (here.at[pl.ds(i, layers)], there.at[pl.ds(i, layers)])
+        for i in range(0, here.shape[0], layers)
+    ]
 
 
 def pack_kernel(
@@ -36,7 +44,9 @@
         field = cond_ref if row < cond_ref.shape[0] else pot_ref
         row %= cond_ref.shape[0]
         pairs.append((field.at[pl.ds(row, rows)], pieces_ref.at[piece, pl.ds(0, rows)]))
-    pairs += [(noise_ref, noise_out), (source_ref, source_out)]
+    for move in range(noise_ref.shape[0]):
+        pairs += quarters(noise_ref.at[move], noise_out.at[move])
+    pairs += quarters(source_ref, source_out)
     copies = [
         pltpu.make_async_copy(here, there, sems.at[i]) for i, (here, there) in enumerate(pairs)
     ]
@@ -64,7 +74,7 @@
         ),
         in_specs=[ANY] * 7,
         out_specs=(SMEM,) * 3 + (VMEM,) * 3,
-        scratch_shapes=[pltpu.SemaphoreType.DMA((pairs + 5,))],
+        scratch_shapes=[pltpu.SemaphoreType.DMA((pairs + 3 + 8 * (1 + noise.shape[0]),))],
         name="pack",
     )(weights, parents, accept, log_cond.reshape(-1, nz), potential.reshape(-1, nz), noise, source)
 
@@ -289,11 +299,19 @@
     )(in_vmem(conduct), in_vmem(pot), in_vmem(half))
 
 
-def store_other_kernel(half_ref, held_ref, rows_out, sem):
+def store_other_kernel(half_ref, held_ref, rows_out, sems):
     other = own_rows(rows_out, half_ref.shape[0], 1 - lax.axis_index("member"))
-    copy = pltpu.make_async_copy(half_ref, other, sem)
-    copy.start()
-    copy.wait()
+    rows = half_ref.shape[0] // sems.shape[0]
+    copies = [
+        pltpu.make_async_copy(
+            half_ref.at[pl.ds(i * rows, rows)], other.at[pl.ds(i * rows, rows)], sems.at[i]
+        )
+        for i in range(sems.shape[0])
+    ]
+    for copy in copies:
+        copy.start()
+    for copy in copies:
+        copy.wait()
 
 
 def store_other(half, held):
@@ -302,7 +320,7 @@
         out_shape=jax.ShapeDtypeStruct(held.shape, jnp.float32),
         in_specs=[VMEM, ANY],
         out_specs=ANY,
-        scratch_shapes=[pltpu.SemaphoreType.DMA],
+        scratch_shapes=[pltpu.SemaphoreType.DMA((max(1, half.shape[0] // 16),))],
         input_output_aliases={1: 0},
         name="store_other",
     )(in_vmem(half), held)

time: 79 us -> 79.2 us (level)
  no operation moved by 1% of the time
where the time goes in v11:
time: 79.2 us; the launch traced here: 78.8 us
  blocking collectives  57 us (72%)
  waiting for transfers between devices  10.4 us (13%)
  starting transfers between devices  4.86 us (6%)
  Pallas kernels  4.13 us (5%)
  between operations  1.38 us (2%)
  matrix products  0.85 us (1%)
    all_gather x1, blocking collectives, local(): piece = lax.all_gather(traces, 'tile', axis=0, tiled=True)  15.6 us
    all_to_all x1, blocking collectives, local(): parts = lax.all_to_all(product(member) + got, 'pairs', 0, 0, tiled=True)  11.5 us
    all_to_all x1, blocking collectives, local(): pieces = lax.all_to_all(pieces, 'pairs', 0, 0, tiled=True)  11.2 us
    all_to_all x1, blocking collectives, local(): mine = lax.all_to_all(sum_copies(parts), 'pairs', 0, 0, tiled=True)  10.1 us
    all_to_all x1, blocking collectives, local(): lax.all_to_all(chosen, 'pairs', 0, 0, tiled=True).reshape(2, width, ny, nz)  8.68 us
    ppermute x1, waiting for transfers between devices, exchange_halo(): high = lax.ppermute(low_edge, 'tile', backward)  4.14 us
    ppermute x3, waiting for transfers between devices, swap(): return lax.ppermute(block, 'member', [(0, 1), (1, 0)])  4.01 us
    ppermute x1, starting transfers between devices, exchange_halo(): low = lax.ppermute(high_edge, 'tile', forward)  3.49 us
  transfers between devices with their start and end apart: 5, of which 5 were waited for; matrix products, arithmetic and copies ran while one was open for 1% of the time, Pallas kernels for 1%

profile of v11, /device:TPU:0, one launch (start us, length us, event | category | flops | bytes accessed | tf_op | source)
XLA Modules:
  0.0 78.8 jit_solution(14598820168982827058)
XLA Ops:
  1.3 1.3 %pack.1 = (f32[1]{0:T(128)S(4)}, s32[8]{0:T(128)S(4)}, s32[2]{0:T(128)S(4)}, f32[4,136,128]{2,1,0:T(8,128)S(1)}, f32[2,8,32,128]{3,2,1,0:T(8,128)S(1)}, /*index=5*/f32[8,32,128]{2,1,0:T(8,128)S(1)}) custom-call(f32[1]{0:T(128)S(6)} %copy.12.weight_ref, s32[8]{0:T(128)} %parents_ref.1, s32[2]{0:T(128)} %bitcast.22, f32[256,128]{1,0:T(8,128)} %bitcast.20, ...), custom_call_target="tpu_custom_call" | custom-call | tf_op jit(solution)/shard_map/pack/pallas_call | solution.py:65
  2.6 11.2 %all_to_all.20.mine_ref = f32[4,136,128]{2,1,0:T(8,128)S(1)} all-to-all(f32[4,136,128]{2,1,0:T(8,128)S(1)} %get-tuple-element.22), channel_id=1, replica_groups=mesh['pairs'=4,'member'=2,'tile'=4] {'pairs'}, dimensions={0} | all-to-all | bytes 557056 | tf_op jit(solution)/shard_map/all_to_all | solution.py:349
  13.8 0.0 collective-permute-start
  13.8 1.6 %collective-permute-done.other_ref = f32[4,136,128]{2,1,0:T(8,128)S(1)} collective-permute-done((f32[4,136,128]{2,1,0:T(8,128)S(1)}, f32[4,136,128]{2,1,0:T(8,128)S(1)}, u32[]{:S(2)}, u32[]{:S(2)}) %collective-permute-start) | collective-permute-done | bytes 278560 | tf_op jit(solution)/shard_map/ppermute | solution.py:339
  15.4 8.7 %all_to_all.21 = f32[4,128,128]{2,1,0:T(8,128)S(1)} all-to-all(f32[4,128,128]{2,1,0:T(8,128)S(1)} %get-tuple-element.24), channel_id=1, replica_groups=mesh['pairs'=4,'member'=2,'tile'=4] {'pairs'}, dimensions={0} | all-to-all | bytes 524288 | tf_op jit(solution)/shard_map/all_to_all | solution.py:351
  24.1 3.5 %collective-permute-start.1 = (f32[13,32,128]{2,1,0:T(8,128)S(1)}, f32[13,32,128]{2,1,0:T(8,128)S(1)}, u32[]{:S(2)}, u32[]{:S(2)}) collective-permute-start(f32[13,32,128]{2,1,0:T(8,128)S(1)} %get-tuple-element.27), channel_id=1, source_target_pairs={{0,1},{1,2},{2,3},{4,5},{5,6},{6,7},{8,9},{9,10},{10,11},{12,13},{... | collective-permute-start | bytes 638984 | tf_op jit(solution)/shard_map/ppermute | solution.py:333
  27.6 1.3 %collective-permute-start.2 = (f32[13,32,128]{2,1,0:T(8,128)S(1)}, f32[13,32,128]{2,1,0:T(8,128)S(1)}, u32[]{:S(2)}, u32[]{:S(2)}) collective-permute-start(f32[13,32,128]{2,1,0:T(8,128)S(1)} %get-tuple-element.28), channel_id=1, source_target_pairs={{1,0},{2,1},{3,2},{5,4},{6,5},{7,6},{9,8},{10,9},{11,10},{13,12},{... | collective-permute-start | bytes 638984 | tf_op jit(solution)/shard_map/ppermute | solution.py:334
  28.9 2.3 %collective-permute-done.1.low_ref = f32[13,32,128]{2,1,0:T(8,128)S(1)} collective-permute-done((f32[13,32,128]{2,1,0:T(8,128)S(1)}, f32[13,32,128]{2,1,0:T(8,128)S(1)}, u32[]{:S(2)}, u32[]{:S(2)}) %collective-permute-start.1) | collective-permute-done | bytes 213024 | tf_op jit(solution)/shard_map/ppermute | solution.py:333
  31.2 4.1 %collective-permute-done.2.high_ref = f32[13,32,128]{2,1,0:T(8,128)S(1)} collective-permute-done((f32[13,32,128]{2,1,0:T(8,128)S(1)}, f32[13,32,128]{2,1,0:T(8,128)S(1)}, u32[]{:S(2)}, u32[]{:S(2)}) %collective-permute-start.2) | collective-permute-done | bytes 213024 | tf_op jit(solution)/shard_map/ppermute | solution.py:334
  35.3 0.9 %moves.1 = (f32[8,32,128]{2,1,0:T(8,128)S(1)}, f32[8,32,128]{2,1,0:T(8,128)S(1)}, f32[32,1024]{1,0:T(8,128)S(1)}) custom-call(s32[2]{0:T(128)S(4)} %get-tuple-element.19.accept_ref, f32[8,128]{1,0:T(8,128)S(1)} %get-tuple-element.23.root_ref, f32[2,8,32,128]{3,2,1,0:T(8,128)S(1)} %bitcast.14, f32[2,8,32,128]{3,2,1,0:T(8,128)S(1)} %get-tuple-element.25.noise_ref, ...), custom_call_target="tpu_custom_call" | custom-call | tf_op jit(solution)/shard_map/moves/pallas_call | solution.py:238
  36.3 15.6 %all_gather.3 = f32[128,1024]{1,0:T(8,128)S(1)} all-gather(f32[32,1024]{1,0:T(8,128)S(1)} %get-tuple-element.31), channel_id=1, replica_groups=mesh['pairs'=4,'member'=2,'tile'=4] {'tile'}, dimensions={0}, use_global_device_ids=true | all-gather | bytes 655360 | tf_op jit(solution)/shard_map/all_gather | solution.py:357
  51.9 0.4 fusion
  52.3 0.1 collective-permute-start.3
  52.4 0.4 fusion.2
  52.9 1.5 %collective-permute-done.3 = f32[4,32,1024]{2,1,0:T(8,128)S(1)} collective-permute-done((f32[4,32,1024]{2,1,0:T(8,128)S(1)}, f32[4,32,1024]{2,1,0:T(8,128)S(1)}, u32[]{:S(2)}, u32[]{:S(2)}) %collective-permute-start.3) | collective-permute-done | bytes 524320 | tf_op jit(solution)/shard_map/ppermute | solution.py:339
  54.3 0.1 add.19
  54.4 11.5 %all_to_all.22.parts_ref = f32[4,32,1024]{2,1,0:T(8,128)S(1)} all-to-all(f32[4,32,1024]{2,1,0:T(8,128)S(1)} %add.19), channel_id=1, replica_groups=mesh['pairs'=4,'member'=2,'tile'=4] {'pairs'}, dimensions={0} | all-to-all | bytes 1048576 | tf_op jit(solution)/shard_map/all_to_all | solution.py:372
  65.9 10.1 %all_to_all.23 = f32[4,32,1024]{2,1,0:T(8,128)S(1)} all-to-all(f32[4,32,1024]{2,1,0:T(8,128)S(1)} %sum_copies.1), channel_id=1, replica_groups=mesh['pairs'=4,'member'=2,'tile'=4] {'pairs'}, dimensions={0} | all-to-all | bytes 1048576 | tf_op jit(solution)/shard_map/all_to_all | solution.py:373
  76.0 0.0 collective-permute-start.4
  76.0 0.9 %store.1 = (f32[8,32,128]{2,1,0:T(8,128)}, f32[8,32,128]{2,1,0:T(8,128)}, f32[256,1024]{1,0:T(8,128)}) custom-call(f32[8,32,128]{2,1,0:T(8,128)S(1)} %get-tuple-element.29.cond_ref, f32[8,32,128]{2,1,0:T(8,128)S(1)} %get-tuple-element.30.pot_ref, f32[128,1024]{1,0:T(8,128)S(1)} %bitcast.15), custom_call_target="tpu_custom_call" | custom-call | tf_op jit(solution)/shard_map/store/pallas_call | solution.py:288
  76.9 1.0 %collective-permute-done.4 = f32[4,32,1024]{2,1,0:T(8,128)S(1)} collective-permute-done((f32[4,32,1024]{2,1,0:T(8,128)S(1)}, f32[4,32,1024]{2,1,0:T(8,128)S(1)}, u32[]{:S(2)}, u32[]{:S(2)}) %collective-permute-start.4) | collective-permute-done | bytes 524320 | tf_op jit(solution)/shard_map/ppermute | solution.py:339
  77.9 0.8 %store_other.1 = f32[256,1024]{1,0:T(8,128)} custom-call(f32[128,1024]{1,0:T(8,128)S(1)} %bitcast.16, f32[256,1024]{1,0:T(8,128)} %get-tuple-element.34.held_ref), custom_call_target="tpu_custom_call", output_to_operand_aliasing={{}: (1, {})} | custom-call | tf_op jit(solution)/shard_map/store_other/pallas_call | solution.py:318
  (3 shorter events, 0.1 us)
Async XLA Ops:
  13.8 1.6 %collective-permute-start = (f32[4,136,128]{2,1,0:T(8,128)S(1)}, f32[4,136,128]{2,1,0:T(8,128)S(1)}, u32[]{:S(2)}, u32[]{:S(2)}) collective-permute-start(f32[4,136,128]{2,1,0:T(8,128)S(1)} %all_to_all.20.mine_ref), channel_id=1, source_target_pairs={{0,4},{4,0},{1,5},{5,1},{2,6},{6,2},{3,7},{7,3},{8,12},{12,8},{9,1... | collective-permute-start | bytes 835592 | tf_op jit(solution)/shard_map/ppermute | solution.py:339
  24.1 7.1 %collective-permute-start.1 = (f32[13,32,128]{2,1,0:T(8,128)S(1)}, f32[13,32,128]{2,1,0:T(8,128)S(1)}, u32[]{:S(2)}, u32[]{:S(2)}) collective-permute-start(f32[13,32,128]{2,1,0:T(8,128)S(1)} %get-tuple-element.27), channel_id=1, source_target_pairs={{0,1},{1,2},{2,3},{4,5},{5,6},{6,7},{8,9},{9,10},{10,11},{12,13},{... | collective-permute-start | bytes 638984 | tf_op jit(solution)/shard_map/ppermute | solution.py:333
  27.6 7.7 %collective-permute-start.2 = (f32[13,32,128]{2,1,0:T(8,128)S(1)}, f32[13,32,128]{2,1,0:T(8,128)S(1)}, u32[]{:S(2)}, u32[]{:S(2)}) collective-permute-start(f32[13,32,128]{2,1,0:T(8,128)S(1)} %get-tuple-element.28), channel_id=1, source_target_pairs={{1,0},{2,1},{3,2},{5,4},{6,5},{7,6},{9,8},{10,9},{11,10},{13,12},{... | collective-permute-start | bytes 638984 | tf_op jit(solution)/shard_map/ppermute | solution.py:334
  52.3 2.0 %collective-permute-start.3 = (f32[4,32,1024]{2,1,0:T(8,128)S(1)}, f32[4,32,1024]{2,1,0:T(8,128)S(1)}, u32[]{:S(2)}, u32[]{:S(2)}) collective-permute-start(f32[4,32,1024]{2,1,0:T(8,128)S(1)} %bitcast.18), channel_id=1, source_target_pairs={{0,4},{4,0},{1,5},{5,1},{2,6},{6,2},{3,7},{7,3},{8,12},{12,8},{9,1... | collective-permute-start | bytes 1572872 | tf_op jit(solution)/shard_map/ppermute | solution.py:339
  76.0 1.9 %collective-permute-start.4 = (f32[4,32,1024]{2,1,0:T(8,128)S(1)}, f32[4,32,1024]{2,1,0:T(8,128)S(1)}, u32[]{:S(2)}, u32[]{:S(2)}) collective-permute-start(f32[4,32,1024]{2,1,0:T(8,128)S(1)} %all_to_all.23), channel_id=1, source_target_pairs={{0,4},{4,0},{1,5},{5,1},{2,6},{6,2},{3,7},{7,3},{8,12},{12,8},{9,1... | collective-permute-start | bytes 1572872 | tf_op jit(solution)/shard_map/ppermute | solution.py:339

commit v12 on v10

--- a/solution.py
+++ b/solution.py
@@ -240,21 +240,20 @@
     )(in_smem(accept), in_vmem(root), *[in_vmem(field) for field in fields])
 
 
-def sum_copies_kernel(parts_ref, copies_ref):
+def sum_parts_kernel(parts_ref, total_ref):
     total = parts_ref[0]
     for place in range(1, parts_ref.shape[0]):
         total += parts_ref[place]
-    for place in range(copies_ref.shape[0]):
-        copies_ref[place] = total
-
-
-def sum_copies(parts):
-    return pl.pallas_call(
-        sum_copies_kernel,
-        out_shape=pltpu.VMEM(parts.shape, jnp.float32),
+    total_ref[...] = total
+
+
+def sum_parts(parts):
+    return pl.pallas_call(
+        sum_parts_kernel,
+        out_shape=pltpu.VMEM(parts.shape[1:], jnp.float32),
         in_specs=[VMEM],
         out_specs=VMEM,
-        name="sum_copies",
+        name="sum_parts",
     )(in_vmem(parts))
 
 
@@ -352,7 +351,7 @@
 
     got = swap(product(1 - member))
     parts = lax.all_to_all(product(member) + got, "pairs", 0, 0, tiled=True)
-    mine = lax.all_to_all(sum_copies(parts), "pairs", 0, 0, tiled=True)
+    mine = lax.all_gather(sum_parts(parts), "pairs", axis=0, tiled=True)
     other = swap(mine).reshape(rows, -1)
     conduct, pot, held = store(conduct, pot, mine.reshape(rows, -1))
     moments = store_other(other, held)

time: 79 us -> 78.8 us (level)
    all_to_all x1 -> x0, blocking collectives: 10.1 us -> none  [local(): mine = lax.all_to_all(sum_copies(parts), 'pairs', 0, 0, tiled=True)]
    all_gather x0 -> x1, blocking collectives: none -> 10 us  [local(): mine = lax.all_gather(sum_parts(parts), 'pairs', axis=0, tiled=True)]
where the time goes in v12:
time: 78.8 us; the launch traced here: 78.6 us
  blocking collectives  57 us (72%)
  waiting for transfers between devices  10.4 us (13%)
  starting transfers between devices  4.86 us (6%)
  Pallas kernels  3.97 us (5%)
  between operations  1.38 us (2%)
  matrix products  0.85 us (1%)
    all_gather x1, blocking collectives, local(): piece = lax.all_gather(traces, 'tile', axis=0, tiled=True)  15.6 us
    all_to_all x1, blocking collectives, local(): parts = lax.all_to_all(product(member) + got, 'pairs', 0, 0, tiled=True)  11.5 us
    all_to_all x1, blocking collectives, local(): pieces = lax.all_to_all(pieces, 'pairs', 0, 0, tiled=True)  11.2 us
    all_gather x1, blocking collectives, local(): mine = lax.all_gather(sum_parts(parts), 'pairs', axis=0, tiled=True)  10 us
    all_to_all x1, blocking collectives, local(): lax.all_to_all(chosen, 'pairs', 0, 0, tiled=True).reshape(2, width, ny, nz)  8.68 us
    ppermute x1, waiting for transfers between devices, exchange_halo(): high = lax.ppermute(low_edge, 'tile', backward)  4.14 us
    ppermute x3, waiting for transfers between devices, swap(): return lax.ppermute(block, 'member', [(0, 1), (1, 0)])  4.01 us
    ppermute x1, starting transfers between devices, exchange_halo(): low = lax.ppermute(high_edge, 'tile', forward)  3.49 us
  transfers between devices with their start and end apart: 5, of which 5 were waited for; matrix products, arithmetic and copies ran while one was open for 1% of the time, Pallas kernels for 1%

profile of v12, /device:TPU:0, one launch (start us, length us, event | category | flops | bytes accessed | tf_op | source)
XLA Modules:
  0.0 78.6 jit_solution(4586808149862821623)
XLA Ops:
  1.3 1.2 %pack.1 = (f32[1]{0:T(128)S(4)}, s32[8]{0:T(128)S(4)}, s32[2]{0:T(128)S(4)}, f32[4,136,128]{2,1,0:T(8,128)S(1)}, f32[2,8,32,128]{3,2,1,0:T(8,128)S(1)}, /*index=5*/f32[8,32,128]{2,1,0:T(8,128)S(1)}) custom-call(f32[1]{0:T(128)S(6)} %copy.12.weight_ref, s32[8]{0:T(128)} %parents_ref.1, s32[2]{0:T(128)} %bitcast.18, f32[256,128]{1,0:T(8,128)} %bitcast.16, ...), custom_call_target="tpu_custom_call" | custom-call | tf_op jit(solution)/shard_map/pack/pallas_call | solution.py:55
  2.5 11.2 %all_to_all.15.mine_ref = f32[4,136,128]{2,1,0:T(8,128)S(1)} all-to-all(f32[4,136,128]{2,1,0:T(8,128)S(1)} %get-tuple-element.22), channel_id=1, replica_groups=mesh['pairs'=4,'member'=2,'tile'=4] {'pairs'}, dimensions={0} | all-to-all | bytes 557056 | tf_op jit(solution)/shard_map/all_to_all | solution.py:330
  13.7 0.0 collective-permute-start
  13.7 1.6 %collective-permute-done.other_ref = f32[4,136,128]{2,1,0:T(8,128)S(1)} collective-permute-done((f32[4,136,128]{2,1,0:T(8,128)S(1)}, f32[4,136,128]{2,1,0:T(8,128)S(1)}, u32[]{:S(2)}, u32[]{:S(2)}) %collective-permute-start) | collective-permute-done | bytes 278560 | tf_op jit(solution)/shard_map/ppermute | solution.py:320
  15.3 8.7 %all_to_all.16 = f32[4,128,128]{2,1,0:T(8,128)S(1)} all-to-all(f32[4,128,128]{2,1,0:T(8,128)S(1)} %get-tuple-element.24), channel_id=1, replica_groups=mesh['pairs'=4,'member'=2,'tile'=4] {'pairs'}, dimensions={0} | all-to-all | bytes 524288 | tf_op jit(solution)/shard_map/all_to_all | solution.py:332
  24.0 3.5 %collective-permute-start.1 = (f32[13,32,128]{2,1,0:T(8,128)S(1)}, f32[13,32,128]{2,1,0:T(8,128)S(1)}, u32[]{:S(2)}, u32[]{:S(2)}) collective-permute-start(f32[13,32,128]{2,1,0:T(8,128)S(1)} %get-tuple-element.27), channel_id=1, source_target_pairs={{0,1},{1,2},{2,3},{4,5},{5,6},{6,7},{8,9},{9,10},{10,11},{12,13},{... | collective-permute-start | bytes 638984 | tf_op jit(solution)/shard_map/ppermute | solution.py:314
  27.5 1.3 %collective-permute-start.2 = (f32[13,32,128]{2,1,0:T(8,128)S(1)}, f32[13,32,128]{2,1,0:T(8,128)S(1)}, u32[]{:S(2)}, u32[]{:S(2)}) collective-permute-start(f32[13,32,128]{2,1,0:T(8,128)S(1)} %get-tuple-element.28), channel_id=1, source_target_pairs={{1,0},{2,1},{3,2},{5,4},{6,5},{7,6},{9,8},{10,9},{11,10},{13,12},{... | collective-permute-start | bytes 638984 | tf_op jit(solution)/shard_map/ppermute | solution.py:315
  28.8 2.3 %collective-permute-done.1.low_ref = f32[13,32,128]{2,1,0:T(8,128)S(1)} collective-permute-done((f32[13,32,128]{2,1,0:T(8,128)S(1)}, f32[13,32,128]{2,1,0:T(8,128)S(1)}, u32[]{:S(2)}, u32[]{:S(2)}) %collective-permute-start.1) | collective-permute-done | bytes 213024 | tf_op jit(solution)/shard_map/ppermute | solution.py:314
  31.1 4.1 %collective-permute-done.2.high_ref = f32[13,32,128]{2,1,0:T(8,128)S(1)} collective-permute-done((f32[13,32,128]{2,1,0:T(8,128)S(1)}, f32[13,32,128]{2,1,0:T(8,128)S(1)}, u32[]{:S(2)}, u32[]{:S(2)}) %collective-permute-start.2) | collective-permute-done | bytes 213024 | tf_op jit(solution)/shard_map/ppermute | solution.py:315
  35.2 0.9 %moves.1 = (f32[8,32,128]{2,1,0:T(8,128)S(1)}, f32[8,32,128]{2,1,0:T(8,128)S(1)}, f32[32,1024]{1,0:T(8,128)S(1)}) custom-call(s32[2]{0:T(128)S(4)} %get-tuple-element.19.accept_ref, f32[8,128]{1,0:T(8,128)S(1)} %get-tuple-element.23.root_ref, f32[2,8,32,128]{3,2,1,0:T(8,128)S(1)} %bitcast.12, f32[2,8,32,128]{3,2,1,0:T(8,128)S(1)} %get-tuple-element.25.noise_ref, ...), custom_call_target="tpu_custom_call" | custom-call | tf_op jit(solution)/shard_map/moves/pallas_call | solution.py:228
  36.2 15.6 %all_gather.6 = f32[128,1024]{1,0:T(8,128)S(1)} all-gather(f32[32,1024]{1,0:T(8,128)S(1)} %get-tuple-element.31), channel_id=1, replica_groups=mesh['pairs'=4,'member'=2,'tile'=4] {'tile'}, dimensions={0}, use_global_device_ids=true | all-gather | bytes 655360 | tf_op jit(solution)/shard_map/all_gather | solution.py:338
  51.8 0.4 fusion
  52.2 0.1 collective-permute-start.3
  52.3 0.4 fusion.2
  52.8 1.5 %collective-permute-done.3 = f32[4,32,1024]{2,1,0:T(8,128)S(1)} collective-permute-done((f32[4,32,1024]{2,1,0:T(8,128)S(1)}, f32[4,32,1024]{2,1,0:T(8,128)S(1)}, u32[]{:S(2)}, u32[]{:S(2)}) %collective-permute-start.3) | collective-permute-done | bytes 524320 | tf_op jit(solution)/shard_map/ppermute | solution.py:320
  54.2 0.1 add.19
  54.3 11.5 %all_to_all.17.parts_ref = f32[4,32,1024]{2,1,0:T(8,128)S(1)} all-to-all(f32[4,32,1024]{2,1,0:T(8,128)S(1)} %add.19), channel_id=1, replica_groups=mesh['pairs'=4,'member'=2,'tile'=4] {'pairs'}, dimensions={0} | all-to-all | bytes 1048576 | tf_op jit(solution)/shard_map/all_to_all | solution.py:353
  65.8 10.0 %all_gather.7.half_ref = f32[128,1024]{1,0:T(8,128)S(1)} all-gather(f32[32,1024]{1,0:T(8,128)S(1)} %sum_parts.1), channel_id=1, replica_groups=mesh['pairs'=4,'member'=2,'tile'=4] {'pairs'}, dimensions={0}, use_global_device_ids=true | all-gather | bytes 655360 | tf_op jit(solution)/shard_map/all_gather | solution.py:354
  75.9 0.0 collective-permute-start.4
  75.9 0.9 %store.1 = (f32[8,32,128]{2,1,0:T(8,128)}, f32[8,32,128]{2,1,0:T(8,128)}, f32[256,1024]{1,0:T(8,128)}) custom-call(f32[8,32,128]{2,1,0:T(8,128)S(1)} %get-tuple-element.29.cond_ref, f32[8,32,128]{2,1,0:T(8,128)S(1)} %get-tuple-element.30.pot_ref, f32[128,1024]{1,0:T(8,128)S(1)} %all_gather.7.half_ref), custom_call_target="tpu_custom_call" | custom-call | tf_op jit(solution)/shard_map/store/pallas_call | solution.py:277
  76.8 1.0 %collective-permute-done.4.half_ref = f32[128,1024]{1,0:T(8,128)S(1)} collective-permute-done((f32[128,1024]{1,0:T(8,128)S(1)}, f32[128,1024]{1,0:T(8,128)S(1)}, u32[]{:S(2)}, u32[]{:S(2)}) %collective-permute-start.4) | collective-permute-done | bytes 524320 | tf_op jit(solution)/shard_map/ppermute | solution.py:320
  77.8 0.8 %store_other.1 = f32[256,1024]{1,0:T(8,128)} custom-call(f32[128,1024]{1,0:T(8,128)S(1)} %collective-permute-done.4.half_ref, f32[256,1024]{1,0:T(8,128)} %get-tuple-element.34.held_ref), custom_call_target="tpu_custom_call", output_to_operand_aliasing={{}: (1, {})} | custom-call | tf_op jit(solution)/shard_map/store_other/pallas_call | solution.py:299
  (3 shorter events, 0.1 us)
Async XLA Ops:
  13.7 1.6 %collective-permute-start = (f32[4,136,128]{2,1,0:T(8,128)S(1)}, f32[4,136,128]{2,1,0:T(8,128)S(1)}, u32[]{:S(2)}, u32[]{:S(2)}) collective-permute-start(f32[4,136,128]{2,1,0:T(8,128)S(1)} %all_to_all.15.mine_ref), channel_id=1, source_target_pairs={{0,4},{4,0},{1,5},{5,1},{2,6},{6,2},{3,7},{7,3},{8,12},{12,8},{9,1... | collective-permute-start | bytes 835592 | tf_op jit(solution)/shard_map/ppermute | solution.py:320
  24.0 7.1 %collective-permute-start.1 = (f32[13,32,128]{2,1,0:T(8,128)S(1)}, f32[13,32,128]{2,1,0:T(8,128)S(1)}, u32[]{:S(2)}, u32[]{:S(2)}) collective-permute-start(f32[13,32,128]{2,1,0:T(8,128)S(1)} %get-tuple-element.27), channel_id=1, source_target_pairs={{0,1},{1,2},{2,3},{4,5},{5,6},{6,7},{8,9},{9,10},{10,11},{12,13},{... | collective-permute-start | bytes 638984 | tf_op jit(solution)/shard_map/ppermute | solution.py:314
  27.5 7.7 %collective-permute-start.2 = (f32[13,32,128]{2,1,0:T(8,128)S(1)}, f32[13,32,128]{2,1,0:T(8,128)S(1)}, u32[]{:S(2)}, u32[]{:S(2)}) collective-permute-start(f32[13,32,128]{2,1,0:T(8,128)S(1)} %get-tuple-element.28), channel_id=1, source_target_pairs={{1,0},{2,1},{3,2},{5,4},{6,5},{7,6},{9,8},{10,9},{11,10},{13,12},{... | collective-permute-start | bytes 638984 | tf_op jit(solution)/shard_map/ppermute | solution.py:315
  52.2 2.0 %collective-permute-start.3 = (f32[4,32,1024]{2,1,0:T(8,128)S(1)}, f32[4,32,1024]{2,1,0:T(8,128)S(1)}, u32[]{:S(2)}, u32[]{:S(2)}) collective-permute-start(f32[4,32,1024]{2,1,0:T(8,128)S(1)} %bitcast.14), channel_id=1, source_target_pairs={{0,4},{4,0},{1,5},{5,1},{2,6},{6,2},{3,7},{7,3},{8,12},{12,8},{9,1... | collective-permute-start | bytes 1572872 | tf_op jit(solution)/shard_map/ppermute | solution.py:320
  75.9 1.9 %collective-permute-start.4 = (f32[128,1024]{1,0:T(8,128)S(1)}, f32[128,1024]{1,0:T(8,128)S(1)}, u32[]{:S(2)}, u32[]{:S(2)}) collective-permute-start(f32[128,1024]{1,0:T(8,128)S(1)} %all_gather.7.half_ref), channel_id=1, source_target_pairs={{0,4},{4,0},{1,5},{5,1},{2,6},{6,2},{3,7},{7,3},{8,12},{12,8},{9,1... | collective-permute-start | bytes 1572872 | tf_op jit(solution)/shard_map/ppermute | solution.py:320

commit v13 on v12

--- a/solution.py
+++ b/solution.py
@@ -288,23 +288,23 @@
     )(in_vmem(conduct), in_vmem(pot), in_vmem(half))
 
 
-def store_other_kernel(half_ref, held_ref, rows_out, sem):
-    other = own_rows(rows_out, half_ref.shape[0], 1 - lax.axis_index("member"))
-    copy = pltpu.make_async_copy(half_ref, other, sem)
+def store_other_kernel(at, part_ref, held_ref, rows_out, sem):
+    other = own_rows(rows_out, rows_out.shape[0] // pair, 1 - lax.axis_index("member"))
+    copy = pltpu.make_async_copy(part_ref, other.at[pl.ds(at, part_ref.shape[0])], sem)
     copy.start()
     copy.wait()
 
 
-def store_other(half, held):
-    return pl.pallas_call(
-        store_other_kernel,
+def store_other(part, held, at):
+    return pl.pallas_call(
+        functools.partial(store_other_kernel, at),
         out_shape=jax.ShapeDtypeStruct(held.shape, jnp.float32),
         in_specs=[VMEM, ANY],
         out_specs=ANY,
         scratch_shapes=[pltpu.SemaphoreType.DMA],
         input_output_aliases={1: 0},
         name="store_other",
-    )(in_vmem(half), held)
+    )(in_vmem(part), held)
 
 
 def exchange_halo(low_edge, high_edge):
@@ -352,9 +352,11 @@
     got = swap(product(1 - member))
     parts = lax.all_to_all(product(member) + got, "pairs", 0, 0, tiled=True)
     mine = lax.all_gather(sum_parts(parts), "pairs", axis=0, tiled=True)
-    other = swap(mine).reshape(rows, -1)
-    conduct, pot, held = store(conduct, pot, mine.reshape(rows, -1))
-    moments = store_other(other, held)
+    half = rows // 2
+    others = [swap(mine.reshape(rows, -1)[at:at + half]) for at in (0, half)]
+    conduct, pot, moments = store(conduct, pot, mine.reshape(rows, -1))
+    for at, other in zip((0, half), others):
+        moments = store_other(other, moments, at)
     return (conduct[None], pot[None], moments)
 
 

time: 78.8 us -> 79.2 us (level)
  waiting for transfers between devices: 10.4 us -> 9.56 us
    ppermute x3 -> x4, waiting for transfers between devices: 4.01 us -> 3.13 us  [swap(): return lax.ppermute(block, 'member', [(0, 1), (1, 0)])]
  transfers between devices with their start and end apart: 5 -> 6, of which waited for: 5 -> 5; matrix products, arithmetic and copies ran while one was open for 1% -> 1% of each run, Pallas kernels for 1% -> 2%
where the time goes in v13:
time: 79.2 us; the launch traced here: 79 us
  blocking collectives  57 us (72%)
  waiting for transfers between devices  9.56 us (12%)
  starting transfers between devices  5.43 us (7%)
  Pallas kernels  4.6 us (6%)
  between operations  1.41 us (2%)
  matrix products  0.85 us (1%)
    all_gather x1, blocking collectives, local(): piece = lax.all_gather(traces, 'tile', axis=0, tiled=True)  15.6 us
    all_to_all x1, blocking collectives, local(): parts = lax.all_to_all(product(member) + got, 'pairs', 0, 0, tiled=True)  11.5 us
    all_to_all x1, blocking collectives, local(): pieces = lax.all_to_all(pieces, 'pairs', 0, 0, tiled=True)  11.2 us
    all_gather x1, blocking collectives, local(): mine = lax.all_gather(sum_parts(parts), 'pairs', axis=0, tiled=True)  10 us
    all_to_all x1, blocking collectives, local(): lax.all_to_all(chosen, 'pairs', 0, 0, tiled=True).reshape(2, width, ny, nz)  8.68 us
    ppermute x1, waiting for transfers between devices, exchange_halo(): high = lax.ppermute(low_edge, 'tile', backward)  4.14 us
    ppermute x1, starting transfers between devices, exchange_halo(): low = lax.ppermute(high_edge, 'tile', forward)  3.49 us
    ppermute x4, waiting for transfers between devices, swap(): return lax.ppermute(block, 'member', [(0, 1), (1, 0)])  3.13 us
  transfers between devices with their start and end apart: 6, of which 5 were waited for; matrix products, arithmetic and copies ran while one was open for 1% of the time, Pallas kernels for 2%

profile of v13, /device:TPU:0, one launch (start us, length us, event | category | flops | bytes accessed | tf_op | source)
XLA Modules:
  0.0 79.0 jit_solution(2519752123064761350)
XLA Ops:
  1.3 1.2 %pack.1 = (f32[1]{0:T(128)S(4)}, s32[8]{0:T(128)S(4)}, s32[2]{0:T(128)S(4)}, f32[4,136,128]{2,1,0:T(8,128)S(1)}, f32[2,8,32,128]{3,2,1,0:T(8,128)S(1)}, /*index=5*/f32[8,32,128]{2,1,0:T(8,128)S(1)}) custom-call(f32[1]{0:T(128)S(6)} %copy.14.weight_ref, s32[8]{0:T(128)} %parents_ref.1, s32[2]{0:T(128)} %bitcast.18, f32[256,128]{1,0:T(8,128)} %bitcast.16, ...), custom_call_target="tpu_custom_call" | custom-call | tf_op jit(solution)/shard_map/pack/pallas_call | solution.py:55
  2.5 11.2 %all_to_all.15.mine_ref = f32[4,136,128]{2,1,0:T(8,128)S(1)} all-to-all(f32[4,136,128]{2,1,0:T(8,128)S(1)} %get-tuple-element.22), channel_id=1, replica_groups=mesh['pairs'=4,'member'=2,'tile'=4] {'pairs'}, dimensions={0} | all-to-all | bytes 557056 | tf_op jit(solution)/shard_map/all_to_all | solution.py:330
  13.7 1.6 %collective-permute-done.other_ref = f32[4,136,128]{2,1,0:T(8,128)S(1)} collective-permute-done((f32[4,136,128]{2,1,0:T(8,128)S(1)}, f32[4,136,128]{2,1,0:T(8,128)S(1)}, u32[]{:S(2)}, u32[]{:S(2)}) %collective-permute-start) | collective-permute-done | bytes 278560 | tf_op jit(solution)/shard_map/ppermute | solution.py:320
  15.3 8.7 %all_to_all.16 = f32[4,128,128]{2,1,0:T(8,128)S(1)} all-to-all(f32[4,128,128]{2,1,0:T(8,128)S(1)} %get-tuple-element.24), channel_id=1, replica_groups=mesh['pairs'=4,'member'=2,'tile'=4] {'pairs'}, dimensions={0} | all-to-all | bytes 524288 | tf_op jit(solution)/shard_map/all_to_all | solution.py:332
  24.0 3.5 %collective-permute-start.1 = (f32[13,32,128]{2,1,0:T(8,128)S(1)}, f32[13,32,128]{2,1,0:T(8,128)S(1)}, u32[]{:S(2)}, u32[]{:S(2)}) collective-permute-start(f32[13,32,128]{2,1,0:T(8,128)S(1)} %get-tuple-element.27), channel_id=1, source_target_pairs={{0,1},{1,2},{2,3},{4,5},{5,6},{6,7},{8,9},{9,10},{10,11},{12,13},{... | collective-permute-start | bytes 638984 | tf_op jit(solution)/shard_map/ppermute | solution.py:314
  27.5 1.3 %collective-permute-start.2 = (f32[13,32,128]{2,1,0:T(8,128)S(1)}, f32[13,32,128]{2,1,0:T(8,128)S(1)}, u32[]{:S(2)}, u32[]{:S(2)}) collective-permute-start(f32[13,32,128]{2,1,0:T(8,128)S(1)} %get-tuple-element.28), channel_id=1, source_target_pairs={{1,0},{2,1},{3,2},{5,4},{6,5},{7,6},{9,8},{10,9},{11,10},{13,12},{... | collective-permute-start | bytes 638984 | tf_op jit(solution)/shard_map/ppermute | solution.py:315
  28.8 2.3 %collective-permute-done.1.low_ref = f32[13,32,128]{2,1,0:T(8,128)S(1)} collective-permute-done((f32[13,32,128]{2,1,0:T(8,128)S(1)}, f32[13,32,128]{2,1,0:T(8,128)S(1)}, u32[]{:S(2)}, u32[]{:S(2)}) %collective-permute-start.1) | collective-permute-done | bytes 213024 | tf_op jit(solution)/shard_map/ppermute | solution.py:314
  31.1 4.1 %collective-permute-done.2.high_ref = f32[13,32,128]{2,1,0:T(8,128)S(1)} collective-permute-done((f32[13,32,128]{2,1,0:T(8,128)S(1)}, f32[13,32,128]{2,1,0:T(8,128)S(1)}, u32[]{:S(2)}, u32[]{:S(2)}) %collective-permute-start.2) | collective-permute-done | bytes 213024 | tf_op jit(solution)/shard_map/ppermute | solution.py:315
  35.2 0.9 %moves.1 = (f32[8,32,128]{2,1,0:T(8,128)S(1)}, f32[8,32,128]{2,1,0:T(8,128)S(1)}, f32[32,1024]{1,0:T(8,128)S(1)}) custom-call(s32[2]{0:T(128)S(4)} %get-tuple-element.19.accept_ref, f32[8,128]{1,0:T(8,128)S(1)} %get-tuple-element.23.root_ref, f32[2,8,32,128]{3,2,1,0:T(8,128)S(1)} %bitcast.12, f32[2,8,32,128]{3,2,1,0:T(8,128)S(1)} %get-tuple-element.25.noise_ref, ...), custom_call_target="tpu_custom_call" | custom-call | tf_op jit(solution)/shard_map/moves/pallas_call | solution.py:228
  36.2 15.6 %all_gather.6 = f32[128,1024]{1,0:T(8,128)S(1)} all-gather(f32[32,1024]{1,0:T(8,128)S(1)} %get-tuple-element.31), channel_id=1, replica_groups=mesh['pairs'=4,'member'=2,'tile'=4] {'tile'}, dimensions={0}, use_global_device_ids=true | all-gather | bytes 655360 | tf_op jit(solution)/shard_map/all_gather | solution.py:338
  51.8 0.4 fusion
  52.2 0.1 collective-permute-start.3
  52.3 0.4 fusion.2
  52.8 1.5 %collective-permute-done.3 = f32[4,32,1024]{2,1,0:T(8,128)S(1)} collective-permute-done((f32[4,32,1024]{2,1,0:T(8,128)S(1)}, f32[4,32,1024]{2,1,0:T(8,128)S(1)}, u32[]{:S(2)}, u32[]{:S(2)}) %collective-permute-start.3) | collective-permute-done | bytes 524320 | tf_op jit(solution)/shard_map/ppermute | solution.py:320
  54.2 0.1 add.19
  54.3 11.5 %all_to_all.17.parts_ref = f32[4,32,1024]{2,1,0:T(8,128)S(1)} all-to-all(f32[4,32,1024]{2,1,0:T(8,128)S(1)} %add.19), channel_id=1, replica_groups=mesh['pairs'=4,'member'=2,'tile'=4] {'pairs'}, dimensions={0} | all-to-all | bytes 1048576 | tf_op jit(solution)/shard_map/all_to_all | solution.py:353
  65.8 10.0 %all_gather.7.half_ref = f32[128,1024]{1,0:T(8,128)S(1)} all-gather(f32[32,1024]{1,0:T(8,128)S(1)} %sum_parts.1), channel_id=1, replica_groups=mesh['pairs'=4,'member'=2,'tile'=4] {'pairs'}, dimensions={0}, use_global_device_ids=true | all-gather | bytes 655360 | tf_op jit(solution)/shard_map/all_gather | solution.py:354
  75.9 0.1 collective-permute-start.5
  76.0 0.5 collective-permute-start.4
  76.5 0.9 %store.1 = (f32[8,32,128]{2,1,0:T(8,128)}, f32[8,32,128]{2,1,0:T(8,128)}, f32[256,1024]{1,0:T(8,128)}) custom-call(f32[8,32,128]{2,1,0:T(8,128)S(1)} %get-tuple-element.29.cond_ref, f32[8,32,128]{2,1,0:T(8,128)S(1)} %get-tuple-element.30.pot_ref, f32[128,1024]{1,0:T(8,128)S(1)} %all_gather.7.half_ref), custom_call_target="tpu_custom_call" | custom-call | tf_op jit(solution)/shard_map/store/pallas_call | solution.py:277
  77.4 0.1 collective-permute-done.5.part_ref
  77.5 0.7 store_other.2.held_ref
  78.2 0.0 collective-permute-done.4.part_ref
  78.3 0.7 store_other.3
  (5 shorter events, 0.2 us)
Async XLA Ops:
  13.7 1.6 %collective-permute-start = (f32[4,136,128]{2,1,0:T(8,128)S(1)}, f32[4,136,128]{2,1,0:T(8,128)S(1)}, u32[]{:S(2)}, u32[]{:S(2)}) collective-permute-start(f32[4,136,128]{2,1,0:T(8,128)S(1)} %all_to_all.15.mine_ref), channel_id=1, source_target_pairs={{0,4},{4,0},{1,5},{5,1},{2,6},{6,2},{3,7},{7,3},{8,12},{12,8},{9,1... | collective-permute-start | bytes 835592 | tf_op jit(solution)/shard_map/ppermute | solution.py:320
  24.0 7.1 %collective-permute-start.1 = (f32[13,32,128]{2,1,0:T(8,128)S(1)}, f32[13,32,128]{2,1,0:T(8,128)S(1)}, u32[]{:S(2)}, u32[]{:S(2)}) collective-permute-start(f32[13,32,128]{2,1,0:T(8,128)S(1)} %get-tuple-element.27), channel_id=1, source_target_pairs={{0,1},{1,2},{2,3},{4,5},{5,6},{6,7},{8,9},{9,10},{10,11},{12,13},{... | collective-permute-start | bytes 638984 | tf_op jit(solution)/shard_map/ppermute | solution.py:314
  27.5 7.7 %collective-permute-start.2 = (f32[13,32,128]{2,1,0:T(8,128)S(1)}, f32[13,32,128]{2,1,0:T(8,128)S(1)}, u32[]{:S(2)}, u32[]{:S(2)}) collective-permute-start(f32[13,32,128]{2,1,0:T(8,128)S(1)} %get-tuple-element.28), channel_id=1, source_target_pairs={{1,0},{2,1},{3,2},{5,4},{6,5},{7,6},{9,8},{10,9},{11,10},{13,12},{... | collective-permute-start | bytes 638984 | tf_op jit(solution)/shard_map/ppermute | solution.py:315
  52.2 2.0 %collective-permute-start.3 = (f32[4,32,1024]{2,1,0:T(8,128)S(1)}, f32[4,32,1024]{2,1,0:T(8,128)S(1)}, u32[]{:S(2)}, u32[]{:S(2)}) collective-permute-start(f32[4,32,1024]{2,1,0:T(8,128)S(1)} %bitcast.14), channel_id=1, source_target_pairs={{0,4},{4,0},{1,5},{5,1},{2,6},{6,2},{3,7},{7,3},{8,12},{12,8},{9,1... | collective-permute-start | bytes 1572872 | tf_op jit(solution)/shard_map/ppermute | solution.py:320
  75.9 1.6 %collective-permute-start.5 = (f32[64,1024]{1,0:T(8,128)S(1)}, f32[64,1024]{1,0:T(8,128)S(1)}, u32[]{:S(2)}, u32[]{:S(2)}) collective-permute-start(f32[64,1024]{1,0:T(8,128)S(1)} %get-tuple-element.35), channel_id=1, source_target_pairs={{0,4},{4,0},{1,5},{5,1},{2,6},{6,2},{3,7},{7,3},{8,12},{12,8},{9,1... | collective-permute-start | bytes 786440 | tf_op jit(solution)/shard_map/ppermute | solution.py:320
  76.0 2.2 %collective-permute-start.4 = (f32[64,1024]{1,0:T(8,128)S(1)}, f32[64,1024]{1,0:T(8,128)S(1)}, u32[]{:S(2)}, u32[]{:S(2)}) collective-permute-start(f32[64,1024]{1,0:T(8,128)S(1)} %get-tuple-element.36), channel_id=1, source_target_pairs={{0,4},{4,0},{1,5},{5,1},{2,6},{6,2},{3,7},{7,3},{8,12},{12,8},{9,1... | collective-permute-start | bytes 786440 | tf_op jit(solution)/shard_map/ppermute | solution.py:320

commit v14 on v12

--- a/solution.py
+++ b/solution.py
@@ -311,8 +311,8 @@
     count = lax.axis_size("tile")
     forward = [(i, i + 1) for i in range(count - 1)]
     backward = [(target, source) for source, target in forward]
+    high = lax.ppermute(low_edge, "tile", backward)
     low = lax.ppermute(high_edge, "tile", forward)
-    high = lax.ppermute(low_edge, "tile", backward)
     return low, high
 
 

time: 78.8 us -> 78.9 us (level)
  no operation moved by 1% of the time
where the time goes in v14:
time: 78.9 us; the launch traced here: 78.6 us
  blocking collectives  57 us (72%)
  waiting for transfers between devices  10.4 us (13%)
  starting transfers between devices  4.86 us (6%)
  Pallas kernels  3.97 us (5%)
  between operations  1.38 us (2%)
  matrix products  0.85 us (1%)
    all_gather x1, blocking collectives, local(): piece = lax.all_gather(traces, 'tile', axis=0, tiled=True)  15.6 us
    all_to_all x1, blocking collectives, local(): parts = lax.all_to_all(product(member) + got, 'pairs', 0, 0, tiled=True)  11.5 us
    all_to_all x1, blocking collectives, local(): pieces = lax.all_to_all(pieces, 'pairs', 0, 0, tiled=True)  11.2 us
    all_gather x1, blocking collectives, local(): mine = lax.all_gather(sum_parts(parts), 'pairs', axis=0, tiled=True)  10 us
    all_to_all x1, blocking collectives, local(): lax.all_to_all(chosen, 'pairs', 0, 0, tiled=True).reshape(2, width, ny, nz)  8.68 us
    ppermute x1, waiting for transfers between devices, exchange_halo(): high = lax.ppermute(low_edge, 'tile', backward)  4.14 us
    ppermute x3, waiting for transfers between devices, swap(): return lax.ppermute(block, 'member', [(0, 1), (1, 0)])  4.01 us
    ppermute x1, starting transfers between devices, exchange_halo(): low = lax.ppermute(high_edge, 'tile', forward)  3.49 us
  transfers between devices with their start and end apart: 5, of which 5 were waited for; matrix products, arithmetic and copies ran while one was open for 1% of the time, Pallas kernels for 1%

profile of v14, /device:TPU:0, one launch (start us, length us, event | category | flops | bytes accessed | tf_op | source)
XLA Modules:
  0.0 78.6 jit_solution(4586808149862821623)
XLA Ops:
  1.3 1.2 %pack.1 = (f32[1]{0:T(128)S(4)}, s32[8]{0:T(128)S(4)}, s32[2]{0:T(128)S(4)}, f32[4,136,128]{2,1,0:T(8,128)S(1)}, f32[2,8,32,128]{3,2,1,0:T(8,128)S(1)}, /*index=5*/f32[8,32,128]{2,1,0:T(8,128)S(1)}) custom-call(f32[1]{0:T(128)S(6)} %copy.12.weight_ref, s32[8]{0:T(128)} %parents_ref.1, s32[2]{0:T(128)} %bitcast.18, f32[256,128]{1,0:T(8,128)} %bitcast.16, ...), custom_call_target="tpu_custom_call" | custom-call | tf_op jit(solution)/shard_map/pack/pallas_call | solution.py:55
  2.5 11.2 %all_to_all.15.mine_ref = f32[4,136,128]{2,1,0:T(8,128)S(1)} all-to-all(f32[4,136,128]{2,1,0:T(8,128)S(1)} %get-tuple-element.22), channel_id=1, replica_groups=mesh['pairs'=4,'member'=2,'tile'=4] {'pairs'}, dimensions={0} | all-to-all | bytes 557056 | tf_op jit(solution)/shard_map/all_to_all | solution.py:330
  13.7 0.0 collective-permute-start
  13.7 1.6 %collective-permute-done.other_ref = f32[4,136,128]{2,1,0:T(8,128)S(1)} collective-permute-done((f32[4,136,128]{2,1,0:T(8,128)S(1)}, f32[4,136,128]{2,1,0:T(8,128)S(1)}, u32[]{:S(2)}, u32[]{:S(2)}) %collective-permute-start) | collective-permute-done | bytes 278560 | tf_op jit(solution)/shard_map/ppermute | solution.py:320
  15.3 8.7 %all_to_all.16 = f32[4,128,128]{2,1,0:T(8,128)S(1)} all-to-all(f32[4,128,128]{2,1,0:T(8,128)S(1)} %get-tuple-element.24), channel_id=1, replica_groups=mesh['pairs'=4,'member'=2,'tile'=4] {'pairs'}, dimensions={0} | all-to-all | bytes 524288 | tf_op jit(solution)/shard_map/all_to_all | solution.py:332
  24.0 3.5 %collective-permute-start.1 = (f32[13,32,128]{2,1,0:T(8,128)S(1)}, f32[13,32,128]{2,1,0:T(8,128)S(1)}, u32[]{:S(2)}, u32[]{:S(2)}) collective-permute-start(f32[13,32,128]{2,1,0:T(8,128)S(1)} %get-tuple-element.27), channel_id=1, source_target_pairs={{0,1},{1,2},{2,3},{4,5},{5,6},{6,7},{8,9},{9,10},{10,11},{12,13},{... | collective-permute-start | bytes 638984 | tf_op jit(solution)/shard_map/ppermute | solution.py:315
  27.5 1.3 %collective-permute-start.2 = (f32[13,32,128]{2,1,0:T(8,128)S(1)}, f32[13,32,128]{2,1,0:T(8,128)S(1)}, u32[]{:S(2)}, u32[]{:S(2)}) collective-permute-start(f32[13,32,128]{2,1,0:T(8,128)S(1)} %get-tuple-element.28), channel_id=1, source_target_pairs={{1,0},{2,1},{3,2},{5,4},{6,5},{7,6},{9,8},{10,9},{11,10},{13,12},{... | collective-permute-start | bytes 638984 | tf_op jit(solution)/shard_map/ppermute | solution.py:314
  28.8 2.3 %collective-permute-done.1.low_ref = f32[13,32,128]{2,1,0:T(8,128)S(1)} collective-permute-done((f32[13,32,128]{2,1,0:T(8,128)S(1)}, f32[13,32,128]{2,1,0:T(8,128)S(1)}, u32[]{:S(2)}, u32[]{:S(2)}) %collective-permute-start.1) | collective-permute-done | bytes 213024 | tf_op jit(solution)/shard_map/ppermute | solution.py:315
  31.1 4.1 %collective-permute-done.2.high_ref = f32[13,32,128]{2,1,0:T(8,128)S(1)} collective-permute-done((f32[13,32,128]{2,1,0:T(8,128)S(1)}, f32[13,32,128]{2,1,0:T(8,128)S(1)}, u32[]{:S(2)}, u32[]{:S(2)}) %collective-permute-start.2) | collective-permute-done | bytes 213024 | tf_op jit(solution)/shard_map/ppermute | solution.py:314
  35.2 0.9 %moves.1 = (f32[8,32,128]{2,1,0:T(8,128)S(1)}, f32[8,32,128]{2,1,0:T(8,128)S(1)}, f32[32,1024]{1,0:T(8,128)S(1)}) custom-call(s32[2]{0:T(128)S(4)} %get-tuple-element.19.accept_ref, f32[8,128]{1,0:T(8,128)S(1)} %get-tuple-element.23.root_ref, f32[2,8,32,128]{3,2,1,0:T(8,128)S(1)} %bitcast.12, f32[2,8,32,128]{3,2,1,0:T(8,128)S(1)} %get-tuple-element.25.noise_ref, ...), custom_call_target="tpu_custom_call" | custom-call | tf_op jit(solution)/shard_map/moves/pallas_call | solution.py:228
  36.2 15.6 %all_gather.6 = f32[128,1024]{1,0:T(8,128)S(1)} all-gather(f32[32,1024]{1,0:T(8,128)S(1)} %get-tuple-element.31), channel_id=1, replica_groups=mesh['pairs'=4,'member'=2,'tile'=4] {'tile'}, dimensions={0}, use_global_device_ids=true | all-gather | bytes 655360 | tf_op jit(solution)/shard_map/all_gather | solution.py:338
  51.8 0.4 fusion
  52.2 0.1 collective-permute-start.3
  52.3 0.4 fusion.2
  52.8 1.5 %collective-permute-done.3 = f32[4,32,1024]{2,1,0:T(8,128)S(1)} collective-permute-done((f32[4,32,1024]{2,1,0:T(8,128)S(1)}, f32[4,32,1024]{2,1,0:T(8,128)S(1)}, u32[]{:S(2)}, u32[]{:S(2)}) %collective-permute-start.3) | collective-permute-done | bytes 524320 | tf_op jit(solution)/shard_map/ppermute | solution.py:320
  54.2 0.1 add.19
  54.3 11.5 %all_to_all.17.parts_ref = f32[4,32,1024]{2,1,0:T(8,128)S(1)} all-to-all(f32[4,32,1024]{2,1,0:T(8,128)S(1)} %add.19), channel_id=1, replica_groups=mesh['pairs'=4,'member'=2,'tile'=4] {'pairs'}, dimensions={0} | all-to-all | bytes 1048576 | tf_op jit(solution)/shard_map/all_to_all | solution.py:353
  65.8 10.0 %all_gather.7.half_ref = f32[128,1024]{1,0:T(8,128)S(1)} all-gather(f32[32,1024]{1,0:T(8,128)S(1)} %sum_parts.1), channel_id=1, replica_groups=mesh['pairs'=4,'member'=2,'tile'=4] {'pairs'}, dimensions={0}, use_global_device_ids=true | all-gather | bytes 655360 | tf_op jit(solution)/shard_map/all_gather | solution.py:354
  75.9 0.0 collective-permute-start.4
  75.9 0.9 %store.1 = (f32[8,32,128]{2,1,0:T(8,128)}, f32[8,32,128]{2,1,0:T(8,128)}, f32[256,1024]{1,0:T(8,128)}) custom-call(f32[8,32,128]{2,1,0:T(8,128)S(1)} %get-tuple-element.29.cond_ref, f32[8,32,128]{2,1,0:T(8,128)S(1)} %get-tuple-element.30.pot_ref, f32[128,1024]{1,0:T(8,128)S(1)} %all_gather.7.half_ref), custom_call_target="tpu_custom_call" | custom-call | tf_op jit(solution)/shard_map/store/pallas_call | solution.py:277
  76.8 1.0 %collective-permute-done.4.half_ref = f32[128,1024]{1,0:T(8,128)S(1)} collective-permute-done((f32[128,1024]{1,0:T(8,128)S(1)}, f32[128,1024]{1,0:T(8,128)S(1)}, u32[]{:S(2)}, u32[]{:S(2)}) %collective-permute-start.4) | collective-permute-done | bytes 524320 | tf_op jit(solution)/shard_map/ppermute | solution.py:320
  77.8 0.8 %store_other.1 = f32[256,1024]{1,0:T(8,128)} custom-call(f32[128,1024]{1,0:T(8,128)S(1)} %collective-permute-done.4.half_ref, f32[256,1024]{1,0:T(8,128)} %get-tuple-element.34.held_ref), custom_call_target="tpu_custom_call", output_to_operand_aliasing={{}: (1, {})} | custom-call | tf_op jit(solution)/shard_map/store_other/pallas_call | solution.py:299
  (3 shorter events, 0.1 us)
Async XLA Ops:
  13.7 1.6 %collective-permute-start = (f32[4,136,128]{2,1,0:T(8,128)S(1)}, f32[4,136,128]{2,1,0:T(8,128)S(1)}, u32[]{:S(2)}, u32[]{:S(2)}) collective-permute-start(f32[4,136,128]{2,1,0:T(8,128)S(1)} %all_to_all.15.mine_ref), channel_id=1, source_target_pairs={{0,4},{4,0},{1,5},{5,1},{2,6},{6,2},{3,7},{7,3},{8,12},{12,8},{9,1... | collective-permute-start | bytes 835592 | tf_op jit(solution)/shard_map/ppermute | solution.py:320
  24.0 7.1 %collective-permute-start.1 = (f32[13,32,128]{2,1,0:T(8,128)S(1)}, f32[13,32,128]{2,1,0:T(8,128)S(1)}, u32[]{:S(2)}, u32[]{:S(2)}) collective-permute-start(f32[13,32,128]{2,1,0:T(8,128)S(1)} %get-tuple-element.27), channel_id=1, source_target_pairs={{0,1},{1,2},{2,3},{4,5},{5,6},{6,7},{8,9},{9,10},{10,11},{12,13},{... | collective-permute-start | bytes 638984 | tf_op jit(solution)/shard_map/ppermute | solution.py:315
  27.5 7.7 %collective-permute-start.2 = (f32[13,32,128]{2,1,0:T(8,128)S(1)}, f32[13,32,128]{2,1,0:T(8,128)S(1)}, u32[]{:S(2)}, u32[]{:S(2)}) collective-permute-start(f32[13,32,128]{2,1,0:T(8,128)S(1)} %get-tuple-element.28), channel_id=1, source_target_pairs={{1,0},{2,1},{3,2},{5,4},{6,5},{7,6},{9,8},{10,9},{11,10},{13,12},{... | collective-permute-start | bytes 638984 | tf_op jit(solution)/shard_map/ppermute | solution.py:314
  52.2 2.0 %collective-permute-start.3 = (f32[4,32,1024]{2,1,0:T(8,128)S(1)}, f32[4,32,1024]{2,1,0:T(8,128)S(1)}, u32[]{:S(2)}, u32[]{:S(2)}) collective-permute-start(f32[4,32,1024]{2,1,0:T(8,128)S(1)} %bitcast.14), channel_id=1, source_target_pairs={{0,4},{4,0},{1,5},{5,1},{2,6},{6,2},{3,7},{7,3},{8,12},{12,8},{9,1... | collective-permute-start | bytes 1572872 | tf_op jit(solution)/shard_map/ppermute | solution.py:320
  75.9 1.9 %collective-permute-start.4 = (f32[128,1024]{1,0:T(8,128)S(1)}, f32[128,1024]{1,0:T(8,128)S(1)}, u32[]{:S(2)}, u32[]{:S(2)}) collective-permute-start(f32[128,1024]{1,0:T(8,128)S(1)} %all_gather.7.half_ref), channel_id=1, source_target_pairs={{0,4},{4,0},{1,5},{5,1},{2,6},{6,2},{3,7},{7,3},{8,12},{12,8},{9,1... | collective-permute-start | bytes 1572872 | tf_op jit(solution)/shard_map/ppermute | solution.py:320
